TPU v7x, 512 devices: a whole 4x8x8 slice. The times are simulated.
512 devices in a mesh: gz: 16 (over z, core), gy: 8 (over y), gx: 4 (over x).
Axes of the slice: x: 4, y: 8, z: 8, core: 2. Of those that a mesh axis runs over, the one named last changes fastest.
Arguments:
- features: bfloat16 [48, 32, 16, 512], P(None, 'gz', 'gy', 'gx'), may hold values from -20 to 20
- segment_ids: int32 [32, 16, 512], P('gz', 'gy', 'gx'), may hold values from 0 to 2047, as said below
- kernel_one: bfloat16 [3, 3, 3, 48, 48], replicated, may hold values from -0.15625 to 0.15625
- bias_one: float32 [48], replicated, may hold values from -3 to 3
- kernel_two: bfloat16 [3, 3, 3, 16, 48], replicated, may hold values from -0.15625 to 0.15625
Outputs:
- grad_features: bfloat16 [48, 32, 16, 512], P(None, 'gz', 'gy', 'gx')
- grad_kernel_one: float32 [3, 3, 3, 48, 48], replicated
- grad_bias_one: float32 [48], replicated
- grad_kernel_two: float32 [3, 3, 3, 16, 48], replicated
Inputs may be any that keep to these rules, and one draw needn't show every extreme that they name: `segment_ids`: every id occurs at some voxel.
All inputs are finite; a program needn't handle non-finite values.
Results may differ from a plain program's by a relative error of at most 0.017.
Values may be sent and summed in bfloat16 or wider, within the bound.
No kernel may reach another device: no remote copies, remote signals or barrier semaphores. Data moves between devices by JAX's collectives and lax.ppermute only.
A program may use at most 64 MiB of HBM per device.

v0:
```python
import jax
import jax.numpy as jnp
from jax import lax
from jax.sharding import PartitionSpec as P

EMBED_DIM = 16
SEG_DEV = 4


pull_margin = 4.0
push_margin = 8.0


def extended(block, sides, width):
    for axis, dim in sides:
        count = lax.axis_size(axis)
        forward = [(i, i + 1) for i in range(count - 1)]
        backward = [(target, source) for source, target in forward]
        low = lax.ppermute(
            lax.slice_in_dim(block, block.shape[dim] - width, None, axis=dim), axis, forward
        )
        high = lax.ppermute(lax.slice_in_dim(block, 0, width, axis=dim), axis, backward)
        block = jnp.concatenate([low, block, high], axis=dim)
    return block


def correlate(padded, weights, depth_len, rows_len, cols_len):
    accumulated = jnp.zeros((weights.shape[3], depth_len * rows_len * cols_len), jnp.float32)
    for offset_depth in range(3):
        for offset_row in range(3):
            for offset_col in range(3):
                window_slice = padded[
                    :,
                    offset_depth : offset_depth + depth_len,
                    offset_row : offset_row + rows_len,
                    offset_col : offset_col + cols_len,
                ].reshape(padded.shape[0], -1)
                accumulated = accumulated + jnp.dot(
                    weights[offset_depth, offset_row, offset_col],
                    window_slice,
                    preferred_element_type=jnp.float32,
                )
    return accumulated


def taps_grad(padded, upstream, depth_len, rows_len, cols_len):
    results = []
    for offset_depth in range(3):
        for offset_row in range(3):
            for offset_col in range(3):
                window_slice = padded[
                    :,
                    offset_depth : offset_depth + depth_len,
                    offset_row : offset_row + rows_len,
                    offset_col : offset_col + cols_len,
                ].reshape(padded.shape[0], -1)
                results.append(
                    lax.dot_general(
                        upstream,
                        window_slice,
                        (((1,), (1,)), ((), ())),
                        preferred_element_type=jnp.float32,
                    )
                )
    return jnp.stack(results).reshape(3, 3, 3, upstream.shape[0], padded.shape[0])


def flipped(weights):
    return jnp.transpose(weights[::-1, ::-1, ::-1], (0, 1, 2, 4, 3))


def push_rows(own_centers, centers, scale):
    difference = own_centers.T[:, :, None] - centers.T[:, None, :]
    distance = jnp.sum(difference * difference, 0)
    hinge_term = jnp.maximum(push_margin - distance, 0.0)
    return -scale * jnp.sum(hinge_term[None, :, :] * difference, 2).T


def shards(features, segment_ids, kernel_one, bias_one, kernel_two):
    channels_in, depth_len, rows_len, cols_len = features.shape
    cells_here = depth_len * rows_len * cols_len
    device_count = lax.axis_size("gz") * lax.axis_size("gy") * lax.axis_size("gx")
    voxels_total = cells_here * device_count
    segment_count = SEG_DEV * device_count
    padded_in = extended(features, (("gz", 1), ("gy", 2), ("gx", 3)), 1)
    hidden = jnp.maximum(
        correlate(padded_in, kernel_one, depth_len, rows_len, cols_len) + bias_one[:, None], 0.0
    ).astype(jnp.bfloat16)
    hidden = hidden.reshape(channels_in, depth_len, rows_len, cols_len)
    padded_hidden = extended(hidden, (("gz", 1), ("gy", 2), ("gx", 3)), 1)
    embedding = correlate(padded_hidden, kernel_two, depth_len, rows_len, cols_len)
    segment_flat = segment_ids.reshape(-1)
    local_sums = jax.ops.segment_sum(embedding.T, segment_flat, num_segments=segment_count)
    local_counts = jax.ops.segment_sum(
        jnp.ones((cells_here,), jnp.float32), segment_flat, num_segments=segment_count
    )
    first_row = lax.axis_index(("gz", "gy", "gx")) * SEG_DEV
    push_scale = 8.0 / (segment_count * (segment_count - 1.0))
    segment_sums, counts = lax.psum((local_sums, local_counts), ("gz", "gy", "gx"))
    centers = segment_sums / counts[:, None]
    own_centers = lax.dynamic_slice_in_dim(centers, first_row, SEG_DEV, 0)
    push_grad = push_rows(own_centers, centers, push_scale)
    near_center = centers[segment_flat].T
    near_count = counts[segment_flat]
    offset_vec = embedding - near_center
    hinge_term = jnp.maximum(jnp.sum(offset_vec * offset_vec, 0) - pull_margin, 0.0)
    direct = 4.0 * hinge_term * offset_vec / (segment_count * near_count)
    local_direct = jax.ops.segment_sum(direct.T, segment_flat, num_segments=segment_count)
    placed = lax.dynamic_update_slice_in_dim(
        jnp.zeros((segment_count, EMBED_DIM), jnp.float32), push_grad, first_row, 0
    )
    center_grad = lax.psum(placed - local_direct, ("gz", "gy", "gx"))
    upstream = (voxels_total * (direct + center_grad[segment_flat].T / near_count)).astype(
        jnp.bfloat16
    )
    padded_up = extended(
        upstream.reshape(EMBED_DIM, depth_len, rows_len, cols_len),
        (("gz", 1), ("gy", 2), ("gx", 3)),
        1,
    )
    hidden_grad = jnp.where(
        hidden.reshape(channels_in, -1) > 0,
        correlate(padded_up, flipped(kernel_two), depth_len, rows_len, cols_len),
        0.0,
    ).astype(jnp.bfloat16)
    padded_grad = extended(
        hidden_grad.reshape(channels_in, depth_len, rows_len, cols_len),
        (("gz", 1), ("gy", 2), ("gx", 3)),
        1,
    )
    grad_features = (
        correlate(padded_grad, flipped(kernel_one), depth_len, rows_len, cols_len)
        .astype(jnp.bfloat16)
        .reshape(channels_in, depth_len, rows_len, cols_len)
    )
    grad_one = taps_grad(padded_in, hidden_grad, depth_len, rows_len, cols_len)
    grad_two = taps_grad(padded_hidden, upstream, depth_len, rows_len, cols_len)
    grad_bias = jnp.sum(hidden_grad.astype(jnp.float32), 1)
    grad_one, grad_two, grad_bias = lax.psum((grad_one, grad_two, grad_bias), ("gz", "gy", "gx"))
    return (
        grad_features,
        grad_one / voxels_total,
        grad_bias / voxels_total,
        grad_two / voxels_total,
    )


def solution(mesh):
    return jax.shard_map(
        shards,
        mesh=mesh,
        in_specs=(P(None, "gz", "gy", "gx"), P("gz", "gy", "gx"), P(), P(), P()),
        out_specs=(P(None, "gz", "gy", "gx"), P(), P(), P()),
        check_vma=False,
    )
```

profile of v0, /device:TPU:1, one launch (start us, length us, event | category | flops | bytes accessed | tf_op | source)
XLA Modules:
  0.0 1196.3 jit_solution(10424008943027878126)
XLA Ops:
  8.0 8.8 collective-permute-start.1
  16.8 1.9 collective-permute-start
  21.6 4.0 collective-permute-start.2
  25.6 4.0 scatter_custom_fusion.1
  29.6 100.6 %psum.43 = f32[2048]{0:T(1024)S(1)} all-reduce(f32[2048]{0:T(1024)S(1)} %scatter_custom_fusion.1), channel_id=1, replica_groups=mesh['gz'=16,'gy'=8,'gx'=4] {'gz','gy','gx'}, use_global_device_ids=true, to_apply=%region_3.0 | all-reduce | flops 2048 | bytes 16384 | tf_op jit(solution)/shard_map/psum | solution.py:99
  130.2 3.1 gather_fusion.1
  134.0 2.5 collective-permute-start.4
  140.0 3.9 collective-permute-done.5
  152.8 3.5 collective-permute-start.6
  158.9 3.2 collective-permute-done.7
  163.7 4.0 collective-permute-start.8
  170.7 1.9 collective-permute-start.10
  174.5 2.4 collective-permute-done.10
  176.8 4.2 collective-permute-done.11
  189.3 4.8 scatter_custom_fusion
  194.2 272.1 %all-reduce.5.cloned.1.call-done = f32[2048,16]{1,0:T(8,128)} async-done(((f32[2048,16]{1,0:T(8,128)}), f32[2048,16]{1,0:T(8,128)}) %all-reduce.5.cloned.1.call-update) | async-done | bytes 131088 | tf_op jit(solution)/shard_map/psum | solution.py:99
  472.8 4.2 scatter_custom_fusion.2
  479.1 268.0 %all-reduce.7.cloned.1.call-done = f32[2048,16]{1,0:T(8,128)} async-done(((f32[2048,16]{1,0:T(8,128)}), f32[2048,16]{1,0:T(8,128)}) %all-reduce.7.cloned.1.call-update) | async-done | bytes 131088 | tf_op jit(solution)/shard_map/psum | solution.py:112
  747.0 2.3 gather_fusion.2
  750.9 1.9 collective-permute-start.13
  752.9 3.6 collective-permute-start.12
  764.6 4.0 collective-permute-start.14
  769.8 2.7 collective-permute-start.16
  774.5 3.3 collective-permute-done.17
  785.4 2.9 collective-permute-start.19
  788.3 3.3 collective-permute-start.18
  811.1 98.3 %psum.46 = f32[48]{0:T(128)S(1)} all-reduce(f32[48]{0:T(128)S(1)} %get-tuple-element.162), channel_id=1, replica_groups=mesh['gz'=16,'gy'=8,'gx'=4] {'gz','gy','gx'}, use_global_device_ids=true, to_apply=%region_11.12 | all-reduce | flops 48 | bytes 384 | tf_op jit(solution)/shard_map/psum | solution.py:139
  911.0 4.0 collective-permute-start.20
  917.2 3.4 collective-permute-start.22
  923.2 3.8 collective-permute-done.23
  935.9 251.1 %all-reduce.9.cloned.1.call-done = (f32[3,3,3,48,48]{4,3,2,1,0:T(8,128)}, f32[3,3,3,16,48]{4,3,2,1,0:T(8,128)}) async-done(((f32[3,3,3,48,48]{4,3,2,1,0:T(8,128)}, f32[3,3,3,16,48]{4,3,2,1,0:T(8,128)}), (f32[3,3,3,48,48]{4,3,2,1,0:T(8,128)}, f32[3,3,3,16,48]{4,3,2,1,0:T(8,128)})) %all-reduce.9.cloned.1.call-update) | async-done | bytes 331792 | tf_op jit(solution)/shard_map/psum | solution.py:139
  1187.0 2.0 broadcast_multiply_fusion
  (582 shorter events, 96.5 us)
Async XLA Ops:
  7.2 459.2 %all-reduce.5.cloned.1.call-start = ((), (), s32[]{:S(2)}) async-start(), calls=%async_computation | async-start | bytes 2097152 | tf_op jit(solution)/shard_map/psum | solution.py:99
  8.0 11.9 collective-permute-start.1
  16.8 3.1 collective-permute-start
  20.3 113.1 %collective-permute-start.3 = (bf16[48,4,1,128]{3,2,1,0:T(2,128)(2,1)S(1)}, bf16[48,4,1,128]{3,2,1,0:T(2,128)(2,1)S(1)}, u32[]{:S(2)}, u32[]{:S(2)}) collective-permute-start(bf16[48,4,1,128]{3,2,1,0:T(2,128)(2,1)S(1)} %get-tuple-element.126), channel_id=1, source_target_pairs={{4,0},{8,4},{12,8},{16,12},{20,16},{24,20},{28,24},{5,1},{9,5},{13... | collective-permute-start | bytes 147464 | tf_op jit(solution)/shard_map/ppermute | solution.py:22
  21.6 111.8 %collective-permute-start.2 = (bf16[48,4,1,128]{3,2,1,0:T(2,128)(2,1)S(1)}, bf16[48,4,1,128]{3,2,1,0:T(2,128)(2,1)S(1)}, u32[]{:S(2)}, u32[]{:S(2)}) collective-permute-start(bf16[48,4,1,128]{3,2,1,0:T(2,128)(2,1)S(1)} %get-tuple-element.125), channel_id=1, source_target_pairs={{0,4},{4,8},{8,12},{12,16},{16,20},{20,24},{24,28},{1,5},{5,9},{9,... | collective-permute-start | bytes 147464 | tf_op jit(solution)/shard_map/ppermute | solution.py:19
  133.3 23.0 %copy-start.100 = (f32[512]{0:T(512)}, f32[512]{0:T(512)S(1)}, u32[]{:S(2)}) copy-start(f32[512]{0:T(512)S(1)} %gather_fusion.1) | copy-start | bytes 6148
  133.4 18.1 %copy-start.30 = (bf16[48,512]{1,0:T(8,128)(2,1)}, bf16[48,512]{1,0:T(8,128)(2,1)S(1)}, u32[]{:S(2)}) copy-start(bf16[48,512]{1,0:T(8,128)(2,1)S(1)} %reshape.462) | copy-start | bytes 147460
  134.0 6.0 collective-permute-start.4
  136.5 7.5 collective-permute-start.5
  152.8 6.0 collective-permute-start.6
  156.9 5.1 collective-permute-start.7
  162.4 5.5 collective-permute-start.9
  163.7 5.6 collective-permute-start.8
  167.9 20.0 %copy-start.76 = (f32[512,16]{0,1:T(8,128)}, f32[512,16]{0,1:T(8,128)S(1)}, u32[]{:S(2)}) copy-start(f32[512,16]{0,1:T(8,128)S(1)} %fusion.192) | copy-start | bytes 98308
  170.1 17.7 %copy-start.78 = (f32[512,16]{0,1:T(8,128)}, f32[512,16]{0,1:T(8,128)S(1)}, u32[]{:S(2)}) copy-start(f32[512,16]{0,1:T(8,128)S(1)} %fusion.186) | copy-start | bytes 98308
  170.7 6.2 collective-permute-start.10
  172.6 8.5 collective-permute-start.11
  194.1 552.9 %all-reduce.7.cloned.1.call-start = ((), (), s32[]{:S(2)}) async-start(), calls=%async_computation.1 | async-start | bytes 2097152 | tf_op jit(solution)/shard_map/psum | solution.py:112
  478.2 708.8 %all-reduce.9.cloned.1.call-start = ((), (), s32[]{:S(2)}) async-start(), calls=%async_computation.2 | async-start | bytes 1769472 | tf_op jit(solution)/shard_map/psum | solution.py:139
  750.9 12.2 %collective-permute-start.13 = (bf16[16,1,2,128]{3,2,1,0:T(2,128)(2,1)S(1)}, bf16[16,1,2,128]{3,2,1,0:T(2,128)(2,1)S(1)}, u32[]{:S(2)}, u32[]{:S(2)}) collective-permute-start(bf16[16,1,2,128]{3,2,1,0:T(2,128)(2,1)S(1)} %get-tuple-element.158), channel_id=1, source_target_pairs={{32,0},{64,32},{96,64},{128,96},{160,128},{192,160},{224,192},{256... | collective-permute-start | bytes 24584 | tf_op jit(solution)/shard_map/ppermute | solution.py:22
  752.9 10.2 collective-permute-start.12
  763.3 5.5 collective-permute-start.15
  764.6 5.0 collective-permute-start.14
  769.8 4.7 collective-permute-start.16
  772.5 5.4 collective-permute-start.17
  785.4 124.0 %collective-permute-start.19 = (bf16[48,1,2,128]{3,2,1,0:T(2,128)(2,1)S(1)}, bf16[48,1,2,128]{3,2,1,0:T(2,128)(2,1)S(1)}, u32[]{:S(2)}, u32[]{:S(2)}) collective-permute-start(bf16[48,1,2,128]{3,2,1,0:T(2,128)(2,1)S(1)} %get-tuple-element.138), channel_id=1, source_target_pairs={{32,0},{64,32},{96,64},{128,96},{160,128},{192,160},{224,192},{256... | collective-permute-start | bytes 73736 | tf_op jit(solution)/shard_map/ppermute | solution.py:22
  788.3 121.0 %collective-permute-start.18 = (bf16[48,1,2,128]{3,2,1,0:T(2,128)(2,1)S(1)}, bf16[48,1,2,128]{3,2,1,0:T(2,128)(2,1)S(1)}, u32[]{:S(2)}, u32[]{:S(2)}) collective-permute-start(bf16[48,1,2,128]{3,2,1,0:T(2,128)(2,1)S(1)} %get-tuple-element.139), channel_id=1, source_target_pairs={{0,32},{32,64},{64,96},{96,128},{128,160},{160,192},{192,224},{224... | collective-permute-start | bytes 73736 | tf_op jit(solution)/shard_map/ppermute | solution.py:19
  811.1 104.5 %copy-start.2 = (f32[27,48,48]{2,1,0:T(8,128)}, f32[27,48,48]{2,1,0:T(8,128)S(1)}, u32[]{:S(2)}) copy-start(f32[27,48,48]{2,1,0:T(8,128)S(1)} %fusion.55) | copy-start | bytes 746500
  909.7 5.9 collective-permute-start.21
  911.0 5.6 collective-permute-start.20
  917.2 6.0 collective-permute-start.22
  920.6 6.4 collective-permute-start.23
  (99 other events, 221.8 us)
Sparse Core Ops, SparseCore 0:
  194.2 272.0 all-reduce.4
  478.3 268.6 all-reduce.6
  915.7 271.2 all-reduce.8
where the time goes:
time: 1200 us
  waiting for transfers between devices  816 us (68%)
  blocking collectives  199 us (17%)
  starting transfers between devices  65.3 us (5%)
  local copies, waits for them, and re-layouts  45.3 us (4%)
  other arithmetic  28.8 us (2%)
  matrix products  25.4 us (2%)
  between operations  16.2 us (1%)
    psum x1, waiting for transfers between devices, shards(): lax.psum((local_sums, local_counts), ('gz', 'gy', 'gx'))  272 us
    psum x1, waiting for transfers between devices, shards(): center_grad = lax.psum(placed - local_direct, ('gz', 'gy', 'gx'))  268 us
    psum x1, waiting for transfers between devices, shards(): lax.psum((grad_one, grad_two, grad_bias), ('gz', 'gy', 'gx'))  251 us
    psum x1, blocking collectives, shards(): lax.psum((local_sums, local_counts), ('gz', 'gy', 'gx'))  101 us
    psum x1, blocking collectives, shards(): lax.psum((grad_one, grad_two, grad_bias), ('gz', 'gy', 'gx'))  98.3 us
    ppermute x12, starting transfers between devices, extended(): lax.ppermute(lax.slice_in_dim(block, block.shape[dim] - width, None, axis...  38.7 us
    unnamed x212, local copies, waits for them, and re-layouts  29.1 us
    ppermute x12, starting transfers between devices, extended(): lax.ppermute(lax.slice_in_dim(block, 0, width, axis=dim), axis, backward)  26.4 us
  transfers between devices with their start and end apart: 27, of which 15 were waited for; matrix products, arithmetic and copies ran while one was open for 2% of the time, Pallas kernels for 0%

commit v1 on v0

v1 whole, which is shorter than its diff:
```python
import functools

import jax
import jax.numpy as jnp
from jax import lax
from jax.experimental import pallas as pl
from jax.experimental.pallas import tpu as pltpu
from jax.sharding import PartitionSpec as P

EMBED = 16
CHANNELS = 48
LANES = 128
WIDE = 2 * LANES
CELLS = 512
GROUPS = 4
ROW_COLS = 512
VOXELS = 262144.0
SEGMENTS = 2048.0
pull_margin = 4.0
push_margin = 8.0
f32, bf16 = jnp.float32, jnp.bfloat16


def kernel_call(body, outs, scratch=(), scalars=0, flops=0):
    def call(*args):
        specs = [pl.BlockSpec(memory_space=pltpu.SMEM)] * scalars
        specs += [pl.BlockSpec(memory_space=pltpu.VMEM)] * (len(args) - scalars)
        return pl.pallas_call(
            body,
            out_shape=[jax.ShapeDtypeStruct(shape, dtype) for shape, dtype in outs],
            in_specs=specs,
            out_specs=[pl.BlockSpec(memory_space=pltpu.VMEM)] * len(outs),
            scratch_shapes=[pltpu.VMEM(shape, dtype) for shape, dtype in scratch],
            compiler_params=pltpu.CompilerParams(vmem_limit_bytes=40 * 1024 * 1024),
        )(*args)

    return call


def lane(shape):
    return lax.broadcasted_iota(jnp.int32, shape, len(shape) - 1)


def edges(rows):
    at = lane(rows[0].shape)
    first = jnp.zeros(rows[0].shape, f32)
    last = jnp.zeros(rows[0].shape, f32)
    for r, row in enumerate(rows):
        turned = row.astype(f32) if r == 0 else pltpu.roll(row.astype(f32), 8 * r, 1)
        first = jnp.where((at >= 8 * r) & (at < 8 * r + 2), turned, first)
        start = (8 * r - 2) % LANES
        last = jnp.where((at >= start) & (at < start + 2), turned, last)
    return first.astype(bf16), last.astype(bf16)


def widen(blocks, wide_ref):
    for yb, ref in enumerate(blocks):
        for zb in range(3):
            pack = ref[zb, 4].astype(f32)
            for r in range(4):
                edge = pack if r == 0 else pltpu.roll(pack, LANES - 8 * r, 1)
                z, y = 2 * zb + r // 2, 2 * yb + r % 2
                wide_ref[z, y, :, 0:LANES] = ref[zb, r]
                wide_ref[z, y, :, LANES:WIDE] = edge.astype(bf16)


def window(ref, z, y):
    size = ref.shape[2]
    return jnp.concatenate([ref[z + a, y : y + 3].reshape(3 * size, WIDE) for a in range(3)], axis=0)


def fold(taps):
    size = taps.shape[0] // 3
    return pltpu.roll(taps[:size], 1, 1) + taps[size : 2 * size] + pltpu.roll(taps[2 * size :], WIDE - 1, 1)


def split(value):
    high = value.astype(bf16)
    return high, (value - high.astype(f32)).astype(bf16)


def hot(cell):
    return jnp.where(lax.broadcasted_iota(jnp.int32, (CELLS, cell.shape[1]), 0) == cell, 1.0, 0.0).astype(bf16)


def scatter(values, ids):
    group, cell = ids >> 9, ids & (CELLS - 1)
    spread = jnp.concatenate([jnp.where(group == g, values, 0.0) for g in range(GROUPS)], axis=0)
    size = spread.shape[0]
    both = jnp.concatenate(split(spread), axis=0)
    sums = lax.dot_general(both, hot(cell), (((1,), (1,)), ((), ())), preferred_element_type=f32)
    return sums[:size] + sums[size:]


def gather(table, ids):
    group, cell = ids >> 9, ids & (CELLS - 1)
    size = table.shape[0]
    both = jnp.concatenate(split(table), axis=0)
    found = jnp.dot(both, hot(cell), preferred_element_type=f32)
    found = found[:size] + found[size:]
    part = size // GROUPS
    picked = jnp.where(group == 0, found[:part], 0.0)
    for g in range(1, GROUPS):
        picked = picked + jnp.where(group == g, found[g * part : (g + 1) * part], 0.0)
    return picked


def store_tiles(tiles_ref, array):
    rows, cols = array.shape[0] // 8, array.shape[1] // LANES
    for i in range(rows):
        for k in range(cols):
            tiles_ref[i * cols + k] = array[8 * i : 8 * i + 8, LANES * k : LANES * (k + 1)]


def load_tiles(tiles_ref, first, count):
    cols = 4
    return jnp.concatenate(
        [jnp.concatenate([tiles_ref[i * cols + k] for k in range(cols)], axis=1) for i in range(first, first + count)],
        axis=0,
    )


def edge_kernel(rows_ref, first_ref, last_ref):
    first_ref[...], last_ref[...] = edges([rows_ref[r] for r in range(4)])


def embed_kernel(place, low, mid, high, taps_one, taps_two, bias, ids_ref, wide_ref, hidden_ref, embed_ref, tiles_ref):
    widen((low, mid, high), wide_ref)
    gz, gy, gx = place[0], place[1], place[2]
    at = lane((CHANNELS, WIDE))
    inside = (at < LANES) | ((at == LANES) & (gx < place[6])) | ((at == WIDE - 1) & (gx > 0))

    def layer(z, carry):
        for y in range(4):
            folded = fold(jnp.dot(taps_one[...], window(wide_ref, z, y), preferred_element_type=f32))
            folded = jnp.maximum(folded + bias[...], 0.0)
            depth, row = 2 * gz - 1 + z, 2 * gy - 1 + y
            exists = (depth >= 0) & (depth < 2 * place[4] + 2) & (row >= 0) & (row < 2 * place[5] + 2)
            hidden_ref[z, y] = jnp.where(inside & exists, folded, 0.0).astype(bf16)
        return carry

    lax.fori_loop(0, 4, layer, 0)
    for r in range(4):
        folded = fold(jnp.dot(taps_two[...], window(hidden_ref, r // 2, r % 2), preferred_element_type=f32))
        embed_ref[:, LANES * r : LANES * (r + 1)] = folded[:, :LANES]
    row = lax.broadcasted_iota(jnp.int32, (16, CELLS), 0)
    values = jnp.concatenate([embed_ref[...], jnp.where(row == 0, 1.0, 0.0)], axis=0)
    store_tiles(tiles_ref, scatter(values, ids_ref[...]))


def direct_kernel(place, tiles_ref, embed_ref, ids_ref, direct_ref, share_ref, out_ref):
    centers, table = [], []
    for g in range(GROUPS):
        part = load_tiles(tiles_ref, 4 * g, 3)
        counts = part[EMBED : EMBED + 1]
        centers.append(part[:EMBED] / counts)
        row = lax.broadcasted_iota(jnp.int32, (16, CELLS), 0)
        table += [centers[g], jnp.where(row == 0, 1.0 / counts, 0.0)]
    near = gather(jnp.concatenate(table, axis=0), ids_ref[...])
    share = near[EMBED : EMBED + 1]
    offset = embed_ref[...] - near[:EMBED]
    hinge = jnp.maximum(jnp.sum(offset * offset, axis=0, keepdims=True) - pull_margin, 0.0)
    direct = (4.0 / SEGMENTS) * hinge * share * offset
    direct_ref[...] = direct
    share_ref[...] = jnp.broadcast_to(share, share_ref.shape)
    sums = scatter(direct, ids_ref[...])
    mine = lane((EMBED, CELLS)) == place[3]
    scale = 8.0 / (SEGMENTS * (SEGMENTS - 1.0))
    for g in range(GROUPS):
        own = jnp.sum(jnp.where(mine, centers[g], 0.0), axis=1, keepdims=True)
        total = jnp.zeros((EMBED, CELLS), f32)
        for other in centers:
            difference = own - other
            distance = jnp.sum(difference * difference, axis=0, keepdims=True)
            total = total + jnp.maximum(push_margin - distance, 0.0) * difference
        push = -scale * jnp.sum(total, axis=1, keepdims=True)
        grad = jnp.where(mine, push, 0.0) - sums[EMBED * g : EMBED * (g + 1)]
        for i in range(2):
            for k in range(4):
                out_ref[(2 * g + i) * 4 + k] = grad[8 * i : 8 * i + 8, LANES * k : LANES * (k + 1)]


def upstream_kernel(tiles_ref, direct_ref, share_ref, ids_ref, rows_ref, first_ref, last_ref):
    found = gather(load_tiles(tiles_ref, 0, 8), ids_ref[...])
    upstream = (VOXELS * (direct_ref[...] + found * share_ref[0:1])).astype(bf16)
    rows = [upstream[:, LANES * r : LANES * (r + 1)] for r in range(4)]
    for r in range(4):
        rows_ref[r] = rows[r]
    first_ref[...], last_ref[...] = edges(rows)


def backward_kernel(low, mid, high, wide_ref, hidden_ref, taps_two, taps_one, features_ref, tiles_ref, up_ref, grad_ref):
    widen((low, mid, high), up_ref)

    def layer(z, carry):
        for y in range(4):
            folded = fold(jnp.dot(taps_two[...], window(up_ref, z, y), preferred_element_type=f32))
            grad_ref[z, y] = jnp.where(hidden_ref[z, y].astype(f32) > 0.0, folded, 0.0).astype(bf16)
        return carry

    lax.fori_loop(0, 4, layer, 0)
    over_cells = (((1,), (1,)), ((), ()))
    one = jnp.zeros((3 * CHANNELS, 9 * CHANNELS + 16), f32)
    two = jnp.zeros((3 * EMBED, 9 * CHANNELS), f32)

    def shifted(row):
        row = jnp.where(lane(row.shape) < LANES, row.astype(f32), 0.0)
        return jnp.concatenate([pltpu.roll(row, WIDE - 1, 1), row, pltpu.roll(row, 1, 1)], axis=0).astype(bf16)

    for r in range(4):
        z, y = r // 2, r % 2
        folded = fold(jnp.dot(taps_one[...], window(grad_ref, z, y), preferred_element_type=f32))
        features_ref[r] = folded[:, :LANES].astype(bf16)
        seen = jnp.concatenate([window(wide_ref, z + 1, y + 1), jnp.ones((16, WIDE), bf16)], axis=0)
        one = one + lax.dot_general(shifted(grad_ref[z + 1, y + 1]), seen, over_cells, preferred_element_type=f32)
        two = two + lax.dot_general(
            shifted(up_ref[z + 2, y + 2]), window(hidden_ref, z, y), over_cells, preferred_element_type=f32
        )
    one = jnp.concatenate([one, jnp.zeros((3 * CHANNELS, 64), f32)], axis=1)
    two = jnp.concatenate([two, jnp.zeros((3 * EMBED, 80), f32)], axis=1)
    store_tiles(tiles_ref, jnp.concatenate([one, two], axis=0))


def result_kernel(tiles_ref, one_ref, bias_ref, two_ref):
    for c in range(3):
        part = load_tiles(tiles_ref, 6 * c, 6) * (1.0 / VOXELS)
        for ab in range(9):
            one_ref[ab * 3 + c] = part[:, CHANNELS * ab : CHANNELS * (ab + 1)]
        if c == 1:
            bias_ref[...] = part[:, 9 * CHANNELS : 9 * CHANNELS + 1]
        part = load_tiles(tiles_ref, 18 + 2 * c, 2) * (1.0 / VOXELS)
        for ab in range(9):
            two_ref[ab * 3 + c] = part[:, CHANNELS * ab : CHANNELS * (ab + 1)]


def passed(low, high, axis):
    count = lax.axis_size(axis)
    forward = [(i, i + 1) for i in range(count - 1)]
    backward = [(target, source) for source, target in forward]
    return lax.ppermute(high, axis, forward), lax.ppermute(low, axis, backward)


def surround(rows, first, last):
    left, right = passed(first, last, "gx")
    block = jnp.concatenate([rows, (left + right)[None]], axis=0)
    low, high = passed(block, block, "gz")
    block = jnp.stack([low, block, high])
    low, high = passed(block, block, "gy")
    return low, block, high


def total(tiles):
    plane = lax.axis_size(("gy", "gx"))
    depth = lax.axis_size("gz")
    lines = tiles.shape[0] // plane * 8
    pieces = tiles.reshape(plane, lines, LANES)
    piece = jnp.sum(lax.all_to_all(pieces, ("gy", "gx"), 0, 0), 0)
    pieces = jnp.broadcast_to(piece[None], (depth, lines, LANES))
    piece = jnp.sum(lax.all_to_all(pieces, "gz", 0, 0), 0)
    pieces = jnp.broadcast_to(piece[None], (plane, lines, LANES))
    return lax.all_to_all(pieces, ("gy", "gx"), 0, 0).reshape(tiles.shape)


def shards(features, segment_ids, kernel_one, bias_one, kernel_two):
    axes = ("gz", "gy", "gx")
    place = jnp.stack(
        [lax.axis_index(axis) for axis in axes]
        + [lax.axis_index(axes)]
        + [jnp.int32(lax.axis_size(axis) - 1) for axis in axes]
    ).astype(jnp.int32)
    taps_one = jnp.transpose(kernel_one, (2, 3, 0, 1, 4)).reshape(3 * CHANNELS, 9 * CHANNELS)
    taps_two = jnp.transpose(kernel_two, (2, 3, 0, 1, 4)).reshape(3 * EMBED, 9 * CHANNELS)
    back_one = jnp.transpose(kernel_one[::-1, ::-1, ::-1], (2, 4, 0, 1, 3)).reshape(3 * CHANNELS, 9 * CHANNELS)
    back_two = jnp.transpose(kernel_two[::-1, ::-1, ::-1], (2, 4, 0, 1, 3)).reshape(3 * CHANNELS, 9 * EMBED)
    ids = segment_ids.reshape(1, ROW_COLS)
    rows = jnp.transpose(features, (1, 2, 0, 3)).reshape(4, CHANNELS, LANES)

    first, last = kernel_call(edge_kernel, [((CHANNELS, LANES), bf16)] * 2)(rows)
    low, mid, high = surround(rows, first, last)
    wide, hidden, embedding, tiles = kernel_call(
        embed_kernel,
        [
            ((6, 6, CHANNELS, WIDE), bf16),
            ((4, 4, CHANNELS, WIDE), bf16),
            ((EMBED, CELLS), f32),
            ((64, 8, LANES), f32),
        ],
        scalars=1,
    )(place, low, mid, high, taps_one, taps_two, bias_one[:, None], ids)
    tiles = total(tiles)
    direct, share, tiles = kernel_call(
        direct_kernel, [((EMBED, CELLS), f32), ((8, CELLS), f32), ((32, 8, LANES), f32)], scalars=1
    )(place, tiles, embedding, ids)
    tiles = total(tiles)
    rows, first, last = kernel_call(
        upstream_kernel, [((4, EMBED, LANES), bf16), ((EMBED, LANES), bf16), ((EMBED, LANES), bf16)]
    )(tiles, direct, share, ids)
    low, mid, high = surround(rows, first, last)
    rows, tiles = kernel_call(
        backward_kernel,
        [((4, CHANNELS, LANES), bf16), ((96, 8, LANES), f32)],
        scratch=[((6, 6, EMBED, WIDE), bf16), ((4, 4, CHANNELS, WIDE), bf16)],
    )(low, mid, high, wide, hidden, back_two, back_one)
    grad_features = jnp.transpose(rows.reshape(2, 2, CHANNELS, LANES), (2, 0, 1, 3))
    grad_one, grad_bias, grad_two = kernel_call(
        result_kernel, [((27, CHANNELS, CHANNELS), f32), ((CHANNELS, 1), f32), ((27, EMBED, CHANNELS), f32)]
    )(total(tiles))
    return (
        grad_features,
        grad_one.reshape(3, 3, 3, CHANNELS, CHANNELS),
        grad_bias.reshape(CHANNELS),
        grad_two.reshape(3, 3, 3, EMBED, CHANNELS),
    )


def solution(mesh):
    return jax.shard_map(
        shards,
        mesh=mesh,
        in_specs=(P(None, "gz", "gy", "gx"), P("gz", "gy", "gx"), P(), P(), P()),
        out_specs=(P(None, "gz", "gy", "gx"), P(), P(), P()),
        check_vma=False,
    )
```

time: 1200 us -> 217 us (0.18)
  waiting for transfers between devices: 816 us -> 32.3 us
  blocking collectives: 199 us -> 132 us
  local copies, waits for them, and re-layouts: 45.3 us -> 5.18 us
  starting transfers between devices: 65.3 us -> 36.6 us
  other arithmetic: 28.8 us -> 0.85 us
  matrix products: 25.4 us -> 0 us
  between operations: 16.2 us -> 0.96 us
    psum x3 -> x0, waiting for transfers between devices: 791 us -> none  [the longest x1 272 us: shards(): lax.psum((local_sums, local_counts), ('gz', 'gy', 'gx'))]
    psum x2 -> x0, blocking collectives: 199 us -> none  [the longest x1 101 us: shards(): lax.psum((local_sums, local_counts), ('gz', 'gy', 'gx'))]
    all_to_all x0 -> x8, blocking collectives: none -> 132 us  [the longest x3 55.1 us: total(): piece = jnp.sum(lax.all_to_all(pieces, ('gy', 'gx'), 0, 0), 0)]
    ppermute x24 -> x12, starting transfers between devices: 65.1 us -> 32.6 us  [the longest x6 22.9 us: passed(): lax.ppermute(high, axis, forward)]
    unnamed x212 -> x8, local copies, waits for them, and re-layouts: 29.1 us -> 1.29 us
    dot_general x162 -> x0, matrix products: 25.4 us -> none  [the longest x108 18.7 us: correlate(): jnp.dot(weights[offset_depth, offset_row, offset_col], window_slice, pref...]
    all_to_all x0 -> x1, waiting for transfers between devices: none -> 14 us  [total(): return lax.all_to_all(pieces, ('gy', 'gx'), 0, 0).reshape(tiles.shape)]
    scatter-add x3 -> x0, other arithmetic: 12.9 us -> none  [the longest x1 4.81 us: shards(): jax.ops.segment_sum(embedding.T, segment_flat, num_segments=segment_count)]
  transfers between devices with their start and end apart: 27 -> 13, of which waited for: 15 -> 7; matrix products, arithmetic and copies ran while one was open for 2% -> 1% of each run, Pallas kernels for 0% -> 0%
where the time goes in v1:
time: 217 us; the launch traced here: 216 us
  blocking collectives  132 us (61%)
  starting transfers between devices  36.6 us (17%)
  waiting for transfers between devices  32.3 us (15%)
  Pallas kernels  7.92 us (4%)
  local copies, waits for them, and re-layouts  5.18 us (2%)
    all_to_all x3, blocking collectives, total(): piece = jnp.sum(lax.all_to_all(pieces, ('gy', 'gx'), 0, 0), 0)  55.1 us
    all_to_all x3, blocking collectives, total(): piece = jnp.sum(lax.all_to_all(pieces, 'gz', 0, 0), 0)  48.4 us
    all_to_all x2, blocking collectives, total(): return lax.all_to_all(pieces, ('gy', 'gx'), 0, 0).reshape(tiles.shape)  28.4 us
    ppermute x6, starting transfers between devices, passed(): lax.ppermute(high, axis, forward)  22.9 us
    ppermute x6, waiting for transfers between devices, passed(): lax.ppermute(low, axis, backward)  18.3 us
    all_to_all x1, waiting for transfers between devices, total(): return lax.all_to_all(pieces, ('gy', 'gx'), 0, 0).reshape(tiles.shape)  14 us
    ppermute x6, starting transfers between devices, passed(): lax.ppermute(low, axis, backward)  9.67 us
    pallas_call x6, Pallas kernels, call(): pl.pallas_call(body, out_shape=[jax.ShapeDtypeStruct(shape, dtype) for sh...  7.92 us
  transfers between devices with their start and end apart: 13, of which 7 were waited for; matrix products, arithmetic and copies ran while one was open for 1% of the time, Pallas kernels for 0%

profile of v1, /device:TPU:1, one launch (start us, length us, event | category | flops | bytes accessed | tf_op | source)
XLA Modules:
  0.0 215.7 jit_solution(6725928135558934565)
XLA Ops:
  1.5 3.9 %collective-permute-start = (bf16[48,128]{1,0:T(8,128)(2,1)S(1)}, bf16[48,128]{1,0:T(8,128)(2,1)S(1)}, u32[]{:S(2)}, u32[]{:S(2)}) collective-permute-start(bf16[48,128]{1,0:T(8,128)(2,1)S(1)} %get-tuple-element.21), channel_id=1, source_target_pairs={{0,1},{1,2},{2,3},{4,5},{5,6},{6,7},{8,9},{9,10},{10,11},{12,13},{... | collective-permute-start | bytes 36872 | tf_op jit(solution)/shard_map/ppermute | solution.py:240
  5.5 1.3 collective-permute-start.1
  6.8 3.1 %collective-permute-done.1 = bf16[48,128]{1,0:T(8,128)(2,1)S(1)} collective-permute-done((bf16[48,128]{1,0:T(8,128)(2,1)S(1)}, bf16[48,128]{1,0:T(8,128)(2,1)S(1)}, u32[]{:S(2)}, u32[]{:S(2)}) %collective-permute-start.1) | collective-permute-done | bytes 12320 | tf_op jit(solution)/shard_map/ppermute | solution.py:240
  9.9 6.0 %collective-permute-start.2 = (bf16[5,48,128]{2,1,0:T(8,128)(2,1)S(1)}, bf16[5,48,128]{2,1,0:T(8,128)(2,1)S(1)}, u32[]{:S(2)}, u32[]{:S(2)}) collective-permute-start(bf16[5,48,128]{2,1,0:T(8,128)(2,1)S(1)} %get-tuple-element.39), channel_id=1, source_target_pairs={{0,32},{32,64},{64,96},{96,128},{128,160},{160,192},{192,224},{224... | collective-permute-start | bytes 184328 | tf_op jit(solution)/shard_map/ppermute | solution.py:240
  15.9 2.6 %collective-permute-start.3 = (bf16[5,48,128]{2,1,0:T(8,128)(2,1)S(1)}, bf16[5,48,128]{2,1,0:T(8,128)(2,1)S(1)}, u32[]{:S(2)}, u32[]{:S(2)}) collective-permute-start(bf16[5,48,128]{2,1,0:T(8,128)(2,1)S(1)} %get-tuple-element.39), channel_id=1, source_target_pairs={{32,0},{64,32},{96,64},{128,96},{160,128},{192,160},{224,192},{256... | collective-permute-start | bytes 184328 | tf_op jit(solution)/shard_map/ppermute | solution.py:240
  18.5 2.9 %collective-permute-done.3 = bf16[5,48,128]{2,1,0:T(8,128)(2,1)S(1)} collective-permute-done((bf16[5,48,128]{2,1,0:T(8,128)(2,1)S(1)}, bf16[5,48,128]{2,1,0:T(8,128)(2,1)S(1)}, u32[]{:S(2)}, u32[]{:S(2)}) %collective-permute-start.3) | collective-permute-done | bytes 61472 | tf_op jit(solution)/shard_map/ppermute | solution.py:240
  21.5 3.2 %collective-permute-start.4 = (bf16[3,5,48,128]{3,2,1,0:T(8,128)(2,1)S(1)}, bf16[3,5,48,128]{3,2,1,0:T(8,128)(2,1)S(1)}, u32[]{:S(2)}, u32[]{:S(2)}) collective-permute-start(bf16[3,5,48,128]{3,2,1,0:T(8,128)(2,1)S(1)} %pad_maximum_fusion.mid), channel_id=1, source_target_pairs={{0,4},{4,8},{8,12},{12,16},{16,20},{20,24},{24,28},{1,5},{5,9},{9,... | collective-permute-start | bytes 552968 | tf_op jit(solution)/shard_map/ppermute | solution.py:240
  24.7 1.3 collective-permute-start.5
  28.2 3.2 %collective-permute-done.5.high = bf16[3,5,48,128]{3,2,1,0:T(8,128)(2,1)S(1)} collective-permute-done((bf16[3,5,48,128]{3,2,1,0:T(8,128)(2,1)S(1)}, bf16[3,5,48,128]{3,2,1,0:T(8,128)(2,1)S(1)}, u32[]{:S(2)}, u32[]{:S(2)}) %collective-permute-start.5) | collective-permute-done | bytes 184352 | tf_op jit(solution)/shard_map/ppermute | solution.py:240
  31.3 2.9 %shard_map.85 = (bf16[6,6,48,256]{3,2,1,0:T(8,128)(2,1)S(1)}, bf16[4,4,48,256]{3,2,1,0:T(8,128)(2,1)S(1)}, f32[16,512]{1,0:T(8,128)S(1)}, f32[64,8,128]{2,1,0:T(8,128)S(1)}) custom-call(s32[7]{0:T(128)S(1)} %stack.43.place, bf16[3,5,48,128]{3,2,1,0:T(8,128)(2,1)S(1)} %collective-permute-done.4.low, bf16[3,5,48,128]{3,2,1,0:T(8,128)(2,1)S(1)} %pad_maximum_fusion.mid, ...), custom_call_target="tpu_custom_call" | custom-call | tf_op jit(solution)/shard_map/pallas_call | solution.py:28
  34.3 22.0 %all_to_all.45 = f32[32,16,128]{2,1,0:T(8,128)S(1)} all-to-all(f32[32,16,128]{2,1,0:T(8,128)S(1)} %bitcast.43), channel_id=1, replica_groups=mesh['gz'=16,'gy'=8,'gx'=4] {'gy','gx'}, dimensions={0} | all-to-all | bytes 524288 | tf_op jit(solution)/shard_map/all_to_all | solution.py:257
  56.3 21.0 %all_to_all.46 = f32[16,16,128]{2,1,0:T(8,128)S(1)} all-to-all(f32[16,16,128]{2,1,0:T(8,128)S(1)} %broadcast_in_dim.20), channel_id=1, replica_groups=mesh['gz'=16,'gy'=8,'gx'=4] {'gz'}, dimensions={0} | all-to-all | bytes 262144 | tf_op jit(solution)/shard_map/all_to_all | solution.py:259
  77.3 15.7 %all_to_all.47 = f32[32,16,128]{2,1,0:T(8,128)S(1)} all-to-all(f32[32,16,128]{2,1,0:T(8,128)S(1)} %broadcast_in_dim.21), channel_id=1, replica_groups=mesh['gz'=16,'gy'=8,'gx'=4] {'gy','gx'}, dimensions={0} | all-to-all | bytes 524288 | tf_op jit(solution)/shard_map/all_to_all | solution.py:261
  93.0 1.2 shard_map.86
  94.1 13.2 %all_to_all.48 = f32[32,8,128]{2,1,0:T(8,128)S(1)} all-to-all(f32[32,8,128]{2,1,0:T(8,128)S(1)} %get-tuple-element.25), channel_id=1, replica_groups=mesh['gz'=16,'gy'=8,'gx'=4] {'gy','gx'}, dimensions={0} | all-to-all | bytes 262144 | tf_op jit(solution)/shard_map/all_to_all | solution.py:257
  107.4 12.8 %all_to_all.49 = f32[16,8,128]{2,1,0:T(8,128)S(1)} all-to-all(f32[16,8,128]{2,1,0:T(8,128)S(1)} %broadcast_in_dim.22), channel_id=1, replica_groups=mesh['gz'=16,'gy'=8,'gx'=4] {'gz'}, dimensions={0} | all-to-all | bytes 131072 | tf_op jit(solution)/shard_map/all_to_all | solution.py:259
  120.2 12.8 %all_to_all.50.tiles_ref = f32[32,8,128]{2,1,0:T(8,128)S(1)} all-to-all(f32[32,8,128]{2,1,0:T(8,128)S(1)} %broadcast_in_dim.23), channel_id=1, replica_groups=mesh['gz'=16,'gy'=8,'gx'=4] {'gy','gx'}, dimensions={0} | all-to-all | bytes 262144 | tf_op jit(solution)/shard_map/all_to_all | solution.py:261
  133.3 1.4 collective-permute-start.6
  134.8 1.3 collective-permute-start.7
  136.1 3.0 %collective-permute-done.7 = bf16[16,128]{1,0:T(8,128)(2,1)S(1)} collective-permute-done((bf16[16,128]{1,0:T(8,128)(2,1)S(1)}, bf16[16,128]{1,0:T(8,128)(2,1)S(1)}, u32[]{:S(2)}, u32[]{:S(2)}) %collective-permute-start.7) | collective-permute-done | bytes 4128 | tf_op jit(solution)/shard_map/ppermute | solution.py:240
  139.1 5.3 %collective-permute-start.8 = (bf16[5,16,128]{2,1,0:T(8,128)(2,1)S(1)}, bf16[5,16,128]{2,1,0:T(8,128)(2,1)S(1)}, u32[]{:S(2)}, u32[]{:S(2)}) collective-permute-start(bf16[5,16,128]{2,1,0:T(8,128)(2,1)S(1)} %get-tuple-element.41), channel_id=1, source_target_pairs={{0,32},{32,64},{64,96},{96,128},{128,160},{160,192},{192,224},{224... | collective-permute-start | bytes 61448 | tf_op jit(solution)/shard_map/ppermute | solution.py:240
  144.4 1.9 collective-permute-start.9
  146.9 2.6 %collective-permute-done.9 = bf16[5,16,128]{2,1,0:T(8,128)(2,1)S(1)} collective-permute-done((bf16[5,16,128]{2,1,0:T(8,128)(2,1)S(1)}, bf16[5,16,128]{2,1,0:T(8,128)(2,1)S(1)}, u32[]{:S(2)}, u32[]{:S(2)}) %collective-permute-start.9) | collective-permute-done | bytes 20512 | tf_op jit(solution)/shard_map/ppermute | solution.py:240
  149.5 3.0 %collective-permute-start.10 = (bf16[3,5,16,128]{3,2,1,0:T(8,128)(2,1)S(1)}, bf16[3,5,16,128]{3,2,1,0:T(8,128)(2,1)S(1)}, u32[]{:S(2)}, u32[]{:S(2)}) collective-permute-start(bf16[3,5,16,128]{3,2,1,0:T(8,128)(2,1)S(1)} %pad_maximum_fusion.2.mid), channel_id=1, source_target_pairs={{0,4},{4,8},{8,12},{12,16},{16,20},{20,24},{24,28},{1,5},{5,9},{9,... | collective-permute-start | bytes 184328 | tf_op jit(solution)/shard_map/ppermute | solution.py:240
  152.6 1.3 collective-permute-start.11
  154.2 3.3 %collective-permute-done.11.high = bf16[3,5,16,128]{3,2,1,0:T(8,128)(2,1)S(1)} collective-permute-done((bf16[3,5,16,128]{3,2,1,0:T(8,128)(2,1)S(1)}, bf16[3,5,16,128]{3,2,1,0:T(8,128)(2,1)S(1)}, u32[]{:S(2)}, u32[]{:S(2)}) %collective-permute-start.11) | collective-permute-done | bytes 61472 | tf_op jit(solution)/shard_map/ppermute | solution.py:240
  157.5 2.2 %shard_map.88 = (bf16[4,48,128]{2,1,0:T(8,128)(2,1)S(1)}, f32[96,8,128]{2,1,0:T(8,128)S(1)}) custom-call(bf16[3,5,16,128]{3,2,1,0:T(8,128)(2,1)S(1)} %collective-permute-done.10.low, bf16[3,5,16,128]{3,2,1,0:T(8,128)(2,1)S(1)} %pad_maximum_fusion.2.mid, bf16[3,5,16,128]{3,2,1,0:T(8,128)(2,1)S(1)} %collective-permute-done.11.high, ...), custom_call_target="tpu_custom_call" | custom-call | tf_op jit(solution)/shard_map/pallas_call | solution.py:28
  159.8 19.9 %all_to_all.51 = f32[32,24,128]{2,1,0:T(8,128)S(1)} all-to-all(f32[32,24,128]{2,1,0:T(8,128)S(1)} %bitcast.42), channel_id=1, replica_groups=mesh['gz'=16,'gy'=8,'gx'=4] {'gy','gx'}, dimensions={0} | all-to-all | bytes 786432 | tf_op jit(solution)/shard_map/all_to_all | solution.py:257
  179.8 14.6 %all_to_all.52 = f32[16,24,128]{2,1,0:T(8,128)S(1)} all-to-all(f32[16,24,128]{2,1,0:T(8,128)S(1)} %broadcast_in_dim.25), channel_id=1, replica_groups=mesh['gz'=16,'gy'=8,'gx'=4] {'gz'}, dimensions={0} | all-to-all | bytes 393216 | tf_op jit(solution)/shard_map/all_to_all | solution.py:259
  195.2 4.0 %all-to-all-start.8 = ((f32[32,24,128]{2,1,0:T(8,128)}), f32[32,24,128]{2,1,0:T(8,128)S(1)}, u32[]{:S(2)}, u32[]{:S(2)}) async-start(f32[32,24,128]{2,1,0:T(8,128)} %broadcast_in_dim.26), calls=%async_computation.8 | async-start | bytes 786432 | tf_op jit(solution)/shard_map/all_to_all | solution.py:261
  199.9 14.0 %all-to-all-done.8 = f32[32,24,128]{2,1,0:T(8,128)S(1)} async-done(((f32[32,24,128]{2,1,0:T(8,128)}), f32[32,24,128]{2,1,0:T(8,128)S(1)}, u32[]{:S(2)}, u32[]{:S(2)}) %all-to-all-start.8) | async-done | bytes 393248 | tf_op jit(solution)/shard_map/all_to_all | solution.py:261
  213.9 1.2 shard_map.89
  (50 shorter events, 6.4 us)
Async XLA Ops:
  1.4 24.6 %copy-start.1 = (bf16[3,3,3,48,48]{4,3,2,1,0:T(8,128)(2,1)S(1)}, bf16[3,3,3,48,48]{4,3,2,1,0:T(8,128)(2,1)}, u32[]{:S(2)}) copy-start(bf16[3,3,3,48,48]{4,3,2,1,0:T(8,128)(2,1)} %param.7) | copy-start | bytes 373252
  1.5 5.3 %collective-permute-start = (bf16[48,128]{1,0:T(8,128)(2,1)S(1)}, bf16[48,128]{1,0:T(8,128)(2,1)S(1)}, u32[]{:S(2)}, u32[]{:S(2)}) collective-permute-start(bf16[48,128]{1,0:T(8,128)(2,1)S(1)} %get-tuple-element.21), channel_id=1, source_target_pairs={{0,1},{1,2},{2,3},{4,5},{5,6},{6,7},{8,9},{9,10},{10,11},{12,13},{... | collective-permute-start | bytes 36872 | tf_op jit(solution)/shard_map/ppermute | solution.py:240
  5.5 4.4 %collective-permute-start.1 = (bf16[48,128]{1,0:T(8,128)(2,1)S(1)}, bf16[48,128]{1,0:T(8,128)(2,1)S(1)}, u32[]{:S(2)}, u32[]{:S(2)}) collective-permute-start(bf16[48,128]{1,0:T(8,128)(2,1)S(1)} %get-tuple-element.22), channel_id=1, source_target_pairs={{1,0},{2,1},{3,2},{5,4},{6,5},{7,6},{9,8},{10,9},{11,10},{13,12},{... | collective-permute-start | bytes 36872 | tf_op jit(solution)/shard_map/ppermute | solution.py:240
  9.9 8.6 %collective-permute-start.2 = (bf16[5,48,128]{2,1,0:T(8,128)(2,1)S(1)}, bf16[5,48,128]{2,1,0:T(8,128)(2,1)S(1)}, u32[]{:S(2)}, u32[]{:S(2)}) collective-permute-start(bf16[5,48,128]{2,1,0:T(8,128)(2,1)S(1)} %get-tuple-element.39), channel_id=1, source_target_pairs={{0,32},{32,64},{64,96},{96,128},{128,160},{160,192},{192,224},{224... | collective-permute-start | bytes 184328 | tf_op jit(solution)/shard_map/ppermute | solution.py:240
  15.9 5.5 %collective-permute-start.3 = (bf16[5,48,128]{2,1,0:T(8,128)(2,1)S(1)}, bf16[5,48,128]{2,1,0:T(8,128)(2,1)S(1)}, u32[]{:S(2)}, u32[]{:S(2)}) collective-permute-start(bf16[5,48,128]{2,1,0:T(8,128)(2,1)S(1)} %get-tuple-element.39), channel_id=1, source_target_pairs={{32,0},{64,32},{96,64},{128,96},{160,128},{192,160},{224,192},{256... | collective-permute-start | bytes 184328 | tf_op jit(solution)/shard_map/ppermute | solution.py:240
  21.5 6.6 %collective-permute-start.4 = (bf16[3,5,48,128]{3,2,1,0:T(8,128)(2,1)S(1)}, bf16[3,5,48,128]{3,2,1,0:T(8,128)(2,1)S(1)}, u32[]{:S(2)}, u32[]{:S(2)}) collective-permute-start(bf16[3,5,48,128]{3,2,1,0:T(8,128)(2,1)S(1)} %pad_maximum_fusion.mid), channel_id=1, source_target_pairs={{0,4},{4,8},{8,12},{12,16},{16,20},{20,24},{24,28},{1,5},{5,9},{9,... | collective-permute-start | bytes 552968 | tf_op jit(solution)/shard_map/ppermute | solution.py:240
  24.7 6.6 %collective-permute-start.5 = (bf16[3,5,48,128]{3,2,1,0:T(8,128)(2,1)S(1)}, bf16[3,5,48,128]{3,2,1,0:T(8,128)(2,1)S(1)}, u32[]{:S(2)}, u32[]{:S(2)}) collective-permute-start(bf16[3,5,48,128]{3,2,1,0:T(8,128)(2,1)S(1)} %pad_maximum_fusion.mid), channel_id=1, source_target_pairs={{4,0},{8,4},{12,8},{16,12},{20,16},{24,20},{28,24},{5,1},{9,5},{13... | collective-permute-start | bytes 552968 | tf_op jit(solution)/shard_map/ppermute | solution.py:240
  26.2 0.9 copy-start.2
  27.3 0.7 copy-start.3
  28.1 3.3 %copy-start = (s32[2,2,128]{2,1,0:T(2,128)S(1)}, s32[2,2,128]{2,1,0:T(2,128)}, u32[]{:S(2)}) copy-start(s32[2,2,128]{2,1,0:T(2,128)} %param.6) | copy-start | bytes 6148
  133.3 2.7 %collective-permute-start.6 = (bf16[16,128]{1,0:T(8,128)(2,1)S(1)}, bf16[16,128]{1,0:T(8,128)(2,1)S(1)}, u32[]{:S(2)}, u32[]{:S(2)}) collective-permute-start(bf16[16,128]{1,0:T(8,128)(2,1)S(1)} %get-tuple-element.29), channel_id=1, source_target_pairs={{0,1},{1,2},{2,3},{4,5},{5,6},{6,7},{8,9},{9,10},{10,11},{12,13},{... | collective-permute-start | bytes 12296 | tf_op jit(solution)/shard_map/ppermute | solution.py:240
  134.8 4.4 %collective-permute-start.7 = (bf16[16,128]{1,0:T(8,128)(2,1)S(1)}, bf16[16,128]{1,0:T(8,128)(2,1)S(1)}, u32[]{:S(2)}, u32[]{:S(2)}) collective-permute-start(bf16[16,128]{1,0:T(8,128)(2,1)S(1)} %get-tuple-element.30), channel_id=1, source_target_pairs={{1,0},{2,1},{3,2},{5,4},{6,5},{7,6},{9,8},{10,9},{11,10},{13,12},{... | collective-permute-start | bytes 12296 | tf_op jit(solution)/shard_map/ppermute | solution.py:240
  139.1 7.7 %collective-permute-start.8 = (bf16[5,16,128]{2,1,0:T(8,128)(2,1)S(1)}, bf16[5,16,128]{2,1,0:T(8,128)(2,1)S(1)}, u32[]{:S(2)}, u32[]{:S(2)}) collective-permute-start(bf16[5,16,128]{2,1,0:T(8,128)(2,1)S(1)} %get-tuple-element.41), channel_id=1, source_target_pairs={{0,32},{32,64},{64,96},{96,128},{128,160},{160,192},{192,224},{224... | collective-permute-start | bytes 61448 | tf_op jit(solution)/shard_map/ppermute | solution.py:240
  144.4 5.1 %collective-permute-start.9 = (bf16[5,16,128]{2,1,0:T(8,128)(2,1)S(1)}, bf16[5,16,128]{2,1,0:T(8,128)(2,1)S(1)}, u32[]{:S(2)}, u32[]{:S(2)}) collective-permute-start(bf16[5,16,128]{2,1,0:T(8,128)(2,1)S(1)} %get-tuple-element.41), channel_id=1, source_target_pairs={{32,0},{64,32},{96,64},{128,96},{160,128},{192,160},{224,192},{256... | collective-permute-start | bytes 61448 | tf_op jit(solution)/shard_map/ppermute | solution.py:240
  149.5 4.7 %collective-permute-start.10 = (bf16[3,5,16,128]{3,2,1,0:T(8,128)(2,1)S(1)}, bf16[3,5,16,128]{3,2,1,0:T(8,128)(2,1)S(1)}, u32[]{:S(2)}, u32[]{:S(2)}) collective-permute-start(bf16[3,5,16,128]{3,2,1,0:T(8,128)(2,1)S(1)} %pad_maximum_fusion.2.mid), channel_id=1, source_target_pairs={{0,4},{4,8},{8,12},{12,16},{16,20},{20,24},{24,28},{1,5},{5,9},{9,... | collective-permute-start | bytes 184328 | tf_op jit(solution)/shard_map/ppermute | solution.py:240
  152.6 5.0 %collective-permute-start.11 = (bf16[3,5,16,128]{3,2,1,0:T(8,128)(2,1)S(1)}, bf16[3,5,16,128]{3,2,1,0:T(8,128)(2,1)S(1)}, u32[]{:S(2)}, u32[]{:S(2)}) collective-permute-start(bf16[3,5,16,128]{3,2,1,0:T(8,128)(2,1)S(1)} %pad_maximum_fusion.2.mid), channel_id=1, source_target_pairs={{4,0},{8,4},{12,8},{16,12},{20,16},{24,20},{28,24},{5,1},{9,5},{13... | collective-permute-start | bytes 184328 | tf_op jit(solution)/shard_map/ppermute | solution.py:240
  195.2 18.7 %all-to-all-start.8 = ((f32[32,24,128]{2,1,0:T(8,128)}), f32[32,24,128]{2,1,0:T(8,128)S(1)}, u32[]{:S(2)}, u32[]{:S(2)}) async-start(f32[32,24,128]{2,1,0:T(8,128)} %broadcast_in_dim.26), calls=%async_computation.8 | async-start | bytes 786432 | tf_op jit(solution)/shard_map/all_to_all | solution.py:261

commit v2 on v1

--- a/solution.py
+++ b/solution.py
@@ -50,7 +50,7 @@
         first = jnp.where((at >= 8 * r) & (at < 8 * r + 2), turned, first)
         start = (8 * r - 2) % LANES
         last = jnp.where((at >= start) & (at < start + 2), turned, last)
-    return first.astype(bf16), last.astype(bf16)
+    return first.astype(rows[0].dtype), last.astype(rows[0].dtype)
 
 
 def widen(blocks, wide_ref):
@@ -92,10 +92,9 @@
     return sums[:size] + sums[size:]
 
 
-def gather(table, ids):
+def gather(both, ids):
     group, cell = ids >> 9, ids & (CELLS - 1)
-    size = table.shape[0]
-    both = jnp.concatenate(split(table), axis=0)
+    size = both.shape[0] // 2
     found = jnp.dot(both, hot(cell), preferred_element_type=f32)
     found = found[:size] + found[size:]
     part = size // GROUPS
@@ -105,17 +104,22 @@
     return picked
 
 
-def store_tiles(tiles_ref, array):
-    rows, cols = array.shape[0] // 8, array.shape[1] // LANES
+def store_tiles(tiles_ref, array, first=0):
+    lines = tiles_ref.shape[1]
+    rows, cols = array.shape[0] // lines, array.shape[1] // LANES
     for i in range(rows):
         for k in range(cols):
-            tiles_ref[i * cols + k] = array[8 * i : 8 * i + 8, LANES * k : LANES * (k + 1)]
+            tile = array[lines * i : lines * (i + 1), LANES * k : LANES * (k + 1)]
+            tiles_ref[(first + i) * cols + k] = tile.astype(tiles_ref.dtype)
 
 
 def load_tiles(tiles_ref, first, count):
     cols = 4
     return jnp.concatenate(
-        [jnp.concatenate([tiles_ref[i * cols + k] for k in range(cols)], axis=1) for i in range(first, first + count)],
+        [
+            jnp.concatenate([tiles_ref[i * cols + k].astype(f32) for k in range(cols)], axis=1)
+            for i in range(first, first + count)
+        ],
         axis=0,
     )
 
@@ -148,21 +152,27 @@
     store_tiles(tiles_ref, scatter(values, ids_ref[...]))
 
 
-def direct_kernel(place, tiles_ref, embed_ref, ids_ref, direct_ref, share_ref, out_ref):
+def direct_kernel(place, tiles_ref, embed_ref, ids_ref, rows_ref, first_ref, last_ref, shares_ref, out_ref):
     centers, table = [], []
+    row = lax.broadcasted_iota(jnp.int32, (16, CELLS), 0)
     for g in range(GROUPS):
         part = load_tiles(tiles_ref, 4 * g, 3)
         counts = part[EMBED : EMBED + 1]
         centers.append(part[:EMBED] / counts)
-        row = lax.broadcasted_iota(jnp.int32, (16, CELLS), 0)
+        shares_ref[EMBED * g : EMBED * (g + 1)] = jnp.broadcast_to(1.0 / counts, (EMBED, CELLS))
         table += [centers[g], jnp.where(row == 0, 1.0 / counts, 0.0)]
-    near = gather(jnp.concatenate(table, axis=0), ids_ref[...])
+    near = gather(jnp.concatenate(split(jnp.concatenate(table, axis=0)), axis=0), ids_ref[...])
     share = near[EMBED : EMBED + 1]
     offset = embed_ref[...] - near[:EMBED]
     hinge = jnp.maximum(jnp.sum(offset * offset, axis=0, keepdims=True) - pull_margin, 0.0)
     direct = (4.0 / SEGMENTS) * hinge * share * offset
-    direct_ref[...] = direct
-    share_ref[...] = jnp.broadcast_to(share, share_ref.shape)
+    row = lax.broadcasted_iota(jnp.int32, (8, CELLS), 0)
+    marks = jnp.where(row == 0, ids_ref[...].astype(f32), jnp.where(row == 1, 1.0, 0.0))
+    sent = jnp.concatenate([direct, marks], axis=0)
+    rows = [sent[:, LANES * r : LANES * (r + 1)] for r in range(4)]
+    for r in range(4):
+        rows_ref[r] = rows[r]
+    first_ref[...], last_ref[...] = edges(rows)
     sums = scatter(direct, ids_ref[...])
     mine = lane((EMBED, CELLS)) == place[3]
     scale = 8.0 / (SEGMENTS * (SEGMENTS - 1.0))
@@ -175,22 +185,30 @@
             total = total + jnp.maximum(push_margin - distance, 0.0) * difference
         push = -scale * jnp.sum(total, axis=1, keepdims=True)
         grad = jnp.where(mine, push, 0.0) - sums[EMBED * g : EMBED * (g + 1)]
-        for i in range(2):
-            for k in range(4):
-                out_ref[(2 * g + i) * 4 + k] = grad[8 * i : 8 * i + 8, LANES * k : LANES * (k + 1)]
-
-
-def upstream_kernel(tiles_ref, direct_ref, share_ref, ids_ref, rows_ref, first_ref, last_ref):
-    found = gather(load_tiles(tiles_ref, 0, 8), ids_ref[...])
-    upstream = (VOXELS * (direct_ref[...] + found * share_ref[0:1])).astype(bf16)
-    rows = [upstream[:, LANES * r : LANES * (r + 1)] for r in range(4)]
-    for r in range(4):
-        rows_ref[r] = rows[r]
-    first_ref[...], last_ref[...] = edges(rows)
-
-
-def backward_kernel(low, mid, high, wide_ref, hidden_ref, taps_two, taps_one, features_ref, tiles_ref, up_ref, grad_ref):
-    widen((low, mid, high), up_ref)
+        store_tiles(out_ref, grad, g)
+
+
+def backward_kernel(
+    low, mid, high, sums_ref, shares_ref, wide_ref, hidden_ref, taps_two, taps_one, features_ref, tiles_ref, up_ref, grad_ref
+):
+    table = jnp.concatenate(split(load_tiles(sums_ref, 0, 4) * shares_ref[...]), axis=0)
+
+    for yb, ref in enumerate((low, mid, high)):
+
+        def block(zb, carry):
+            sent = jnp.concatenate([ref[zb, r] for r in range(5)], axis=1)
+            ids = sent[EMBED : EMBED + 1].astype(jnp.int32)
+            found = gather(table, ids) * sent[EMBED + 1 : EMBED + 2]
+            upstream = VOXELS * (sent[:EMBED] + found)
+            pack = upstream[:, 4 * LANES :]
+            for r in range(4):
+                edge = pack if r == 0 else pltpu.roll(pack, LANES - 8 * r, 1)
+                z, y = 2 * zb + r // 2, 2 * yb + r % 2
+                up_ref[z, y, :, 0:LANES] = upstream[:, LANES * r : LANES * (r + 1)].astype(bf16)
+                up_ref[z, y, :, LANES:WIDE] = edge.astype(bf16)
+            return carry
+
+        lax.fori_loop(0, 3, block, 0)
 
     def layer(z, carry):
         for y in range(4):
@@ -218,17 +236,17 @@
         )
     one = jnp.concatenate([one, jnp.zeros((3 * CHANNELS, 64), f32)], axis=1)
     two = jnp.concatenate([two, jnp.zeros((3 * EMBED, 80), f32)], axis=1)
-    store_tiles(tiles_ref, jnp.concatenate([one, two], axis=0))
+    store_tiles(tiles_ref, jnp.concatenate([one, two, jnp.zeros((64, 512), f32)], axis=0))
 
 
 def result_kernel(tiles_ref, one_ref, bias_ref, two_ref):
     for c in range(3):
-        part = load_tiles(tiles_ref, 6 * c, 6) * (1.0 / VOXELS)
+        part = load_tiles(tiles_ref, 3 * c, 3) * (1.0 / VOXELS)
         for ab in range(9):
             one_ref[ab * 3 + c] = part[:, CHANNELS * ab : CHANNELS * (ab + 1)]
         if c == 1:
             bias_ref[...] = part[:, 9 * CHANNELS : 9 * CHANNELS + 1]
-        part = load_tiles(tiles_ref, 18 + 2 * c, 2) * (1.0 / VOXELS)
+        part = load_tiles(tiles_ref, 9 + c, 1) * (1.0 / VOXELS)
         for ab in range(9):
             two_ref[ab * 3 + c] = part[:, CHANNELS * ab : CHANNELS * (ab + 1)]
 
@@ -240,25 +258,53 @@
     return lax.ppermute(high, axis, forward), lax.ppermute(low, axis, backward)
 
 
-def surround(rows, first, last):
+def surround(rows, first, last, between=()):
+    between = list(between) + [lambda held: held] * 3
     left, right = passed(first, last, "gx")
+    left, right = between[0]((left, right))
     block = jnp.concatenate([rows, (left + right)[None]], axis=0)
     low, high = passed(block, block, "gz")
+    low, high = between[1]((low, high))
     block = jnp.stack([low, block, high])
     low, high = passed(block, block, "gy")
+    low, high = between[2]((low, high))
     return low, block, high
 
 
-def total(tiles):
-    plane = lax.axis_size(("gy", "gx"))
-    depth = lax.axis_size("gz")
-    lines = tiles.shape[0] // plane * 8
-    pieces = tiles.reshape(plane, lines, LANES)
-    piece = jnp.sum(lax.all_to_all(pieces, ("gy", "gx"), 0, 0), 0)
-    pieces = jnp.broadcast_to(piece[None], (depth, lines, LANES))
-    piece = jnp.sum(lax.all_to_all(pieces, "gz", 0, 0), 0)
-    pieces = jnp.broadcast_to(piece[None], (plane, lines, LANES))
-    return lax.all_to_all(pieces, ("gy", "gx"), 0, 0).reshape(tiles.shape)
+def add_up(pieces):
+    return jnp.sum(pieces.astype(f32), 0).astype(pieces.dtype)
+
+
+def copies(piece, axes):
+    return jnp.broadcast_to(piece[None], (lax.axis_size(axes),) + piece.shape)
+
+
+def steps(tiles, outer, inner):
+    held = [tiles.reshape(lax.axis_size(outer), -1, LANES)]
+
+    def scattered(other):
+        other, pieces = lax.optimization_barrier((other, lax.all_to_all(held[0], outer, 0, 0)))
+        held[0] = copies(add_up(pieces), inner)
+        return other
+
+    def exchanged(other):
+        other, pieces = lax.optimization_barrier((other, lax.all_to_all(held[0], inner, 0, 0)))
+        held[0] = copies(add_up(pieces), outer)
+        return other
+
+    def gathered(other):
+        other, pieces = lax.optimization_barrier((other, lax.all_to_all(held[0], outer, 0, 0)))
+        held[0] = pieces.reshape(tiles.shape)
+        return other
+
+    return (scattered, exchanged, gathered), held
+
+
+def total(tiles, outer, inner):
+    moves, held = steps(tiles, outer, inner)
+    for move in moves:
+        move(())
+    return held[0]
 
 
 def shards(features, segment_ids, kernel_one, bias_one, kernel_two):
@@ -287,24 +333,29 @@
         ],
         scalars=1,
     )(place, low, mid, high, taps_one, taps_two, bias_one[:, None], ids)
-    tiles = total(tiles)
-    direct, share, tiles = kernel_call(
-        direct_kernel, [((EMBED, CELLS), f32), ((8, CELLS), f32), ((32, 8, LANES), f32)], scalars=1
+    tiles = total(tiles, ("gy", "gx"), "gz")
+    rows, first, last, shares, tiles = kernel_call(
+        direct_kernel,
+        [
+            ((4, 24, LANES), f32),
+            ((24, LANES), f32),
+            ((24, LANES), f32),
+            ((GROUPS * EMBED, CELLS), f32),
+            ((16, 16, LANES), bf16),
+        ],
+        scalars=1,
     )(place, tiles, embedding, ids)
-    tiles = total(tiles)
-    rows, first, last = kernel_call(
-        upstream_kernel, [((4, EMBED, LANES), bf16), ((EMBED, LANES), bf16), ((EMBED, LANES), bf16)]
-    )(tiles, direct, share, ids)
-    low, mid, high = surround(rows, first, last)
+    moves, held = steps(tiles, "gz", ("gy", "gx"))
+    low, mid, high = surround(rows, first, last, moves)
     rows, tiles = kernel_call(
         backward_kernel,
-        [((4, CHANNELS, LANES), bf16), ((96, 8, LANES), f32)],
+        [((4, CHANNELS, LANES), bf16), ((64, 16, LANES), bf16)],
         scratch=[((6, 6, EMBED, WIDE), bf16), ((4, 4, CHANNELS, WIDE), bf16)],
-    )(low, mid, high, wide, hidden, back_two, back_one)
+    )(low, mid, high, held[0], shares, wide, hidden, back_two, back_one)
     grad_features = jnp.transpose(rows.reshape(2, 2, CHANNELS, LANES), (2, 0, 1, 3))
     grad_one, grad_bias, grad_two = kernel_call(
         result_kernel, [((27, CHANNELS, CHANNELS), f32), ((CHANNELS, 1), f32), ((27, EMBED, CHANNELS), f32)]
-    )(total(tiles))
+    )(total(tiles, ("gy", "gx"), "gz"))
     return (
         grad_features,
         grad_one.reshape(3, 3, 3, CHANNELS, CHANNELS),

time: 217 us -> 202 us (0.931)
  blocking collectives: 132 us -> 91.3 us
  starting transfers between devices: 36.6 us -> 57.2 us
  Pallas kernels: 7.92 us -> 11.4 us
    all_to_all x8 -> x5, blocking collectives: 132 us -> 91.3 us  [the longest x2 41.5 us: scattered(): lax.all_to_all(held[0], outer, 0, 0)]
    all_to_all x1 -> x4, starting transfers between devices: 4 us -> 22.6 us  [the longest x2 13.9 us: gathered(): lax.all_to_all(held[0], outer, 0, 0)]
    ppermute x6, waiting for transfers between devices: 18.3 us -> 8.72 us  [passed(): lax.ppermute(low, axis, backward)]
    all_to_all x1 -> x4, waiting for transfers between devices: 14 us -> 22.1 us  [the longest x2 19.1 us: gathered(): lax.all_to_all(held[0], outer, 0, 0)]
    ppermute x6, starting transfers between devices: 9.67 us -> 15.7 us  [passed(): lax.ppermute(low, axis, backward)]
    ppermute x6, starting transfers between devices: 22.9 us -> 18.9 us  [passed(): lax.ppermute(high, axis, forward)]
    pallas_call x6 -> x5, Pallas kernels: 7.92 us -> 11.4 us  [call(): pl.pallas_call(body, out_shape=[jax.ShapeDtypeStruct(shape, dtype) for sh...]
    ppermute x6, waiting for transfers between devices: 0.02 us -> 3.15 us  [passed(): lax.ppermute(high, axis, forward)]
  transfers between devices with their start and end apart: 13 -> 16, of which waited for: 7 -> 11; matrix products, arithmetic and copies ran while one was open for 1% -> 1% of each run, Pallas kernels for 0% -> 0%
where the time goes in v2:
time: 202 us; the launch traced here: 201 us
  blocking collectives  91.3 us (45%)
  starting transfers between devices  57.2 us (28%)
  waiting for transfers between devices  34 us (17%)
  Pallas kernels  11.4 us (6%)
  local copies, waits for them, and re-layouts  5.18 us (3%)
    all_to_all x2, blocking collectives, scattered(): lax.all_to_all(held[0], outer, 0, 0)  41.5 us
    all_to_all x2, blocking collectives, exchanged(): lax.all_to_all(held[0], inner, 0, 0)  34 us
    all_to_all x2, waiting for transfers between devices, gathered(): lax.all_to_all(held[0], outer, 0, 0)  19.1 us
    ppermute x6, starting transfers between devices, passed(): lax.ppermute(high, axis, forward)  18.9 us
    all_to_all x1, blocking collectives, gathered(): lax.all_to_all(held[0], outer, 0, 0)  15.8 us
    ppermute x6, starting transfers between devices, passed(): lax.ppermute(low, axis, backward)  15.7 us
    all_to_all x2, starting transfers between devices, gathered(): lax.all_to_all(held[0], outer, 0, 0)  13.9 us
    pallas_call x5, Pallas kernels, call(): pl.pallas_call(body, out_shape=[jax.ShapeDtypeStruct(shape, dtype) for sh...  11.4 us
  transfers between devices with their start and end apart: 16, of which 11 were waited for; matrix products, arithmetic and copies ran while one was open for 1% of the time, Pallas kernels for 0%

profile of v2, /device:TPU:1, one launch (start us, length us, event | category | flops | bytes accessed | tf_op | source)
XLA Modules:
  0.0 200.9 jit_solution(46265161395550704)
XLA Ops:
  1.5 3.9 %collective-permute-start = (bf16[48,128]{1,0:T(8,128)(2,1)S(1)}, bf16[48,128]{1,0:T(8,128)(2,1)S(1)}, u32[]{:S(2)}, u32[]{:S(2)}) collective-permute-start(bf16[48,128]{1,0:T(8,128)(2,1)S(1)} %get-tuple-element.29), channel_id=1, source_target_pairs={{0,1},{1,2},{2,3},{4,5},{5,6},{6,7},{8,9},{9,10},{10,11},{12,13},{... | collective-permute-start | bytes 36872 | tf_op jit(solution)/shard_map/ppermute | solution.py:258
  5.5 1.3 collective-permute-start.1
  6.8 3.1 %collective-permute-done.1 = bf16[48,128]{1,0:T(8,128)(2,1)S(1)} collective-permute-done((bf16[48,128]{1,0:T(8,128)(2,1)S(1)}, bf16[48,128]{1,0:T(8,128)(2,1)S(1)}, u32[]{:S(2)}, u32[]{:S(2)}) %collective-permute-start.1) | collective-permute-done | bytes 12320 | tf_op jit(solution)/shard_map/ppermute | solution.py:258
  9.9 7.3 %collective-permute-start.3 = (bf16[5,48,128]{2,1,0:T(8,128)(2,1)S(1)}, bf16[5,48,128]{2,1,0:T(8,128)(2,1)S(1)}, u32[]{:S(2)}, u32[]{:S(2)}) collective-permute-start(bf16[5,48,128]{2,1,0:T(8,128)(2,1)S(1)} %get-tuple-element.57), channel_id=1, source_target_pairs={{32,0},{64,32},{96,64},{128,96},{160,128},{192,160},{224,192},{256... | collective-permute-start | bytes 184328 | tf_op jit(solution)/shard_map/ppermute | solution.py:258
  17.2 1.9 collective-permute-start.2
  19.2 1.3 collective-permute-done.2
  20.5 1.4 collective-permute-start.5
  21.9 4.0 %collective-permute-start.4 = (bf16[3,5,48,128]{3,2,1,0:T(8,128)(2,1)S(1)}, bf16[3,5,48,128]{3,2,1,0:T(8,128)(2,1)S(1)}, u32[]{:S(2)}, u32[]{:S(2)}) collective-permute-start(bf16[3,5,48,128]{3,2,1,0:T(8,128)(2,1)S(1)} %pad_maximum_fusion.mid), channel_id=1, source_target_pairs={{0,4},{4,8},{8,12},{12,16},{16,20},{20,24},{24,28},{1,5},{5,9},{9,... | collective-permute-start | bytes 552968 | tf_op jit(solution)/shard_map/ppermute | solution.py:258
  26.8 1.9 collective-permute-done.5.high
  29.6 2.9 %shard_map.85 = (bf16[6,6,48,256]{3,2,1,0:T(8,128)(2,1)S(1)}, bf16[4,4,48,256]{3,2,1,0:T(8,128)(2,1)S(1)}, f32[16,512]{1,0:T(8,128)S(1)}, f32[64,8,128]{2,1,0:T(8,128)S(1)}) custom-call(s32[7]{0:T(128)S(1)} %stack.43.place, bf16[3,5,48,128]{3,2,1,0:T(8,128)(2,1)S(1)} %collective-permute-done.4.low, bf16[3,5,48,128]{3,2,1,0:T(8,128)(2,1)S(1)} %pad_maximum_fusion.mid, ...), custom_call_target="tpu_custom_call" | custom-call | tf_op jit(solution)/shard_map/pallas_call | solution.py:28
  32.5 22.2 %all_to_all.45 = f32[32,16,128]{2,1,0:T(8,128)S(1)} all-to-all(f32[32,16,128]{2,1,0:T(8,128)S(1)} %bitcast.43), channel_id=1, replica_groups=mesh['gz'=16,'gy'=8,'gx'=4] {'gy','gx'}, dimensions={0} | all-to-all | bytes 524288 | tf_op jit(solution)/shard_map/all_to_all | solution.py:286
  54.8 20.2 %all_to_all.46 = f32[16,16,128]{2,1,0:T(8,128)S(1)} all-to-all(f32[16,16,128]{2,1,0:T(8,128)S(1)} %broadcast_in_dim.20), channel_id=1, replica_groups=mesh['gz'=16,'gy'=8,'gx'=4] {'gz'}, dimensions={0} | all-to-all | bytes 262144 | tf_op jit(solution)/shard_map/all_to_all | solution.py:291
  75.0 15.8 %all_to_all.47 = f32[32,16,128]{2,1,0:T(8,128)S(1)} all-to-all(f32[32,16,128]{2,1,0:T(8,128)S(1)} %broadcast_in_dim.21), channel_id=1, replica_groups=mesh['gz'=16,'gy'=8,'gx'=4] {'gy','gx'}, dimensions={0} | all-to-all | bytes 524288 | tf_op jit(solution)/shard_map/all_to_all | solution.py:296
  90.9 1.8 shard_map.86
  92.7 4.8 %all-to-all-start.3 = ((bf16[16,16,128]{2,1,0:T(8,128)(2,1)}), bf16[16,16,128]{2,1,0:T(8,128)(2,1)S(1)}, u32[]{:S(2)}, u32[]{:S(2)}) async-start(bf16[16,16,128]{2,1,0:T(8,128)(2,1)} %get-tuple-element.36), calls=%async_computation.3 | async-start | bytes 131072 | tf_op jit(solution)/shard_map/all_to_all | solution.py:286
  97.5 1.7 collective-permute-start.6
  99.3 1.3 collective-permute-start.7
  100.6 3.4 %collective-permute-done.7 = f32[24,128]{1,0:T(8,128)S(1)} collective-permute-done((f32[24,128]{1,0:T(8,128)S(1)}, f32[24,128]{1,0:T(8,128)S(1)}, u32[]{:S(2)}, u32[]{:S(2)}) %collective-permute-start.7) | collective-permute-done | bytes 12320 | tf_op jit(solution)/shard_map/ppermute | solution.py:258
  104.0 1.4 all-to-all-done.3
  106.1 3.9 %all-to-all-start.4 = ((bf16[32,16,128]{2,1,0:T(8,128)(2,1)}), bf16[32,16,128]{2,1,0:T(8,128)(2,1)S(1)}, u32[]{:S(2)}, u32[]{:S(2)}) async-start(bf16[32,16,128]{2,1,0:T(8,128)(2,1)} %broadcast_in_dim.23), calls=%async_computation.4 | async-start | bytes 262144 | tf_op jit(solution)/shard_map/all_to_all | solution.py:291
  110.0 3.1 %collective-permute-start.9 = (f32[5,24,128]{2,1,0:T(8,128)S(1)}, f32[5,24,128]{2,1,0:T(8,128)S(1)}, u32[]{:S(2)}, u32[]{:S(2)}) collective-permute-start(f32[5,24,128]{2,1,0:T(8,128)S(1)} %get-tuple-element.55), channel_id=1, source_target_pairs={{32,0},{64,32},{96,64},{128,96},{160,128},{192,160},{224,192},{256... | collective-permute-start | bytes 184328 | tf_op jit(solution)/shard_map/ppermute | solution.py:258
  113.1 3.3 %collective-permute-start.8 = (f32[5,24,128]{2,1,0:T(8,128)S(1)}, f32[5,24,128]{2,1,0:T(8,128)S(1)}, u32[]{:S(2)}, u32[]{:S(2)}) collective-permute-start(f32[5,24,128]{2,1,0:T(8,128)S(1)} %get-tuple-element.55), channel_id=1, source_target_pairs={{0,32},{32,64},{64,96},{96,128},{128,160},{160,192},{192,224},{224... | collective-permute-start | bytes 184328 | tf_op jit(solution)/shard_map/ppermute | solution.py:258
  117.7 1.6 all-to-all-done.4
  119.4 1.3 collective-permute-start.11
  120.7 4.0 %collective-permute-start.10 = (f32[3,5,24,128]{3,2,1,0:T(8,128)S(1)}, f32[3,5,24,128]{3,2,1,0:T(8,128)S(1)}, u32[]{:S(2)}, u32[]{:S(2)}) collective-permute-start(f32[3,5,24,128]{3,2,1,0:T(8,128)S(1)} %pad_maximum_fusion.1.mid), channel_id=1, source_target_pairs={{0,4},{4,8},{8,12},{12,16},{16,20},{20,24},{24,28},{1,5},{5,9},{9,... | collective-permute-start | bytes 552968 | tf_op jit(solution)/shard_map/ppermute | solution.py:258
  125.4 10.0 %all-to-all-start.5 = ((bf16[16,16,128]{2,1,0:T(8,128)(2,1)}), bf16[16,16,128]{2,1,0:T(8,128)(2,1)S(1)}, u32[]{:S(2)}, u32[]{:S(2)}) async-start(bf16[16,16,128]{2,1,0:T(8,128)(2,1)} %broadcast_in_dim.24), calls=%async_computation.5 | async-start | bytes 131072 | tf_op jit(solution)/shard_map/all_to_all | solution.py:296
  136.2 7.0 %all-to-all-done.5.sums_ref = bf16[16,16,128]{2,1,0:T(8,128)(2,1)S(1)} async-done(((bf16[16,16,128]{2,1,0:T(8,128)(2,1)}), bf16[16,16,128]{2,1,0:T(8,128)(2,1)S(1)}, u32[]{:S(2)}, u32[]{:S(2)}) %all-to-all-start.5) | async-done | bytes 65568 | tf_op jit(solution)/shard_map/all_to_all | solution.py:296
  143.2 5.4 %shard_map.87 = (bf16[4,48,128]{2,1,0:T(8,128)(2,1)S(1)}, bf16[64,16,128]{2,1,0:T(8,128)(2,1)S(1)}) custom-call(f32[3,5,24,128]{3,2,1,0:T(8,128)S(1)} %collective-permute-done.10.low, f32[3,5,24,128]{3,2,1,0:T(8,128)S(1)} %pad_maximum_fusion.1.mid, f32[3,5,24,128]{3,2,1,0:T(8,128)S(1)} %collective-permute-done.11.high, ...), custom_call_target="tpu_custom_call" | custom-call | tf_op jit(solution)/shard_map/pallas_call | solution.py:28
  148.5 19.2 %all_to_all.48 = bf16[32,32,128]{2,1,0:T(8,128)(2,1)S(1)} all-to-all(bf16[32,32,128]{2,1,0:T(8,128)(2,1)S(1)} %bitcast.42), channel_id=1, replica_groups=mesh['gz'=16,'gy'=8,'gx'=4] {'gy','gx'}, dimensions={0} | all-to-all | bytes 524288 | tf_op jit(solution)/shard_map/all_to_all | solution.py:286
  167.9 13.8 %all_to_all.49 = bf16[16,32,128]{2,1,0:T(8,128)(2,1)S(1)} all-to-all(bf16[16,32,128]{2,1,0:T(8,128)(2,1)S(1)} %broadcast_in_dim.25), channel_id=1, replica_groups=mesh['gz'=16,'gy'=8,'gx'=4] {'gz'}, dimensions={0} | all-to-all | bytes 262144 | tf_op jit(solution)/shard_map/all_to_all | solution.py:291
  182.4 3.9 %all-to-all-start.8 = ((bf16[32,32,128]{2,1,0:T(8,128)(2,1)}), bf16[32,32,128]{2,1,0:T(8,128)(2,1)S(1)}, u32[]{:S(2)}, u32[]{:S(2)}) async-start(bf16[32,32,128]{2,1,0:T(8,128)(2,1)} %broadcast_in_dim.26), calls=%async_computation.8 | async-start | bytes 524288 | tf_op jit(solution)/shard_map/all_to_all | solution.py:296
  186.9 12.2 %all-to-all-done.8 = bf16[32,32,128]{2,1,0:T(8,128)(2,1)S(1)} async-done(((bf16[32,32,128]{2,1,0:T(8,128)(2,1)}), bf16[32,32,128]{2,1,0:T(8,128)(2,1)S(1)}, u32[]{:S(2)}, u32[]{:S(2)}) %all-to-all-start.8) | async-done | bytes 262176 | tf_op jit(solution)/shard_map/all_to_all | solution.py:296
  (52 shorter events, 9.5 us)
Async XLA Ops:
  1.5 5.3 %collective-permute-start = (bf16[48,128]{1,0:T(8,128)(2,1)S(1)}, bf16[48,128]{1,0:T(8,128)(2,1)S(1)}, u32[]{:S(2)}, u32[]{:S(2)}) collective-permute-start(bf16[48,128]{1,0:T(8,128)(2,1)S(1)} %get-tuple-element.29), channel_id=1, source_target_pairs={{0,1},{1,2},{2,3},{4,5},{5,6},{6,7},{8,9},{9,10},{10,11},{12,13},{... | collective-permute-start | bytes 36872 | tf_op jit(solution)/shard_map/ppermute | solution.py:258
  5.5 4.4 %collective-permute-start.1 = (bf16[48,128]{1,0:T(8,128)(2,1)S(1)}, bf16[48,128]{1,0:T(8,128)(2,1)S(1)}, u32[]{:S(2)}, u32[]{:S(2)}) collective-permute-start(bf16[48,128]{1,0:T(8,128)(2,1)S(1)} %get-tuple-element.30), channel_id=1, source_target_pairs={{1,0},{2,1},{3,2},{5,4},{6,5},{7,6},{9,8},{10,9},{11,10},{13,12},{... | collective-permute-start | bytes 36872 | tf_op jit(solution)/shard_map/ppermute | solution.py:258
  9.9 9.2 %collective-permute-start.3 = (bf16[5,48,128]{2,1,0:T(8,128)(2,1)S(1)}, bf16[5,48,128]{2,1,0:T(8,128)(2,1)S(1)}, u32[]{:S(2)}, u32[]{:S(2)}) collective-permute-start(bf16[5,48,128]{2,1,0:T(8,128)(2,1)S(1)} %get-tuple-element.57), channel_id=1, source_target_pairs={{32,0},{64,32},{96,64},{128,96},{160,128},{192,160},{224,192},{256... | collective-permute-start | bytes 184328 | tf_op jit(solution)/shard_map/ppermute | solution.py:258
  17.2 3.2 %collective-permute-start.2 = (bf16[5,48,128]{2,1,0:T(8,128)(2,1)S(1)}, bf16[5,48,128]{2,1,0:T(8,128)(2,1)S(1)}, u32[]{:S(2)}, u32[]{:S(2)}) collective-permute-start(bf16[5,48,128]{2,1,0:T(8,128)(2,1)S(1)} %get-tuple-element.57), channel_id=1, source_target_pairs={{0,32},{32,64},{64,96},{96,128},{128,160},{160,192},{192,224},{224... | collective-permute-start | bytes 184328 | tf_op jit(solution)/shard_map/ppermute | solution.py:258
  20.4 5.5 %copy-start.3 = (f32[48]{0:T(128)S(1)}, f32[48]{0:T(128)}, u32[]{:S(2)}) copy-start(f32[48]{0:T(128)} %param.8) | copy-start | bytes 580
  20.4 5.6 %copy-start.2 = (bf16[3,3,3,16,48]{4,3,2,1,0:T(8,128)(2,1)S(1)}, bf16[3,3,3,16,48]{4,3,2,1,0:T(8,128)(2,1)}, u32[]{:S(2)}) copy-start(bf16[3,3,3,16,48]{4,3,2,1,0:T(8,128)(2,1)} %param.9) | copy-start | bytes 124420
  20.5 5.8 %copy-start.1 = (bf16[3,3,3,48,48]{4,3,2,1,0:T(8,128)(2,1)S(1)}, bf16[3,3,3,48,48]{4,3,2,1,0:T(8,128)(2,1)}, u32[]{:S(2)}) copy-start(bf16[3,3,3,48,48]{4,3,2,1,0:T(8,128)(2,1)} %param.7) | copy-start | bytes 373252
  20.5 8.2 %collective-permute-start.5 = (bf16[3,5,48,128]{3,2,1,0:T(8,128)(2,1)S(1)}, bf16[3,5,48,128]{3,2,1,0:T(8,128)(2,1)S(1)}, u32[]{:S(2)}, u32[]{:S(2)}) collective-permute-start(bf16[3,5,48,128]{3,2,1,0:T(8,128)(2,1)S(1)} %pad_maximum_fusion.mid), channel_id=1, source_target_pairs={{4,0},{8,4},{12,8},{16,12},{20,16},{24,20},{28,24},{5,1},{9,5},{13... | collective-permute-start | bytes 552968 | tf_op jit(solution)/shard_map/ppermute | solution.py:258
  21.9 7.7 %collective-permute-start.4 = (bf16[3,5,48,128]{3,2,1,0:T(8,128)(2,1)S(1)}, bf16[3,5,48,128]{3,2,1,0:T(8,128)(2,1)S(1)}, u32[]{:S(2)}, u32[]{:S(2)}) collective-permute-start(bf16[3,5,48,128]{3,2,1,0:T(8,128)(2,1)S(1)} %pad_maximum_fusion.mid), channel_id=1, source_target_pairs={{0,4},{4,8},{8,12},{12,16},{16,20},{20,24},{24,28},{1,5},{5,9},{9,... | collective-permute-start | bytes 552968 | tf_op jit(solution)/shard_map/ppermute | solution.py:258
  26.7 2.9 %copy-start = (s32[2,2,128]{2,1,0:T(2,128)S(1)}, s32[2,2,128]{2,1,0:T(2,128)}, u32[]{:S(2)}) copy-start(s32[2,2,128]{2,1,0:T(2,128)} %param.6) | copy-start | bytes 6148
  92.7 12.7 %all-to-all-start.3 = ((bf16[16,16,128]{2,1,0:T(8,128)(2,1)}), bf16[16,16,128]{2,1,0:T(8,128)(2,1)S(1)}, u32[]{:S(2)}, u32[]{:S(2)}) async-start(bf16[16,16,128]{2,1,0:T(8,128)(2,1)} %get-tuple-element.36), calls=%async_computation.3 | async-start | bytes 131072 | tf_op jit(solution)/shard_map/all_to_all | solution.py:286
  97.5 3.0 %collective-permute-start.6 = (f32[24,128]{1,0:T(8,128)S(1)}, f32[24,128]{1,0:T(8,128)S(1)}, u32[]{:S(2)}, u32[]{:S(2)}) collective-permute-start(f32[24,128]{1,0:T(8,128)S(1)} %get-tuple-element.34), channel_id=1, source_target_pairs={{0,1},{1,2},{2,3},{4,5},{5,6},{6,7},{8,9},{9,10},{10,11},{12,13},{... | collective-permute-start | bytes 36872 | tf_op jit(solution)/shard_map/ppermute | solution.py:258
  99.3 4.7 %collective-permute-start.7 = (f32[24,128]{1,0:T(8,128)S(1)}, f32[24,128]{1,0:T(8,128)S(1)}, u32[]{:S(2)}, u32[]{:S(2)}) collective-permute-start(f32[24,128]{1,0:T(8,128)S(1)} %get-tuple-element.35), channel_id=1, source_target_pairs={{1,0},{2,1},{3,2},{5,4},{6,5},{7,6},{9,8},{10,9},{11,10},{13,12},{... | collective-permute-start | bytes 36872 | tf_op jit(solution)/shard_map/ppermute | solution.py:258
  106.1 13.3 %all-to-all-start.4 = ((bf16[32,16,128]{2,1,0:T(8,128)(2,1)}), bf16[32,16,128]{2,1,0:T(8,128)(2,1)S(1)}, u32[]{:S(2)}, u32[]{:S(2)}) async-start(bf16[32,16,128]{2,1,0:T(8,128)(2,1)} %broadcast_in_dim.23), calls=%async_computation.4 | async-start | bytes 262144 | tf_op jit(solution)/shard_map/all_to_all | solution.py:291
  110.0 6.7 %collective-permute-start.9 = (f32[5,24,128]{2,1,0:T(8,128)S(1)}, f32[5,24,128]{2,1,0:T(8,128)S(1)}, u32[]{:S(2)}, u32[]{:S(2)}) collective-permute-start(f32[5,24,128]{2,1,0:T(8,128)S(1)} %get-tuple-element.55), channel_id=1, source_target_pairs={{32,0},{64,32},{96,64},{128,96},{160,128},{192,160},{224,192},{256... | collective-permute-start | bytes 184328 | tf_op jit(solution)/shard_map/ppermute | solution.py:258
  113.1 4.6 %collective-permute-start.8 = (f32[5,24,128]{2,1,0:T(8,128)S(1)}, f32[5,24,128]{2,1,0:T(8,128)S(1)}, u32[]{:S(2)}, u32[]{:S(2)}) collective-permute-start(f32[5,24,128]{2,1,0:T(8,128)S(1)} %get-tuple-element.55), channel_id=1, source_target_pairs={{0,32},{32,64},{64,96},{96,128},{128,160},{160,192},{192,224},{224... | collective-permute-start | bytes 184328 | tf_op jit(solution)/shard_map/ppermute | solution.py:258
  119.4 23.8 %collective-permute-start.11 = (f32[3,5,24,128]{3,2,1,0:T(8,128)S(1)}, f32[3,5,24,128]{3,2,1,0:T(8,128)S(1)}, u32[]{:S(2)}, u32[]{:S(2)}) collective-permute-start(f32[3,5,24,128]{3,2,1,0:T(8,128)S(1)} %pad_maximum_fusion.1.mid), channel_id=1, source_target_pairs={{4,0},{8,4},{12,8},{16,12},{20,16},{24,20},{28,24},{5,1},{9,5},{13... | collective-permute-start | bytes 552968 | tf_op jit(solution)/shard_map/ppermute | solution.py:258
  120.7 22.5 %collective-permute-start.10 = (f32[3,5,24,128]{3,2,1,0:T(8,128)S(1)}, f32[3,5,24,128]{3,2,1,0:T(8,128)S(1)}, u32[]{:S(2)}, u32[]{:S(2)}) collective-permute-start(f32[3,5,24,128]{3,2,1,0:T(8,128)S(1)} %pad_maximum_fusion.1.mid), channel_id=1, source_target_pairs={{0,4},{4,8},{8,12},{12,16},{16,20},{20,24},{24,28},{1,5},{5,9},{9,... | collective-permute-start | bytes 552968 | tf_op jit(solution)/shard_map/ppermute | solution.py:258
  125.4 17.8 %all-to-all-start.5 = ((bf16[16,16,128]{2,1,0:T(8,128)(2,1)}), bf16[16,16,128]{2,1,0:T(8,128)(2,1)S(1)}, u32[]{:S(2)}, u32[]{:S(2)}) async-start(bf16[16,16,128]{2,1,0:T(8,128)(2,1)} %broadcast_in_dim.24), calls=%async_computation.5 | async-start | bytes 131072 | tf_op jit(solution)/shard_map/all_to_all | solution.py:296
  182.4 16.7 %all-to-all-start.8 = ((bf16[32,32,128]{2,1,0:T(8,128)(2,1)}), bf16[32,32,128]{2,1,0:T(8,128)(2,1)S(1)}, u32[]{:S(2)}, u32[]{:S(2)}) async-start(bf16[32,32,128]{2,1,0:T(8,128)(2,1)} %broadcast_in_dim.26), calls=%async_computation.8 | async-start | bytes 524288 | tf_op jit(solution)/shard_map/all_to_all | solution.py:296

commit v3 on v2

v3 whole, which is shorter than its diff:
```python
import functools

import jax
import jax.numpy as jnp
from jax import lax
from jax.experimental import pallas as pl
from jax.experimental.pallas import tpu as pltpu
from jax.sharding import PartitionSpec as P

EMBED = 16
CHANNELS = 48
LANES = 128
WIDE = 2 * LANES
CELLS = 512
GROUPS = 4
ROW_COLS = 512
VOXELS = 262144.0
SEGMENTS = 2048.0
pull_margin = 4.0
push_margin = 8.0
f32, bf16 = jnp.float32, jnp.bfloat16


def kernel_call(body, outs, scratch=(), scalars=0, flops=0):
    def call(*args):
        specs = [pl.BlockSpec(memory_space=pltpu.SMEM)] * scalars
        specs += [pl.BlockSpec(memory_space=pltpu.VMEM)] * (len(args) - scalars)
        return pl.pallas_call(
            body,
            out_shape=[jax.ShapeDtypeStruct(shape, dtype) for shape, dtype in outs],
            in_specs=specs,
            out_specs=[pl.BlockSpec(memory_space=pltpu.VMEM)] * len(outs),
            scratch_shapes=[pltpu.VMEM(shape, dtype) for shape, dtype in scratch],
            compiler_params=pltpu.CompilerParams(vmem_limit_bytes=40 * 1024 * 1024),
        )(*args)

    return call


def lane(shape):
    return lax.broadcasted_iota(jnp.int32, shape, len(shape) - 1)


def edges(rows):
    at = lane(rows[0].shape)
    first = jnp.zeros(rows[0].shape, f32)
    last = jnp.zeros(rows[0].shape, f32)
    for r, row in enumerate(rows):
        turned = row if r == 0 else pltpu.roll(row, 8 * r, 1)
        first = jnp.where((at >= 8 * r) & (at < 8 * r + 4), turned, first)
        start = (8 * r - 4) % LANES
        last = jnp.where((at >= start) & (at < start + 4), turned, last)
    return first, last


def widen(blocks, wide_ref):
    for yb, ref in enumerate(blocks):
        for zb in range(3):
            pack = ref[zb, 4].astype(f32)
            for r in range(4):
                edge = pack if r == 0 else pltpu.roll(pack, LANES - 8 * r, 1)
                z, y = 2 * zb + r // 2, 2 * yb + r % 2
                wide_ref[z, y, :, 0:LANES] = ref[zb, r]
                wide_ref[z, y, :, LANES:WIDE] = edge.astype(bf16)


def window(ref, z, y):
    size = ref.shape[2]
    return jnp.concatenate([ref[z + a, y : y + 3].reshape(3 * size, WIDE) for a in range(3)], axis=0)


def fold(taps):
    size = taps.shape[0] // 3
    return pltpu.roll(taps[:size], 1, 1) + taps[size : 2 * size] + pltpu.roll(taps[2 * size :], WIDE - 1, 1)


def split(value):
    high = value.astype(bf16)
    return high, (value - high.astype(f32)).astype(bf16)


def hot(cell):
    return jnp.where(lax.broadcasted_iota(jnp.int32, (CELLS, cell.shape[1]), 0) == cell, 1.0, 0.0).astype(bf16)


def scatter(values, ids, more=()):
    group, cell = ids >> 9, ids & (CELLS - 1)
    spread = jnp.concatenate([jnp.where(group == g, values, 0.0) for g in range(GROUPS)], axis=0)
    size = spread.shape[0]
    both = jnp.concatenate(split(spread) + tuple(more), axis=0)
    sums = lax.dot_general(both, hot(cell), (((1,), (1,)), ((), ())), preferred_element_type=f32)
    return sums[:size] + sums[size : 2 * size], sums[2 * size :]


def gather(parts, ids):
    group, cell = ids >> 9, ids & (CELLS - 1)
    size = parts[0].shape[0]
    found = jnp.dot(jnp.concatenate(parts, axis=0), hot(cell), preferred_element_type=f32)
    found = sum(found[size * i : size * (i + 1)] for i in range(1, len(parts))) + found[:size]
    part = size // GROUPS
    picked = jnp.where(group == 0, found[:part], 0.0)
    for g in range(1, GROUPS):
        picked = picked + jnp.where(group == g, found[g * part : (g + 1) * part], 0.0)
    return picked


def store_lines(lines_ref, array):
    cols = array.shape[1] // LANES
    for i in range(array.shape[0] // 8):
        for k in range(cols):
            start = 8 * (i * cols + k)
            lines_ref[start : start + 8, 0, :] = array[8 * i : 8 * i + 8, LANES * k : LANES * (k + 1)]


def load_lines(lines_ref, first, count):
    cols = 4
    return jnp.concatenate(
        [
            jnp.concatenate([lines_ref[8 * (i * cols + k) : 8 * (i * cols + k) + 8, 0, :] for k in range(cols)], axis=1)
            for i in range(first, first + count)
        ],
        axis=0,
    )


def store_tiles(tiles_ref, array, first=0):
    lines = tiles_ref.shape[1]
    rows, cols = array.shape[0] // lines, array.shape[1] // LANES
    for i in range(rows):
        for k in range(cols):
            tile = array[lines * i : lines * (i + 1), LANES * k : LANES * (k + 1)]
            tiles_ref[(first + i) * cols + k] = tile.astype(tiles_ref.dtype)


def load_tiles(tiles_ref, first, count):
    cols = 4
    return jnp.concatenate(
        [
            jnp.concatenate([tiles_ref[i * cols + k].astype(f32) for k in range(cols)], axis=1)
            for i in range(first, first + count)
        ],
        axis=0,
    )


def edge_kernel(rows_ref, ids_ref, first_ref, last_ref):
    row = lax.broadcasted_iota(jnp.int32, (16, ROW_COLS), 0)
    ids = ids_ref[...]
    marks = jnp.where(row == 0, ids >> 8, jnp.where(row == 1, ids & 255, jnp.where(row == 2, 1, 0))).astype(f32)
    rows = [
        jnp.concatenate([rows_ref[r].astype(f32), marks[:, LANES * r : LANES * (r + 1)]], axis=0) for r in range(4)
    ]
    first, last = edges(rows)
    first_ref[...] = first.astype(bf16)
    last_ref[...] = last.astype(bf16)


def embed_kernel(place, low, mid, high, taps_one, taps_two, bias, ids_ref, wide_ref, hidden_ref, embed_ref, lines_ref):
    widen((low, mid, high), wide_ref)
    gz, gy, gx = place[0], place[1], place[2]
    at = lane((CHANNELS, WIDE))
    inside = (at < LANES) | ((at < LANES + 3) & (gx < place[6])) | ((at >= WIDE - 3) & (gx > 0))

    def layer(z, carry):
        for y in range(4):
            folded = fold(jnp.dot(taps_one[...], window(wide_ref, z, y), preferred_element_type=f32))
            folded = jnp.maximum(folded + bias[...], 0.0)
            depth, row = 2 * gz - 1 + z, 2 * gy - 1 + y
            exists = (depth >= 0) & (depth < 2 * place[4] + 2) & (row >= 0) & (row < 2 * place[5] + 2)
            hidden_ref[z, y] = jnp.where(inside & exists, folded, 0.0).astype(bf16)
        return carry

    lax.fori_loop(0, 4, layer, 0)
    pack = jnp.zeros((EMBED, LANES), f32)
    at = lane((EMBED, LANES))
    for r in range(4):
        folded = fold(jnp.dot(taps_two[...], window(hidden_ref, r // 2, r % 2), preferred_element_type=f32))
        embed_ref[:, LANES * r : LANES * (r + 1)] = folded[:, :LANES]
        edge = folded[:, LANES:] if r == 0 else pltpu.roll(folded[:, LANES:], 8 * r, 1)
        pack = jnp.where(((at - 8 * r + 4) & (LANES - 1)) < 8, edge, pack)
    embed_ref[:, ROW_COLS:] = pack
    ids = ids_ref[...]
    row = lax.broadcasted_iota(jnp.int32, (16, CELLS), 0)
    ones = jnp.where((ids >> 9) == row, 1.0, 0.0).astype(bf16)
    sums, counts = scatter(embed_ref[:, :ROW_COLS], ids, (ones,))
    store_lines(lines_ref, jnp.concatenate([sums, counts[:8]], axis=0))


def direct_kernel(place, lines_ref, embed_ref, ids_ref, pack_ref, direct_ref, out_ref):
    centers, table = [], []
    row = lax.broadcasted_iota(jnp.int32, (16, CELLS), 0)
    counts = load_lines(lines_ref, 8, 1)
    for g in range(GROUPS):
        count = counts[g : g + 1]
        centers.append(load_lines(lines_ref, 2 * g, 2) / count)
        table += [centers[g], jnp.where(row == 0, 1.0 / count, 0.0)]
    pack = pack_ref[...].astype(f32)
    pack_ids = (256.0 * pack[0:1] + pack[1:2]).astype(jnp.int32)
    ids = jnp.concatenate([ids_ref[...], pack_ids], axis=1)
    mark = jnp.concatenate([jnp.ones((1, ROW_COLS), f32), pack[2:3]], axis=1)
    near = gather(split(jnp.concatenate(table, axis=0)), ids)
    share = near[EMBED : EMBED + 1] * mark
    offset = embed_ref[...] - near[:EMBED]
    hinge = jnp.maximum(jnp.sum(offset * offset, axis=0, keepdims=True) - pull_margin, 0.0)
    direct = (4.0 / SEGMENTS) * hinge * share * offset
    row = lax.broadcasted_iota(jnp.int32, (8, ids.shape[1]), 0)
    marks = jnp.where(row == 0, ids.astype(f32), jnp.where(row == 1, share, 0.0))
    direct_ref[...] = jnp.concatenate([direct, marks], axis=0)
    sums, _ = scatter(direct[:, :ROW_COLS], ids_ref[...])
    mine = lane((EMBED, CELLS)) == place[3]
    scale = 8.0 / (SEGMENTS * (SEGMENTS - 1.0))
    for g in range(GROUPS):
        own = jnp.sum(jnp.where(mine, centers[g], 0.0), axis=1, keepdims=True)
        total = jnp.zeros((EMBED, CELLS), f32)
        for other in centers:
            difference = own - other
            distance = jnp.sum(difference * difference, axis=0, keepdims=True)
            total = total + jnp.maximum(push_margin - distance, 0.0) * difference
        push = -scale * jnp.sum(total, axis=1, keepdims=True)
        grad = jnp.where(mine, push, 0.0) - sums[EMBED * g : EMBED * (g + 1)]
        store_tiles(out_ref, grad, g)


def backward_layers(hidden_ref, up_ref, taps_two, grad_ref):
    def layer(z, carry):
        for y in range(4):
            folded = fold(jnp.dot(taps_two[...], window(up_ref, z, y), preferred_element_type=f32))
            grad_ref[z, y] = jnp.where(hidden_ref[z, y].astype(f32) > 0.0, folded, 0.0).astype(bf16)
        return carry

    lax.fori_loop(0, 4, layer, 0)


def kernels_kernel(direct_ref, sums_ref, wide_ref, hidden_ref, taps_two, block_ref, tiles_ref, up_ref, grad_ref):
    table = jnp.concatenate(
        [jnp.concatenate([sums_ref[4 * i + k] for k in range(4)], axis=1) for i in range(GROUPS)], axis=0
    )
    direct = direct_ref[...]
    ids = direct[EMBED : EMBED + 1].astype(jnp.int32)
    upstream = VOXELS * (direct[:EMBED] + gather((table,), ids) * direct[EMBED + 1 : EMBED + 2])
    upstream = upstream.astype(bf16)
    for r in range(5):
        block_ref[r] = upstream[:, LANES * r : LANES * (r + 1)]
    up_ref[...] = jnp.zeros(up_ref.shape, bf16)
    for r in range(4):
        up_ref[2 + r // 2, 2 + r % 2, :, 0:LANES] = upstream[:, LANES * r : LANES * (r + 1)]
    backward_layers(hidden_ref, up_ref, taps_two, grad_ref)
    over_cells = (((1,), (1,)), ((), ()))

    def shifted(row):
        row = row.astype(f32)
        return jnp.concatenate([pltpu.roll(row, WIDE - 1, 1), row, pltpu.roll(row, 1, 1)], axis=0).astype(bf16)

    def layer(z, carry):
        one, bias = carry
        for y in range(4):
            moved = shifted(grad_ref[z, y])
            one = one + lax.dot_general(moved, window(wide_ref, z, y), over_cells, preferred_element_type=f32)
            own = moved[CHANNELS : 2 * CHANNELS]
            bias = bias + lax.dot_general(jnp.ones((16, WIDE), bf16), own, over_cells, preferred_element_type=f32)
        return one, bias

    zeros = jnp.zeros((3 * CHANNELS, 9 * CHANNELS), f32), jnp.zeros((16, CHANNELS), f32)
    one, bias = lax.fori_loop(0, 4, layer, zeros)
    two = jnp.zeros((3 * EMBED, 9 * CHANNELS), f32)
    for r in range(4):
        z, y = r // 2, r % 2
        two = two + lax.dot_general(
            shifted(up_ref[z + 2, y + 2]), window(hidden_ref, z, y), over_cells, preferred_element_type=f32
        )
    one = jnp.concatenate([one, jnp.zeros((3 * CHANNELS, 80), f32)], axis=1)
    bias = jnp.concatenate([bias] * 3, axis=0)
    two = jnp.concatenate([two, bias, jnp.zeros((3 * EMBED, 32), f32)], axis=1)
    store_tiles(tiles_ref, jnp.concatenate([one, two], axis=0))


def features_kernel(low, mid, high, hidden_ref, taps_two, taps_one, features_ref, up_ref, grad_ref):
    widen((low, mid, high), up_ref)
    backward_layers(hidden_ref, up_ref, taps_two, grad_ref)
    for r in range(4):
        folded = fold(jnp.dot(taps_one[...], window(grad_ref, r // 2, r % 2), preferred_element_type=f32))
        features_ref[r] = folded[:, :LANES].astype(bf16)


def result_kernel(tiles_ref, one_ref, bias_ref, two_ref):
    whole = load_tiles(tiles_ref, 0, 8) * (1.0 / VOXELS)
    for c in range(3):
        part = whole[CHANNELS * c : CHANNELS * (c + 1)]
        for ab in range(9):
            one_ref[ab * 3 + c] = part[:, CHANNELS * ab : CHANNELS * (ab + 1)]
        part = whole[3 * CHANNELS + EMBED * c : 3 * CHANNELS + EMBED * (c + 1)]
        for ab in range(9):
            two_ref[ab * 3 + c] = part[:, CHANNELS * ab : CHANNELS * (ab + 1)]
    bias_ref[...] = whole[3 * CHANNELS : 3 * CHANNELS + 1, 9 * CHANNELS : 10 * CHANNELS]


def passed(low, high, axis):
    count = lax.axis_size(axis)
    forward = [(i, i + 1) for i in range(count - 1)]
    backward = [(target, source) for source, target in forward]
    return lax.ppermute(high, axis, forward), lax.ppermute(low, axis, backward)


def surround(block, between=None):
    between = between or [lambda held: held] * 2
    low, high = between[0](passed(block, block, "gz"))
    block = jnp.stack([low, block, high])
    low, high = between[1](passed(block, block, "gy"))
    return low, block, high


def add_up(pieces):
    return jnp.sum(pieces.astype(f32), 0).astype(pieces.dtype)


def copies(piece, axes):
    return jnp.broadcast_to(piece[None], (lax.axis_size(axes),) + piece.shape)


def steps(tiles, outer, inner):
    groups = lax.axis_size(outer)
    held = [tiles.reshape((groups, tiles.shape[0] // groups) + tiles.shape[1:])]

    def scattered(other):
        other, pieces = lax.optimization_barrier((other, lax.all_to_all(held[0], outer, 0, 0)))
        held[0] = copies(add_up(pieces), inner)
        return other

    def exchanged(other):
        other, pieces = lax.optimization_barrier((other, lax.all_to_all(held[0], inner, 0, 0)))
        held[0] = copies(add_up(pieces), outer)
        return other

    def gathered(other):
        other, pieces = lax.optimization_barrier((other, lax.all_to_all(held[0], outer, 0, 0)))
        held[0] = pieces.reshape(tiles.shape)
        return other

    return (scattered, exchanged, gathered), held


def total(tiles, outer, inner):
    moves, held = steps(tiles, outer, inner)
    for move in moves:
        move(())
    return held[0]


def shards(features, segment_ids, kernel_one, bias_one, kernel_two):
    axes = ("gz", "gy", "gx")
    place = jnp.stack(
        [lax.axis_index(axis) for axis in axes]
        + [lax.axis_index(axes)]
        + [jnp.int32(lax.axis_size(axis) - 1) for axis in axes]
    ).astype(jnp.int32)
    taps_one = jnp.transpose(kernel_one, (2, 3, 0, 1, 4)).reshape(3 * CHANNELS, 9 * CHANNELS)
    taps_two = jnp.transpose(kernel_two, (2, 3, 0, 1, 4)).reshape(3 * EMBED, 9 * CHANNELS)
    back_one = jnp.transpose(kernel_one[::-1, ::-1, ::-1], (2, 4, 0, 1, 3)).reshape(3 * CHANNELS, 9 * CHANNELS)
    back_two = jnp.transpose(kernel_two[::-1, ::-1, ::-1], (2, 4, 0, 1, 3)).reshape(3 * CHANNELS, 9 * EMBED)
    ids = segment_ids.reshape(1, ROW_COLS)
    rows = jnp.transpose(features, (1, 2, 0, 3)).reshape(4, CHANNELS, LANES)

    first, last = kernel_call(edge_kernel, [((CHANNELS + 16, LANES), bf16)] * 2)(rows, ids)
    left, right = passed(first, last, "gx")
    pack = left + right
    low, mid, high = surround(jnp.concatenate([rows, pack[None, :CHANNELS]], axis=0))
    wide, hidden, embedding, lines = kernel_call(
        embed_kernel,
        [
            ((6, 6, CHANNELS, WIDE), bf16),
            ((4, 4, CHANNELS, WIDE), bf16),
            ((EMBED, ROW_COLS + LANES), f32),
            ((288, 1, LANES), f32),
        ],
        scalars=1,
    )(place, low, mid, high, taps_one, taps_two, bias_one[:, None], ids)
    lines = total(lines, ("gy", "gx"), "gz")
    direct, tiles = kernel_call(direct_kernel, [((24, ROW_COLS + LANES), f32), ((16, 16, LANES), bf16)], scalars=1)(
        place, lines, embedding, ids, pack[CHANNELS:]
    )
    tiles = total(tiles, "gz", ("gy", "gx"))
    back = [((6, 6, EMBED, WIDE), bf16), ((4, 4, CHANNELS, WIDE), bf16)]
    block, tiles = kernel_call(
        kernels_kernel, [((5, EMBED, LANES), bf16), ((32, 24, LANES), bf16)], scratch=back
    )(direct, tiles, wide, hidden, back_two)
    moves, held = steps(tiles, ("gy", "gx"), "gz")
    low, mid, high = surround(block, moves)
    (rows,) = kernel_call(features_kernel, [((4, CHANNELS, LANES), bf16)], scratch=back)(
        low, mid, high, hidden, back_two, back_one
    )
    moves[2](())
    grad_features = jnp.transpose(rows.reshape(2, 2, CHANNELS, LANES), (2, 0, 1, 3))
    grad_one, grad_bias, grad_two = kernel_call(
        result_kernel, [((27, CHANNELS, CHANNELS), f32), ((1, CHANNELS), f32), ((27, EMBED, CHANNELS), f32)]
    )(held[0])
    return (
        grad_features,
        grad_one.reshape(3, 3, 3, CHANNELS, CHANNELS),
        grad_bias.reshape(CHANNELS),
        grad_two.reshape(3, 3, 3, EMBED, CHANNELS),
    )


def solution(mesh):
    return jax.shard_map(
        shards,
        mesh=mesh,
        in_specs=(P(None, "gz", "gy", "gx"), P("gz", "gy", "gx"), P(), P(), P()),
        out_specs=(P(None, "gz", "gy", "gx"), P(), P(), P()),
        check_vma=False,
    )
```

time: 202 us -> 180 us (0.89)
  blocking collectives: 91.3 us -> 64 us
  waiting for transfers between devices: 34 us -> 44.9 us
  starting transfers between devices: 57.2 us -> 48.3 us
  local copies, waits for them, and re-layouts: 5.18 us -> 7.82 us
    all_to_all x1 -> x0, blocking collectives: 15.8 us -> none  [gathered(): lax.all_to_all(held[0], outer, 0, 0)]
    all_to_all x2, blocking collectives: 41.5 us -> 30.4 us  [scattered(): lax.all_to_all(held[0], outer, 0, 0)]
    ppermute x6 -> x5, waiting for transfers between devices: 8.72 us -> 14.8 us  [passed(): lax.ppermute(low, axis, backward)]
    ppermute x6 -> x5, starting transfers between devices: 18.9 us -> 12.8 us  [passed(): lax.ppermute(high, axis, forward)]
    all_to_all x2 -> x3, waiting for transfers between devices: 19.1 us -> 24.5 us  [gathered(): lax.all_to_all(held[0], outer, 0, 0)]
    ppermute x6 -> x5, starting transfers between devices: 15.7 us -> 13.2 us  [passed(): lax.ppermute(low, axis, backward)]
    pallas_call x5 -> x6, Pallas kernels: 11.4 us -> 12 us  [call(): pl.pallas_call(body, out_shape=[jax.ShapeDtypeStruct(shape, dtype) for sh...]
    all_to_all x2 -> x3, starting transfers between devices: 13.9 us -> 13.3 us  [gathered(): lax.all_to_all(held[0], outer, 0, 0)]
  transfers between devices with their start and end apart: 16 -> 15, of which waited for: 11 -> 11; matrix products, arithmetic and copies ran while one was open for 1% -> 1% of each run, Pallas kernels for 0% -> 1%
where the time goes in v3:
time: 180 us; the launch traced here: 178 us
  blocking collectives  64 us (36%)
  starting transfers between devices  48.3 us (27%)
  waiting for transfers between devices  44.9 us (25%)
  Pallas kernels  12 us (7%)
  local copies, waits for them, and re-layouts  7.82 us (4%)
    all_to_all x2, blocking collectives, exchanged(): lax.all_to_all(held[0], inner, 0, 0)  33.6 us
    all_to_all x2, blocking collectives, scattered(): lax.all_to_all(held[0], outer, 0, 0)  30.4 us
    all_to_all x3, waiting for transfers between devices, gathered(): lax.all_to_all(held[0], outer, 0, 0)  24.5 us
    ppermute x5, waiting for transfers between devices, passed(): lax.ppermute(low, axis, backward)  14.8 us
    all_to_all x3, starting transfers between devices, gathered(): lax.all_to_all(held[0], outer, 0, 0)  13.3 us
    ppermute x5, starting transfers between devices, passed(): lax.ppermute(low, axis, backward)  13.2 us
    ppermute x5, starting transfers between devices, passed(): lax.ppermute(high, axis, forward)  12.8 us
    pallas_call x6, Pallas kernels, call(): pl.pallas_call(body, out_shape=[jax.ShapeDtypeStruct(shape, dtype) for sh...  12 us
  transfers between devices with their start and end apart: 15, of which 11 were waited for; matrix products, arithmetic and copies ran while one was open for 1% of the time, Pallas kernels for 1%

profile of v3, /device:TPU:1, one launch (start us, length us, event | category | flops | bytes accessed | tf_op | source)
XLA Modules:
  0.0 178.4 jit_solution(1751752930127555128)
XLA Ops:
  2.2 4.1 %collective-permute-start = (bf16[64,128]{1,0:T(8,128)(2,1)S(1)}, bf16[64,128]{1,0:T(8,128)(2,1)S(1)}, u32[]{:S(2)}, u32[]{:S(2)}) collective-permute-start(bf16[64,128]{1,0:T(8,128)(2,1)S(1)} %get-tuple-element.23), channel_id=1, source_target_pairs={{0,1},{1,2},{2,3},{4,5},{5,6},{6,7},{8,9},{9,10},{10,11},{12,13},{... | collective-permute-start | bytes 49160 | tf_op jit(solution)/shard_map/ppermute | solution.py:301
  6.3 1.3 collective-permute-start.1
  7.6 3.2 %collective-permute-done.1 = bf16[64,128]{1,0:T(8,128)(2,1)S(1)} collective-permute-done((bf16[64,128]{1,0:T(8,128)(2,1)S(1)}, bf16[64,128]{1,0:T(8,128)(2,1)S(1)}, u32[]{:S(2)}, u32[]{:S(2)}) %collective-permute-start.1) | collective-permute-done | bytes 16416 | tf_op jit(solution)/shard_map/ppermute | solution.py:301
  10.8 7.3 %collective-permute-start.3 = (bf16[5,48,128]{2,1,0:T(8,128)(2,1)S(1)}, bf16[5,48,128]{2,1,0:T(8,128)(2,1)S(1)}, u32[]{:S(2)}, u32[]{:S(2)}) collective-permute-start(bf16[5,48,128]{2,1,0:T(8,128)(2,1)S(1)} %get-tuple-element.43), channel_id=1, source_target_pairs={{32,0},{64,32},{96,64},{128,96},{160,128},{192,160},{224,192},{256... | collective-permute-start | bytes 184328 | tf_op jit(solution)/shard_map/ppermute | solution.py:301
  18.1 1.9 %collective-permute-start.2 = (bf16[5,48,128]{2,1,0:T(8,128)(2,1)S(1)}, bf16[5,48,128]{2,1,0:T(8,128)(2,1)S(1)}, u32[]{:S(2)}, u32[]{:S(2)}) collective-permute-start(bf16[5,48,128]{2,1,0:T(8,128)(2,1)S(1)} %get-tuple-element.43), channel_id=1, source_target_pairs={{0,32},{32,64},{64,96},{96,128},{128,160},{160,192},{192,224},{224... | collective-permute-start | bytes 184328 | tf_op jit(solution)/shard_map/ppermute | solution.py:301
  20.1 1.3 collective-permute-done.2
  21.3 1.9 %collective-permute-start.4 = (bf16[3,5,48,128]{3,2,1,0:T(8,128)(2,1)S(1)}, bf16[3,5,48,128]{3,2,1,0:T(8,128)(2,1)S(1)}, u32[]{:S(2)}, u32[]{:S(2)}) collective-permute-start(bf16[3,5,48,128]{3,2,1,0:T(8,128)(2,1)S(1)} %pad_maximum_fusion.mid), channel_id=1, source_target_pairs={{0,4},{4,8},{8,12},{12,16},{16,20},{20,24},{24,28},{1,5},{5,9},{9,... | collective-permute-start | bytes 552968 | tf_op jit(solution)/shard_map/ppermute | solution.py:301
  23.3 1.3 collective-permute-start.5
  27.4 4.3 %collective-permute-done.5.high = bf16[3,5,48,128]{3,2,1,0:T(8,128)(2,1)S(1)} collective-permute-done((bf16[3,5,48,128]{3,2,1,0:T(8,128)(2,1)S(1)}, bf16[3,5,48,128]{3,2,1,0:T(8,128)(2,1)S(1)}, u32[]{:S(2)}, u32[]{:S(2)}) %collective-permute-start.5) | collective-permute-done | bytes 184352 | tf_op jit(solution)/shard_map/ppermute | solution.py:301
  31.7 2.9 %shard_map.85 = (bf16[6,6,48,256]{3,2,1,0:T(8,128)(2,1)S(1)}, bf16[4,4,48,256]{3,2,1,0:T(8,128)(2,1)S(1)}, f32[16,640]{1,0:T(8,128)S(1)}, f32[288,1,128]{2,1,0:T(1,128)S(1)}) custom-call(s32[7]{0:T(128)S(1)} %stack.43.place, bf16[3,5,48,128]{3,2,1,0:T(8,128)(2,1)S(1)} %collective-permute-done.4.low, bf16[3,5,48,128]{3,2,1,0:T(8,128)(2,1)S(1)} %pad_maximum_fusion.mid, ...), custom_call_target="tpu_custom_call" | custom-call | tf_op jit(solution)/shard_map/pallas_call | solution.py:28
  34.7 18.5 %all_to_all.45 = f32[32,9,1,128]{3,2,1,0:T(1,128)S(1)} all-to-all(f32[32,9,1,128]{3,2,1,0:T(1,128)S(1)} %bitcast.48), channel_id=1, replica_groups=mesh['gz'=16,'gy'=8,'gx'=4] {'gy','gx'}, dimensions={0} | all-to-all | bytes 294912 | tf_op jit(solution)/shard_map/all_to_all | solution.py:325
  53.3 20.8 %all_to_all.46 = f32[16,9,1,128]{3,2,1,0:T(1,128)S(1)} all-to-all(f32[16,9,1,128]{3,2,1,0:T(1,128)S(1)} %broadcast_in_dim.18), channel_id=1, replica_groups=mesh['gz'=16,'gy'=8,'gx'=4] {'gz'}, dimensions={0} | all-to-all | bytes 147456 | tf_op jit(solution)/shard_map/all_to_all | solution.py:330
  74.8 3.9 %all-to-all-start.2 = ((f32[32,9,1,128]{3,2,1,0:T(1,128)}), f32[32,9,1,128]{3,2,1,0:T(1,128)S(1)}, u32[]{:S(2)}, u32[]{:S(2)}) async-start(f32[32,9,1,128]{3,2,1,0:T(1,128)} %broadcast_in_dim.19), calls=%async_computation.2 | async-start | bytes 294912 | tf_op jit(solution)/shard_map/all_to_all | solution.py:335
  78.7 10.1 %all-to-all-done.2 = f32[32,9,1,128]{3,2,1,0:T(1,128)S(1)} async-done(((f32[32,9,1,128]{3,2,1,0:T(1,128)}), f32[32,9,1,128]{3,2,1,0:T(1,128)S(1)}, u32[]{:S(2)}, u32[]{:S(2)}) %all-to-all-start.2) | async-done | bytes 147488 | tf_op jit(solution)/shard_map/all_to_all | solution.py:335
  88.8 1.3 shard_map.86
  90.0 11.9 %all_to_all.47 = bf16[16,1,16,128]{3,2,1,0:T(8,128)(2,1)S(1)} all-to-all(bf16[16,1,16,128]{3,2,1,0:T(8,128)(2,1)S(1)} %bitcast.49), channel_id=1, replica_groups=mesh['gz'=16,'gy'=8,'gx'=4] {'gz'}, dimensions={0} | all-to-all | bytes 131072 | tf_op jit(solution)/shard_map/all_to_all | solution.py:325
  102.0 12.9 %all_to_all.48 = bf16[32,1,16,128]{3,2,1,0:T(8,128)(2,1)S(1)} all-to-all(bf16[32,1,16,128]{3,2,1,0:T(8,128)(2,1)S(1)} %broadcast_in_dim.20), channel_id=1, replica_groups=mesh['gz'=16,'gy'=8,'gx'=4] {'gy','gx'}, dimensions={0} | all-to-all | bytes 262144 | tf_op jit(solution)/shard_map/all_to_all | solution.py:330
  115.6 4.9 %all-to-all-start.5 = ((bf16[16,1,16,128]{3,2,1,0:T(8,128)(2,1)}), bf16[16,1,16,128]{3,2,1,0:T(8,128)(2,1)S(1)}, u32[]{:S(2)}, u32[]{:S(2)}) async-start(bf16[16,1,16,128]{3,2,1,0:T(8,128)(2,1)} %broadcast_in_dim.21), calls=%async_computation.5 | async-start | bytes 131072 | tf_op jit(solution)/shard_map/all_to_all | solution.py:335
  120.7 7.5 %all-to-all-done.5 = bf16[16,1,16,128]{3,2,1,0:T(8,128)(2,1)S(1)} async-done(((bf16[16,1,16,128]{3,2,1,0:T(8,128)(2,1)}), bf16[16,1,16,128]{3,2,1,0:T(8,128)(2,1)S(1)}, u32[]{:S(2)}, u32[]{:S(2)}) %all-to-all-start.5) | async-done | bytes 65568 | tf_op jit(solution)/shard_map/all_to_all | solution.py:335
  128.3 4.7 %shard_map.87 = (bf16[5,16,128]{2,1,0:T(8,128)(2,1)S(1)}, bf16[32,24,128]{2,1,0:T(8,128)(2,1)}) custom-call(f32[24,640]{1,0:T(8,128)S(1)} %get-tuple-element.27.direct_ref, bf16[16,16,128]{2,1,0:T(8,128)(2,1)S(1)} %bitcast.46, bf16[6,6,48,256]{3,2,1,0:T(8,128)(2,1)S(1)} %get-tuple-element.29.wide_ref, ...), custom_call_target="tpu_custom_call" | custom-call | tf_op jit(solution)/shard_map/pallas_call | solution.py:28
  132.9 3.9 %all-to-all-start.6 = ((bf16[32,1,24,128]{3,2,1,0:T(8,128)(2,1)}), bf16[32,1,24,128]{3,2,1,0:T(8,128)(2,1)S(1)}, u32[]{:S(2)}, u32[]{:S(2)}) async-start(bf16[32,1,24,128]{3,2,1,0:T(8,128)(2,1)} %bitcast.21), calls=%async_computation.6 | async-start | bytes 393216 | tf_op jit(solution)/shard_map/all_to_all | solution.py:325
  136.8 2.3 %collective-permute-start.6 = (bf16[5,16,128]{2,1,0:T(8,128)(2,1)S(1)}, bf16[5,16,128]{2,1,0:T(8,128)(2,1)S(1)}, u32[]{:S(2)}, u32[]{:S(2)}) collective-permute-start(bf16[5,16,128]{2,1,0:T(8,128)(2,1)S(1)} %get-tuple-element.31), channel_id=1, source_target_pairs={{0,32},{32,64},{64,96},{96,128},{128,160},{160,192},{192,224},{224... | collective-permute-start | bytes 61448 | tf_op jit(solution)/shard_map/ppermute | solution.py:301
  139.1 2.0 %collective-permute-start.7 = (bf16[5,16,128]{2,1,0:T(8,128)(2,1)S(1)}, bf16[5,16,128]{2,1,0:T(8,128)(2,1)S(1)}, u32[]{:S(2)}, u32[]{:S(2)}) collective-permute-start(bf16[5,16,128]{2,1,0:T(8,128)(2,1)S(1)} %get-tuple-element.31), channel_id=1, source_target_pairs={{32,0},{64,32},{96,64},{128,96},{160,128},{192,160},{224,192},{256... | collective-permute-start | bytes 61448 | tf_op jit(solution)/shard_map/ppermute | solution.py:301
  141.2 3.4 %collective-permute-done.7 = bf16[5,16,128]{2,1,0:T(8,128)(2,1)S(1)} collective-permute-done((bf16[5,16,128]{2,1,0:T(8,128)(2,1)S(1)}, bf16[5,16,128]{2,1,0:T(8,128)(2,1)S(1)}, u32[]{:S(2)}, u32[]{:S(2)}) %collective-permute-start.7) | collective-permute-done | bytes 20512 | tf_op jit(solution)/shard_map/ppermute | solution.py:301
  144.5 3.0 %all-to-all-done.6 = bf16[32,1,24,128]{3,2,1,0:T(8,128)(2,1)S(1)} async-done(((bf16[32,1,24,128]{3,2,1,0:T(8,128)(2,1)}), bf16[32,1,24,128]{3,2,1,0:T(8,128)(2,1)S(1)}, u32[]{:S(2)}, u32[]{:S(2)}) %all-to-all-start.6) | async-done | bytes 196640 | tf_op jit(solution)/shard_map/all_to_all | solution.py:325
  148.3 5.2 %all-to-all-start.7 = ((bf16[16,1,24,128]{3,2,1,0:T(8,128)(2,1)}), bf16[16,1,24,128]{3,2,1,0:T(8,128)(2,1)S(1)}, u32[]{:S(2)}, u32[]{:S(2)}) async-start(bf16[16,1,24,128]{3,2,1,0:T(8,128)(2,1)} %broadcast_in_dim.22), calls=%async_computation.7 | async-start | bytes 196608 | tf_op jit(solution)/shard_map/all_to_all | solution.py:330
  153.5 2.6 %collective-permute-start.8 = (bf16[3,5,16,128]{3,2,1,0:T(8,128)(2,1)S(1)}, bf16[3,5,16,128]{3,2,1,0:T(8,128)(2,1)S(1)}, u32[]{:S(2)}, u32[]{:S(2)}) collective-permute-start(bf16[3,5,16,128]{3,2,1,0:T(8,128)(2,1)S(1)} %pad_maximum_fusion.2.mid), channel_id=1, source_target_pairs={{0,4},{4,8},{8,12},{12,16},{16,20},{20,24},{24,28},{1,5},{5,9},{9,... | collective-permute-start | bytes 184328 | tf_op jit(solution)/shard_map/ppermute | solution.py:301
  156.1 1.3 collective-permute-start.9
  157.4 4.0 %collective-permute-done.9.high = bf16[3,5,16,128]{3,2,1,0:T(8,128)(2,1)S(1)} collective-permute-done((bf16[3,5,16,128]{3,2,1,0:T(8,128)(2,1)S(1)}, bf16[3,5,16,128]{3,2,1,0:T(8,128)(2,1)S(1)}, u32[]{:S(2)}, u32[]{:S(2)}) %collective-permute-start.9) | collective-permute-done | bytes 61472 | tf_op jit(solution)/shard_map/ppermute | solution.py:301
  162.7 4.6 %all-to-all-start.8 = ((bf16[32,1,24,128]{3,2,1,0:T(8,128)(2,1)}), bf16[32,1,24,128]{3,2,1,0:T(8,128)(2,1)S(1)}, u32[]{:S(2)}, u32[]{:S(2)}) async-start(bf16[32,1,24,128]{3,2,1,0:T(8,128)(2,1)} %broadcast_in_dim.23), calls=%async_computation.8 | async-start | bytes 393216 | tf_op jit(solution)/shard_map/all_to_all | solution.py:335
  167.8 1.8 %shard_map.88 = bf16[4,48,128]{2,1,0:T(8,128)(2,1)S(1)} custom-call(bf16[3,5,16,128]{3,2,1,0:T(8,128)(2,1)S(1)} %collective-permute-done.8.low, bf16[3,5,16,128]{3,2,1,0:T(8,128)(2,1)S(1)} %pad_maximum_fusion.2.mid, bf16[3,5,16,128]{3,2,1,0:T(8,128)(2,1)S(1)} %collective-permute-done.9.high, bf16[4,4,48,256]{3,2,1,0:T(8,128)(2,1)S(1)} %get-tuple-element.30.hidden_ref, ...), custom_call_target="tpu_custom_call" | custom-call | tf_op jit(solution)/shard_map/pallas_call | solution.py:28
  170.3 6.9 %all-to-all-done.8 = bf16[32,1,24,128]{3,2,1,0:T(8,128)(2,1)S(1)} async-done(((bf16[32,1,24,128]{3,2,1,0:T(8,128)(2,1)}), bf16[32,1,24,128]{3,2,1,0:T(8,128)(2,1)S(1)}, u32[]{:S(2)}, u32[]{:S(2)}) %all-to-all-start.8) | async-done | bytes 196640 | tf_op jit(solution)/shard_map/all_to_all | solution.py:335
  (49 shorter events, 10.8 us)
Async XLA Ops:
  1.4 0.7 copy-start
  2.2 22.4 %copy-start.1 = (bf16[3,3,3,48,48]{4,3,2,1,0:T(8,128)(2,1)S(1)}, bf16[3,3,3,48,48]{4,3,2,1,0:T(8,128)(2,1)}, u32[]{:S(2)}) copy-start(bf16[3,3,3,48,48]{4,3,2,1,0:T(8,128)(2,1)} %param.7) | copy-start | bytes 373252
  2.2 5.4 %collective-permute-start = (bf16[64,128]{1,0:T(8,128)(2,1)S(1)}, bf16[64,128]{1,0:T(8,128)(2,1)S(1)}, u32[]{:S(2)}, u32[]{:S(2)}) collective-permute-start(bf16[64,128]{1,0:T(8,128)(2,1)S(1)} %get-tuple-element.23), channel_id=1, source_target_pairs={{0,1},{1,2},{2,3},{4,5},{5,6},{6,7},{8,9},{9,10},{10,11},{12,13},{... | collective-permute-start | bytes 49160 | tf_op jit(solution)/shard_map/ppermute | solution.py:301
  6.3 4.5 %collective-permute-start.1 = (bf16[64,128]{1,0:T(8,128)(2,1)S(1)}, bf16[64,128]{1,0:T(8,128)(2,1)S(1)}, u32[]{:S(2)}, u32[]{:S(2)}) collective-permute-start(bf16[64,128]{1,0:T(8,128)(2,1)S(1)} %get-tuple-element.24), channel_id=1, source_target_pairs={{1,0},{2,1},{3,2},{5,4},{6,5},{7,6},{9,8},{10,9},{11,10},{13,12},{... | collective-permute-start | bytes 49160 | tf_op jit(solution)/shard_map/ppermute | solution.py:301
  10.8 9.2 %collective-permute-start.3 = (bf16[5,48,128]{2,1,0:T(8,128)(2,1)S(1)}, bf16[5,48,128]{2,1,0:T(8,128)(2,1)S(1)}, u32[]{:S(2)}, u32[]{:S(2)}) collective-permute-start(bf16[5,48,128]{2,1,0:T(8,128)(2,1)S(1)} %get-tuple-element.43), channel_id=1, source_target_pairs={{32,0},{64,32},{96,64},{128,96},{160,128},{192,160},{224,192},{256... | collective-permute-start | bytes 184328 | tf_op jit(solution)/shard_map/ppermute | solution.py:301
  18.1 3.2 %collective-permute-start.2 = (bf16[5,48,128]{2,1,0:T(8,128)(2,1)S(1)}, bf16[5,48,128]{2,1,0:T(8,128)(2,1)S(1)}, u32[]{:S(2)}, u32[]{:S(2)}) collective-permute-start(bf16[5,48,128]{2,1,0:T(8,128)(2,1)S(1)} %get-tuple-element.43), channel_id=1, source_target_pairs={{0,32},{32,64},{64,96},{96,128},{128,160},{160,192},{192,224},{224... | collective-permute-start | bytes 184328 | tf_op jit(solution)/shard_map/ppermute | solution.py:301
  21.3 6.0 %collective-permute-start.4 = (bf16[3,5,48,128]{3,2,1,0:T(8,128)(2,1)S(1)}, bf16[3,5,48,128]{3,2,1,0:T(8,128)(2,1)S(1)}, u32[]{:S(2)}, u32[]{:S(2)}) collective-permute-start(bf16[3,5,48,128]{3,2,1,0:T(8,128)(2,1)S(1)} %pad_maximum_fusion.mid), channel_id=1, source_target_pairs={{0,4},{4,8},{8,12},{12,16},{16,20},{20,24},{24,28},{1,5},{5,9},{9,... | collective-permute-start | bytes 552968 | tf_op jit(solution)/shard_map/ppermute | solution.py:301
  23.3 8.4 %collective-permute-start.5 = (bf16[3,5,48,128]{3,2,1,0:T(8,128)(2,1)S(1)}, bf16[3,5,48,128]{3,2,1,0:T(8,128)(2,1)S(1)}, u32[]{:S(2)}, u32[]{:S(2)}) collective-permute-start(bf16[3,5,48,128]{3,2,1,0:T(8,128)(2,1)S(1)} %pad_maximum_fusion.mid), channel_id=1, source_target_pairs={{4,0},{8,4},{12,8},{16,12},{20,16},{24,20},{28,24},{5,1},{9,5},{13... | collective-permute-start | bytes 552968 | tf_op jit(solution)/shard_map/ppermute | solution.py:301
  24.8 0.9 copy-start.2
  25.9 0.7 copy-start.3
  74.8 13.9 %all-to-all-start.2 = ((f32[32,9,1,128]{3,2,1,0:T(1,128)}), f32[32,9,1,128]{3,2,1,0:T(1,128)S(1)}, u32[]{:S(2)}, u32[]{:S(2)}) async-start(f32[32,9,1,128]{3,2,1,0:T(1,128)} %broadcast_in_dim.19), calls=%async_computation.2 | async-start | bytes 294912 | tf_op jit(solution)/shard_map/all_to_all | solution.py:335
  115.6 12.7 %all-to-all-start.5 = ((bf16[16,1,16,128]{3,2,1,0:T(8,128)(2,1)}), bf16[16,1,16,128]{3,2,1,0:T(8,128)(2,1)S(1)}, u32[]{:S(2)}, u32[]{:S(2)}) async-start(bf16[16,1,16,128]{3,2,1,0:T(8,128)(2,1)} %broadcast_in_dim.21), calls=%async_computation.5 | async-start | bytes 131072 | tf_op jit(solution)/shard_map/all_to_all | solution.py:335
  132.9 14.6 %all-to-all-start.6 = ((bf16[32,1,24,128]{3,2,1,0:T(8,128)(2,1)}), bf16[32,1,24,128]{3,2,1,0:T(8,128)(2,1)S(1)}, u32[]{:S(2)}, u32[]{:S(2)}) async-start(bf16[32,1,24,128]{3,2,1,0:T(8,128)(2,1)} %bitcast.21), calls=%async_computation.6 | async-start | bytes 393216 | tf_op jit(solution)/shard_map/all_to_all | solution.py:325
  136.8 4.3 %collective-permute-start.6 = (bf16[5,16,128]{2,1,0:T(8,128)(2,1)S(1)}, bf16[5,16,128]{2,1,0:T(8,128)(2,1)S(1)}, u32[]{:S(2)}, u32[]{:S(2)}) collective-permute-start(bf16[5,16,128]{2,1,0:T(8,128)(2,1)S(1)} %get-tuple-element.31), channel_id=1, source_target_pairs={{0,32},{32,64},{64,96},{96,128},{128,160},{160,192},{192,224},{224... | collective-permute-start | bytes 61448 | tf_op jit(solution)/shard_map/ppermute | solution.py:301
  139.1 5.4 %collective-permute-start.7 = (bf16[5,16,128]{2,1,0:T(8,128)(2,1)S(1)}, bf16[5,16,128]{2,1,0:T(8,128)(2,1)S(1)}, u32[]{:S(2)}, u32[]{:S(2)}) collective-permute-start(bf16[5,16,128]{2,1,0:T(8,128)(2,1)S(1)} %get-tuple-element.31), channel_id=1, source_target_pairs={{32,0},{64,32},{96,64},{128,96},{160,128},{192,160},{224,192},{256... | collective-permute-start | bytes 61448 | tf_op jit(solution)/shard_map/ppermute | solution.py:301
  148.3 13.7 %all-to-all-start.7 = ((bf16[16,1,24,128]{3,2,1,0:T(8,128)(2,1)}), bf16[16,1,24,128]{3,2,1,0:T(8,128)(2,1)S(1)}, u32[]{:S(2)}, u32[]{:S(2)}) async-start(bf16[16,1,24,128]{3,2,1,0:T(8,128)(2,1)} %broadcast_in_dim.22), calls=%async_computation.7 | async-start | bytes 196608 | tf_op jit(solution)/shard_map/all_to_all | solution.py:330
  153.5 3.9 %collective-permute-start.8 = (bf16[3,5,16,128]{3,2,1,0:T(8,128)(2,1)S(1)}, bf16[3,5,16,128]{3,2,1,0:T(8,128)(2,1)S(1)}, u32[]{:S(2)}, u32[]{:S(2)}) collective-permute-start(bf16[3,5,16,128]{3,2,1,0:T(8,128)(2,1)S(1)} %pad_maximum_fusion.2.mid), channel_id=1, source_target_pairs={{0,4},{4,8},{8,12},{12,16},{16,20},{20,24},{24,28},{1,5},{5,9},{9,... | collective-permute-start | bytes 184328 | tf_op jit(solution)/shard_map/ppermute | solution.py:301
  156.1 5.3 %collective-permute-start.9 = (bf16[3,5,16,128]{3,2,1,0:T(8,128)(2,1)S(1)}, bf16[3,5,16,128]{3,2,1,0:T(8,128)(2,1)S(1)}, u32[]{:S(2)}, u32[]{:S(2)}) collective-permute-start(bf16[3,5,16,128]{3,2,1,0:T(8,128)(2,1)S(1)} %pad_maximum_fusion.2.mid), channel_id=1, source_target_pairs={{4,0},{8,4},{12,8},{16,12},{20,16},{24,20},{28,24},{5,1},{9,5},{13... | collective-permute-start | bytes 184328 | tf_op jit(solution)/shard_map/ppermute | solution.py:301
  162.7 14.5 %all-to-all-start.8 = ((bf16[32,1,24,128]{3,2,1,0:T(8,128)(2,1)}), bf16[32,1,24,128]{3,2,1,0:T(8,128)(2,1)S(1)}, u32[]{:S(2)}, u32[]{:S(2)}) async-start(bf16[32,1,24,128]{3,2,1,0:T(8,128)(2,1)} %broadcast_in_dim.23), calls=%async_computation.8 | async-start | bytes 393216 | tf_op jit(solution)/shard_map/all_to_all | solution.py:335

commit v4 on v3

--- a/solution.py
+++ b/solution.py
@@ -143,19 +143,31 @@
     )
 
 
-def edge_kernel(rows_ref, ids_ref, first_ref, last_ref):
-    row = lax.broadcasted_iota(jnp.int32, (16, ROW_COLS), 0)
-    ids = ids_ref[...]
-    marks = jnp.where(row == 0, ids >> 8, jnp.where(row == 1, ids & 255, jnp.where(row == 2, 1, 0))).astype(f32)
-    rows = [
-        jnp.concatenate([rows_ref[r].astype(f32), marks[:, LANES * r : LANES * (r + 1)]], axis=0) for r in range(4)
+def edge_kernel(features_hbm, ids_hbm, rows_ref, first_ref, last_ref, features_ref, ids_ref, done):
+    fetches = [
+        pltpu.make_async_copy(features_hbm, features_ref, done.at[0]),
+        pltpu.make_async_copy(ids_hbm, ids_ref, done.at[1]),
     ]
+    for fetch in fetches:
+        fetch.start()
+    for fetch in fetches:
+        fetch.wait()
+    features = features_ref[...].astype(f32)
+    row = lax.broadcasted_iota(jnp.int32, (16, LANES), 0)
+    rows = []
+    for r in range(4):
+        mine = features[:, r // 2, r % 2, :]
+        rows_ref[r] = mine.astype(bf16)
+        ids = ids_ref[r // 2, r % 2 : r % 2 + 1]
+        marks = jnp.where(row == 0, ids >> 8, jnp.where(row == 1, ids & 255, jnp.where(row == 2, 1, 0)))
+        rows.append(jnp.concatenate([mine, marks.astype(f32)], axis=0))
     first, last = edges(rows)
     first_ref[...] = first.astype(bf16)
     last_ref[...] = last.astype(bf16)
 
 
-def embed_kernel(place, low, mid, high, taps_one, taps_two, bias, ids_ref, wide_ref, hidden_ref, embed_ref, lines_ref):
+def embed_kernel(place, low, mid, high, taps_one, taps_two, bias, ids_ref, back_one, back_two, marks, *outs):
+    wide_ref, hidden_ref, embed_ref, lines_ref = outs
     widen((low, mid, high), wide_ref)
     gz, gy, gx = place[0], place[1], place[2]
     at = lane((CHANNELS, WIDE))
@@ -253,21 +265,21 @@
 
     def layer(z, carry):
         one, bias = carry
+        moved = jnp.concatenate([shifted(grad_ref[z, y]) for y in range(4)], axis=1)
+        seen = jnp.concatenate([window(wide_ref, z, y) for y in range(4)], axis=1)
+        one = one + lax.dot_general(moved, seen, over_cells, preferred_element_type=f32)
         for y in range(4):
-            moved = shifted(grad_ref[z, y])
-            one = one + lax.dot_general(moved, window(wide_ref, z, y), over_cells, preferred_element_type=f32)
-            own = moved[CHANNELS : 2 * CHANNELS]
-            bias = bias + lax.dot_general(jnp.ones((16, WIDE), bf16), own, over_cells, preferred_element_type=f32)
+            bias = bias + grad_ref[z, y].astype(f32)
         return one, bias
 
-    zeros = jnp.zeros((3 * CHANNELS, 9 * CHANNELS), f32), jnp.zeros((16, CHANNELS), f32)
+    zeros = jnp.zeros((3 * CHANNELS, 9 * CHANNELS), f32), jnp.zeros((CHANNELS, WIDE), f32)
     one, bias = lax.fori_loop(0, 4, layer, zeros)
-    two = jnp.zeros((3 * EMBED, 9 * CHANNELS), f32)
-    for r in range(4):
-        z, y = r // 2, r % 2
-        two = two + lax.dot_general(
-            shifted(up_ref[z + 2, y + 2]), window(hidden_ref, z, y), over_cells, preferred_element_type=f32
-        )
+    ones = jnp.ones((16, 2 * WIDE), bf16)
+    bias = jnp.concatenate(split(bias), axis=1)
+    bias = lax.dot_general(ones, bias, over_cells, preferred_element_type=f32)
+    moved = jnp.concatenate([shifted(up_ref[2 + r // 2, 2 + r % 2]) for r in range(4)], axis=1)
+    seen = jnp.concatenate([window(hidden_ref, r // 2, r % 2) for r in range(4)], axis=1)
+    two = lax.dot_general(seen, moved, over_cells, preferred_element_type=f32).T
     one = jnp.concatenate([one, jnp.zeros((3 * CHANNELS, 80), f32)], axis=1)
     bias = jnp.concatenate([bias] * 3, axis=0)
     two = jnp.concatenate([two, bias, jnp.zeros((3 * EMBED, 32), f32)], axis=1)
@@ -279,7 +291,7 @@
     backward_layers(hidden_ref, up_ref, taps_two, grad_ref)
     for r in range(4):
         folded = fold(jnp.dot(taps_one[...], window(grad_ref, r // 2, r % 2), preferred_element_type=f32))
-        features_ref[r] = folded[:, :LANES].astype(bf16)
+        features_ref[:, r // 2, r % 2, :] = folded[:, :LANES].astype(bf16)
 
 
 def result_kernel(tiles_ref, one_ref, bias_ref, two_ref):
@@ -301,11 +313,10 @@
     return lax.ppermute(high, axis, forward), lax.ppermute(low, axis, backward)
 
 
-def surround(block, between=None):
-    between = between or [lambda held: held] * 2
-    low, high = between[0](passed(block, block, "gz"))
+def surround(block, beside=lambda held: held, then=lambda held: held):
+    low, high = beside(passed(block, block, "gz"))
     block = jnp.stack([low, block, high])
-    low, high = between[1](passed(block, block, "gy"))
+    low, high = then(passed(block, block, "gy"))
     return low, block, high
 
 
@@ -358,12 +369,23 @@
     back_one = jnp.transpose(kernel_one[::-1, ::-1, ::-1], (2, 4, 0, 1, 3)).reshape(3 * CHANNELS, 9 * CHANNELS)
     back_two = jnp.transpose(kernel_two[::-1, ::-1, ::-1], (2, 4, 0, 1, 3)).reshape(3 * CHANNELS, 9 * EMBED)
     ids = segment_ids.reshape(1, ROW_COLS)
-    rows = jnp.transpose(features, (1, 2, 0, 3)).reshape(4, CHANNELS, LANES)
-
-    first, last = kernel_call(edge_kernel, [((CHANNELS + 16, LANES), bf16)] * 2)(rows, ids)
+
+    rows, first, last = pl.pallas_call(
+        edge_kernel,
+        out_shape=[jax.ShapeDtypeStruct((4, CHANNELS, LANES), bf16)]
+        + [jax.ShapeDtypeStruct((CHANNELS + 16, LANES), bf16)] * 2,
+        in_specs=[pl.BlockSpec(memory_space=pl.ANY)] * 2,
+        out_specs=[pl.BlockSpec(memory_space=pltpu.VMEM)] * 3,
+        scratch_shapes=[
+            pltpu.VMEM(features.shape, bf16),
+            pltpu.VMEM(segment_ids.shape, jnp.int32),
+            pltpu.SemaphoreType.DMA((2,)),
+        ],
+    )(features, segment_ids)
     left, right = passed(first, last, "gx")
     pack = left + right
     low, mid, high = surround(jnp.concatenate([rows, pack[None, :CHANNELS]], axis=0))
+    marks = pack[CHANNELS:]
     wide, hidden, embedding, lines = kernel_call(
         embed_kernel,
         [
@@ -373,10 +395,10 @@
             ((288, 1, LANES), f32),
         ],
         scalars=1,
-    )(place, low, mid, high, taps_one, taps_two, bias_one[:, None], ids)
+    )(place, low, mid, high, taps_one, taps_two, bias_one[:, None], ids, back_one, back_two, marks)
     lines = total(lines, ("gy", "gx"), "gz")
     direct, tiles = kernel_call(direct_kernel, [((24, ROW_COLS + LANES), f32), ((16, 16, LANES), bf16)], scalars=1)(
-        place, lines, embedding, ids, pack[CHANNELS:]
+        place, lines, embedding, ids, marks
     )
     tiles = total(tiles, "gz", ("gy", "gx"))
     back = [((6, 6, EMBED, WIDE), bf16), ((4, 4, CHANNELS, WIDE), bf16)]
@@ -384,12 +406,11 @@
         kernels_kernel, [((5, EMBED, LANES), bf16), ((32, 24, LANES), bf16)], scratch=back
     )(direct, tiles, wide, hidden, back_two)
     moves, held = steps(tiles, ("gy", "gx"), "gz")
-    low, mid, high = surround(block, moves)
-    (rows,) = kernel_call(features_kernel, [((4, CHANNELS, LANES), bf16)], scratch=back)(
+    low, mid, high = surround(block, *moves[:2])
+    (grad_features,) = kernel_call(features_kernel, [((CHANNELS, 2, 2, LANES), bf16)], scratch=back)(
         low, mid, high, hidden, back_two, back_one
     )
     moves[2](())
-    grad_features = jnp.transpose(rows.reshape(2, 2, CHANNELS, LANES), (2, 0, 1, 3))
     grad_one, grad_bias, grad_two = kernel_call(
         result_kernel, [((27, CHANNELS, CHANNELS), f32), ((1, CHANNELS), f32), ((27, EMBED, CHANNELS), f32)]
     )(held[0])

time: 180 us -> 179 us (level)
  blocking collectives: 64 us -> 90.2 us
  waiting for transfers between devices: 44.9 us -> 21.1 us
  local copies, waits for them, and re-layouts: 7.82 us -> 4.43 us
  starting transfers between devices: 48.3 us -> 46.1 us
  Pallas kernels: 12 us -> 14.1 us
    all_to_all x0 -> x2, blocking collectives: none -> 25 us  [gathered(): lax.all_to_all(held[0], outer, 0, 0)]
    all_to_all x3 -> x1, waiting for transfers between devices: 24.5 us -> 7.45 us  [gathered(): lax.all_to_all(held[0], outer, 0, 0)]
    ppermute x5, waiting for transfers between devices: 14.8 us -> 3.88 us  [passed(): lax.ppermute(low, axis, backward)]
    all_to_all x3 -> x1, starting transfers between devices: 13.3 us -> 6.18 us  [gathered(): lax.all_to_all(held[0], outer, 0, 0)]
    ppermute x5, starting transfers between devices: 12.8 us -> 17.5 us  [passed(): lax.ppermute(high, axis, forward)]
    pallas_call x6 -> x5, Pallas kernels: 12 us -> 12.4 us  [call(): pl.pallas_call(body, out_shape=[jax.ShapeDtypeStruct(shape, dtype) for sh...]
  transfers between devices with their start and end apart: 15 -> 13, of which waited for: 11 -> 9; matrix products, arithmetic and copies ran while one was open for 1% -> 1% of each run, Pallas kernels for 1% -> 1%
where the time goes in v4:
time: 179 us; the launch traced here: 177 us
  blocking collectives  90.2 us (50%)
  starting transfers between devices  46.1 us (26%)
  waiting for transfers between devices  21.1 us (12%)
  Pallas kernels  14.1 us (8%)
  local copies, waits for them, and re-layouts  4.43 us (2%)
    all_to_all x2, blocking collectives, exchanged(): lax.all_to_all(held[0], inner, 0, 0)  33.7 us
    all_to_all x2, blocking collectives, scattered(): lax.all_to_all(held[0], outer, 0, 0)  31.5 us
    all_to_all x2, blocking collectives, gathered(): lax.all_to_all(held[0], outer, 0, 0)  25 us
    ppermute x5, starting transfers between devices, passed(): lax.ppermute(high, axis, forward)  17.5 us
    ppermute x5, starting transfers between devices, passed(): lax.ppermute(low, axis, backward)  13.4 us
    pallas_call x5, Pallas kernels, call(): pl.pallas_call(body, out_shape=[jax.ShapeDtypeStruct(shape, dtype) for sh...  12.4 us
    all_to_all x1, waiting for transfers between devices, gathered(): lax.all_to_all(held[0], outer, 0, 0)  7.45 us
    all_to_all x1, starting transfers between devices, gathered(): lax.all_to_all(held[0], outer, 0, 0)  6.18 us
  transfers between devices with their start and end apart: 13, of which 9 were waited for; matrix products, arithmetic and copies ran while one was open for 1% of the time, Pallas kernels for 1%

profile of v4, /device:TPU:1, one launch (start us, length us, event | category | flops | bytes accessed | tf_op | source)
XLA Modules:
  0.0 177.2 jit_solution(4085596801084482107)
XLA Ops:
  0.6 1.7 shard_map.84
  2.3 4.1 %collective-permute-start = (bf16[64,128]{1,0:T(8,128)(2,1)}, bf16[64,128]{1,0:T(8,128)(2,1)S(1)}, u32[]{:S(2)}, u32[]{:S(2)}) collective-permute-start(bf16[64,128]{1,0:T(8,128)(2,1)} %get-tuple-element.25), channel_id=1, source_target_pairs={{0,1},{1,2},{2,3},{4,5},{5,6},{6,7},{8,9},{9,10},{10,11},{12,13},{... | collective-permute-start | bytes 49160 | tf_op jit(solution)/shard_map/ppermute | solution.py:313
  6.4 1.3 collective-permute-start.1
  7.7 3.4 %collective-permute-done.1 = bf16[64,128]{1,0:T(8,128)(2,1)S(1)} collective-permute-done((bf16[64,128]{1,0:T(8,128)(2,1)}, bf16[64,128]{1,0:T(8,128)(2,1)S(1)}, u32[]{:S(2)}, u32[]{:S(2)}) %collective-permute-start.1) | collective-permute-done | bytes 16416 | tf_op jit(solution)/shard_map/ppermute | solution.py:313
  11.1 7.3 %collective-permute-start.3 = (bf16[5,48,128]{2,1,0:T(8,128)(2,1)S(1)}, bf16[5,48,128]{2,1,0:T(8,128)(2,1)S(1)}, u32[]{:S(2)}, u32[]{:S(2)}) collective-permute-start(bf16[5,48,128]{2,1,0:T(8,128)(2,1)S(1)} %get-tuple-element.45), channel_id=1, source_target_pairs={{32,0},{64,32},{96,64},{128,96},{160,128},{192,160},{224,192},{256... | collective-permute-start | bytes 184328 | tf_op jit(solution)/shard_map/ppermute | solution.py:313
  18.4 1.9 %collective-permute-start.2 = (bf16[5,48,128]{2,1,0:T(8,128)(2,1)S(1)}, bf16[5,48,128]{2,1,0:T(8,128)(2,1)S(1)}, u32[]{:S(2)}, u32[]{:S(2)}) collective-permute-start(bf16[5,48,128]{2,1,0:T(8,128)(2,1)S(1)} %get-tuple-element.45), channel_id=1, source_target_pairs={{0,32},{32,64},{64,96},{96,128},{128,160},{160,192},{192,224},{224... | collective-permute-start | bytes 184328 | tf_op jit(solution)/shard_map/ppermute | solution.py:313
  21.7 1.4 collective-permute-start.5
  23.1 4.0 %collective-permute-start.4 = (bf16[3,5,48,128]{3,2,1,0:T(8,128)(2,1)S(1)}, bf16[3,5,48,128]{3,2,1,0:T(8,128)(2,1)S(1)}, u32[]{:S(2)}, u32[]{:S(2)}) collective-permute-start(bf16[3,5,48,128]{3,2,1,0:T(8,128)(2,1)S(1)} %pad_maximum_fusion.mid), channel_id=1, source_target_pairs={{0,4},{4,8},{8,12},{12,16},{16,20},{20,24},{24,28},{1,5},{5,9},{9,... | collective-permute-start | bytes 552968 | tf_op jit(solution)/shard_map/ppermute | solution.py:313
  29.9 0.9 collective-permute-done.4.low
  30.8 3.0 %shard_map.85 = (bf16[6,6,48,256]{3,2,1,0:T(8,128)(2,1)S(1)}, bf16[4,4,48,256]{3,2,1,0:T(8,128)(2,1)S(1)}, f32[16,640]{1,0:T(8,128)S(1)}, f32[288,1,128]{2,1,0:T(1,128)S(1)}) custom-call(s32[7]{0:T(128)S(1)} %stack.43.place, bf16[3,5,48,128]{3,2,1,0:T(8,128)(2,1)S(1)} %collective-permute-done.4.low, bf16[3,5,48,128]{3,2,1,0:T(8,128)(2,1)S(1)} %pad_maximum_fusion.mid, ...), custom_call_target="tpu_custom_call" | custom-call | tf_op jit(solution)/shard_map/pallas_call | solution.py:28
  33.7 19.8 %all_to_all.45 = f32[32,9,1,128]{3,2,1,0:T(1,128)S(1)} all-to-all(f32[32,9,1,128]{3,2,1,0:T(1,128)S(1)} %bitcast.39), channel_id=1, replica_groups=mesh['gz'=16,'gy'=8,'gx'=4] {'gy','gx'}, dimensions={0} | all-to-all | bytes 294912 | tf_op jit(solution)/shard_map/all_to_all | solution.py:336
  53.6 20.7 %all_to_all.46 = f32[16,9,1,128]{3,2,1,0:T(1,128)S(1)} all-to-all(f32[16,9,1,128]{3,2,1,0:T(1,128)S(1)} %broadcast_in_dim.18), channel_id=1, replica_groups=mesh['gz'=16,'gy'=8,'gx'=4] {'gz'}, dimensions={0} | all-to-all | bytes 147456 | tf_op jit(solution)/shard_map/all_to_all | solution.py:341
  74.5 13.2 %all_to_all.47 = f32[32,9,1,128]{3,2,1,0:T(1,128)S(1)} all-to-all(f32[32,9,1,128]{3,2,1,0:T(1,128)S(1)} %broadcast_in_dim.19), channel_id=1, replica_groups=mesh['gz'=16,'gy'=8,'gx'=4] {'gy','gx'}, dimensions={0} | all-to-all | bytes 294912 | tf_op jit(solution)/shard_map/all_to_all | solution.py:346
  87.7 1.3 shard_map.86
  89.0 11.8 %all_to_all.48 = bf16[16,1,16,128]{3,2,1,0:T(8,128)(2,1)S(1)} all-to-all(bf16[16,1,16,128]{3,2,1,0:T(8,128)(2,1)S(1)} %bitcast.40), channel_id=1, replica_groups=mesh['gz'=16,'gy'=8,'gx'=4] {'gz'}, dimensions={0} | all-to-all | bytes 131072 | tf_op jit(solution)/shard_map/all_to_all | solution.py:336
  100.8 13.0 %all_to_all.49 = bf16[32,1,16,128]{3,2,1,0:T(8,128)(2,1)S(1)} all-to-all(bf16[32,1,16,128]{3,2,1,0:T(8,128)(2,1)S(1)} %broadcast_in_dim.20), channel_id=1, replica_groups=mesh['gz'=16,'gy'=8,'gx'=4] {'gy','gx'}, dimensions={0} | all-to-all | bytes 262144 | tf_op jit(solution)/shard_map/all_to_all | solution.py:341
  113.8 11.8 %all_to_all.50 = bf16[16,1,16,128]{3,2,1,0:T(8,128)(2,1)S(1)} all-to-all(bf16[16,1,16,128]{3,2,1,0:T(8,128)(2,1)S(1)} %broadcast_in_dim.21), channel_id=1, replica_groups=mesh['gz'=16,'gy'=8,'gx'=4] {'gz'}, dimensions={0} | all-to-all | bytes 131072 | tf_op jit(solution)/shard_map/all_to_all | solution.py:346
  125.6 4.6 %shard_map.87 = (bf16[5,16,128]{2,1,0:T(8,128)(2,1)S(1)}, bf16[32,24,128]{2,1,0:T(8,128)(2,1)}) custom-call(f32[24,640]{1,0:T(8,128)S(1)} %get-tuple-element.29.direct_ref, bf16[16,16,128]{2,1,0:T(8,128)(2,1)S(1)} %bitcast.38, bf16[6,6,48,256]{3,2,1,0:T(8,128)(2,1)S(1)} %get-tuple-element.31.wide_ref, ...), custom_call_target="tpu_custom_call" | custom-call | tf_op jit(solution)/shard_map/pallas_call | solution.py:28
  130.2 3.9 %all-to-all-start.6 = ((bf16[32,1,24,128]{3,2,1,0:T(8,128)(2,1)}), bf16[32,1,24,128]{3,2,1,0:T(8,128)(2,1)S(1)}, u32[]{:S(2)}, u32[]{:S(2)}) async-start(bf16[32,1,24,128]{3,2,1,0:T(8,128)(2,1)} %bitcast.20), calls=%async_computation.6 | async-start | bytes 393216 | tf_op jit(solution)/shard_map/all_to_all | solution.py:336
  134.1 2.1 %collective-permute-start.7 = (bf16[5,16,128]{2,1,0:T(8,128)(2,1)S(1)}, bf16[5,16,128]{2,1,0:T(8,128)(2,1)S(1)}, u32[]{:S(2)}, u32[]{:S(2)}) collective-permute-start(bf16[5,16,128]{2,1,0:T(8,128)(2,1)S(1)} %get-tuple-element.33), channel_id=1, source_target_pairs={{32,0},{64,32},{96,64},{128,96},{160,128},{192,160},{224,192},{256... | collective-permute-start | bytes 61448 | tf_op jit(solution)/shard_map/ppermute | solution.py:313
  136.1 3.5 %collective-permute-start.6 = (bf16[5,16,128]{2,1,0:T(8,128)(2,1)S(1)}, bf16[5,16,128]{2,1,0:T(8,128)(2,1)S(1)}, u32[]{:S(2)}, u32[]{:S(2)}) collective-permute-start(bf16[5,16,128]{2,1,0:T(8,128)(2,1)S(1)} %get-tuple-element.33), channel_id=1, source_target_pairs={{0,32},{32,64},{64,96},{96,128},{128,160},{160,192},{192,224},{224... | collective-permute-start | bytes 61448 | tf_op jit(solution)/shard_map/ppermute | solution.py:313
  139.6 0.9 collective-permute-done.6
  140.5 4.3 %all-to-all-done.6 = bf16[32,1,24,128]{3,2,1,0:T(8,128)(2,1)S(1)} async-done(((bf16[32,1,24,128]{3,2,1,0:T(8,128)(2,1)}), bf16[32,1,24,128]{3,2,1,0:T(8,128)(2,1)S(1)}, u32[]{:S(2)}, u32[]{:S(2)}) %all-to-all-start.6) | async-done | bytes 196640 | tf_op jit(solution)/shard_map/all_to_all | solution.py:336
  145.5 5.2 %all-to-all-start.7 = ((bf16[16,1,24,128]{3,2,1,0:T(8,128)(2,1)}), bf16[16,1,24,128]{3,2,1,0:T(8,128)(2,1)S(1)}, u32[]{:S(2)}, u32[]{:S(2)}) async-start(bf16[16,1,24,128]{3,2,1,0:T(8,128)(2,1)} %broadcast_in_dim.22), calls=%async_computation.7 | async-start | bytes 196608 | tf_op jit(solution)/shard_map/all_to_all | solution.py:341
  150.7 1.3 collective-permute-start.9
  152.0 4.0 %collective-permute-start.8 = (bf16[3,5,16,128]{3,2,1,0:T(8,128)(2,1)S(1)}, bf16[3,5,16,128]{3,2,1,0:T(8,128)(2,1)S(1)}, u32[]{:S(2)}, u32[]{:S(2)}) collective-permute-start(bf16[3,5,16,128]{3,2,1,0:T(8,128)(2,1)S(1)} %pad_maximum_fusion.2.mid), channel_id=1, source_target_pairs={{0,4},{4,8},{8,12},{12,16},{16,20},{20,24},{24,28},{1,5},{5,9},{9,... | collective-permute-start | bytes 184328 | tf_op jit(solution)/shard_map/ppermute | solution.py:313
  156.0 1.3 collective-permute-done.8.low
  157.3 1.9 %all-to-all-done.7 = bf16[16,1,24,128]{3,2,1,0:T(8,128)(2,1)S(1)} async-done(((bf16[16,1,24,128]{3,2,1,0:T(8,128)(2,1)}), bf16[16,1,24,128]{3,2,1,0:T(8,128)(2,1)S(1)}, u32[]{:S(2)}, u32[]{:S(2)}) %all-to-all-start.7) | async-done | bytes 98336 | tf_op jit(solution)/shard_map/all_to_all | solution.py:341
  159.9 6.2 %all-to-all-start.8 = ((bf16[32,1,24,128]{3,2,1,0:T(8,128)(2,1)}), bf16[32,1,24,128]{3,2,1,0:T(8,128)(2,1)S(1)}, u32[]{:S(2)}, u32[]{:S(2)}) async-start(bf16[32,1,24,128]{3,2,1,0:T(8,128)(2,1)} %broadcast_in_dim.23), calls=%async_computation.8 | async-start | bytes 393216 | tf_op jit(solution)/shard_map/all_to_all | solution.py:346
  166.1 2.5 %shard_map.88 = bf16[48,2,2,128]{3,2,1,0:T(2,128)(2,1)} custom-call(bf16[3,5,16,128]{3,2,1,0:T(8,128)(2,1)S(1)} %collective-permute-done.8.low, bf16[3,5,16,128]{3,2,1,0:T(8,128)(2,1)S(1)} %pad_maximum_fusion.2.mid, bf16[3,5,16,128]{3,2,1,0:T(8,128)(2,1)S(1)} %collective-permute-done.9.high, bf16[4,4,48,256]{3,2,1,0:T(8,128)(2,1)S(1)} %get-tuple-element.32.hidden_ref, ...), custom_call_target="tpu_custom_call" | custom-call | tf_op jit(solution)/shard_map/pallas_call | solution.py:28
  168.6 7.5 %all-to-all-done.8 = bf16[32,1,24,128]{3,2,1,0:T(8,128)(2,1)S(1)} async-done(((bf16[32,1,24,128]{3,2,1,0:T(8,128)(2,1)}), bf16[32,1,24,128]{3,2,1,0:T(8,128)(2,1)S(1)}, u32[]{:S(2)}, u32[]{:S(2)}) %all-to-all-start.8) | async-done | bytes 196640 | tf_op jit(solution)/shard_map/all_to_all | solution.py:346
  176.0 1.2 shard_map.89
  (47 shorter events, 5.8 us)
Async XLA Ops:
  2.3 8.8 %copy-start.3 = (bf16[4,48,128]{2,1,0:T(8,128)(2,1)S(1)}, bf16[4,48,128]{2,1,0:T(8,128)(2,1)}, u32[]{:S(2)}) copy-start(bf16[4,48,128]{2,1,0:T(8,128)(2,1)} %get-tuple-element.24) | copy-start | bytes 147460
  2.3 5.4 %collective-permute-start = (bf16[64,128]{1,0:T(8,128)(2,1)}, bf16[64,128]{1,0:T(8,128)(2,1)S(1)}, u32[]{:S(2)}, u32[]{:S(2)}) collective-permute-start(bf16[64,128]{1,0:T(8,128)(2,1)} %get-tuple-element.25), channel_id=1, source_target_pairs={{0,1},{1,2},{2,3},{4,5},{5,6},{6,7},{8,9},{9,10},{10,11},{12,13},{... | collective-permute-start | bytes 49160 | tf_op jit(solution)/shard_map/ppermute | solution.py:313
  6.4 4.7 %collective-permute-start.1 = (bf16[64,128]{1,0:T(8,128)(2,1)}, bf16[64,128]{1,0:T(8,128)(2,1)S(1)}, u32[]{:S(2)}, u32[]{:S(2)}) collective-permute-start(bf16[64,128]{1,0:T(8,128)(2,1)} %get-tuple-element.26), channel_id=1, source_target_pairs={{1,0},{2,1},{3,2},{5,4},{6,5},{7,6},{9,8},{10,9},{11,10},{13,12},{... | collective-permute-start | bytes 49160 | tf_op jit(solution)/shard_map/ppermute | solution.py:313
  11.1 10.0 %collective-permute-start.3 = (bf16[5,48,128]{2,1,0:T(8,128)(2,1)S(1)}, bf16[5,48,128]{2,1,0:T(8,128)(2,1)S(1)}, u32[]{:S(2)}, u32[]{:S(2)}) collective-permute-start(bf16[5,48,128]{2,1,0:T(8,128)(2,1)S(1)} %get-tuple-element.45), channel_id=1, source_target_pairs={{32,0},{64,32},{96,64},{128,96},{160,128},{192,160},{224,192},{256... | collective-permute-start | bytes 184328 | tf_op jit(solution)/shard_map/ppermute | solution.py:313
  18.4 3.2 %collective-permute-start.2 = (bf16[5,48,128]{2,1,0:T(8,128)(2,1)S(1)}, bf16[5,48,128]{2,1,0:T(8,128)(2,1)S(1)}, u32[]{:S(2)}, u32[]{:S(2)}) collective-permute-start(bf16[5,48,128]{2,1,0:T(8,128)(2,1)S(1)} %get-tuple-element.45), channel_id=1, source_target_pairs={{0,32},{32,64},{64,96},{96,128},{128,160},{160,192},{192,224},{224... | collective-permute-start | bytes 184328 | tf_op jit(solution)/shard_map/ppermute | solution.py:313
  20.4 0.7 copy-start.4
  21.6 5.5 %copy-start.2 = (bf16[3,3,3,16,48]{4,3,2,1,0:T(8,128)(2,1)S(1)}, bf16[3,3,3,16,48]{4,3,2,1,0:T(8,128)(2,1)}, u32[]{:S(2)}) copy-start(bf16[3,3,3,16,48]{4,3,2,1,0:T(8,128)(2,1)} %param.9) | copy-start | bytes 124420
  21.7 8.2 %collective-permute-start.5 = (bf16[3,5,48,128]{3,2,1,0:T(8,128)(2,1)S(1)}, bf16[3,5,48,128]{3,2,1,0:T(8,128)(2,1)S(1)}, u32[]{:S(2)}, u32[]{:S(2)}) collective-permute-start(bf16[3,5,48,128]{3,2,1,0:T(8,128)(2,1)S(1)} %pad_maximum_fusion.mid), channel_id=1, source_target_pairs={{4,0},{8,4},{12,8},{16,12},{20,16},{24,20},{28,24},{5,1},{9,5},{13... | collective-permute-start | bytes 552968 | tf_op jit(solution)/shard_map/ppermute | solution.py:313
  23.1 7.7 %collective-permute-start.4 = (bf16[3,5,48,128]{3,2,1,0:T(8,128)(2,1)S(1)}, bf16[3,5,48,128]{3,2,1,0:T(8,128)(2,1)S(1)}, u32[]{:S(2)}, u32[]{:S(2)}) collective-permute-start(bf16[3,5,48,128]{3,2,1,0:T(8,128)(2,1)S(1)} %pad_maximum_fusion.mid), channel_id=1, source_target_pairs={{0,4},{4,8},{8,12},{12,16},{16,20},{20,24},{24,28},{1,5},{5,9},{9,... | collective-permute-start | bytes 552968 | tf_op jit(solution)/shard_map/ppermute | solution.py:313
  27.3 1.0 copy-start.1
  29.4 1.4 copy-start
  130.2 14.6 %all-to-all-start.6 = ((bf16[32,1,24,128]{3,2,1,0:T(8,128)(2,1)}), bf16[32,1,24,128]{3,2,1,0:T(8,128)(2,1)S(1)}, u32[]{:S(2)}, u32[]{:S(2)}) async-start(bf16[32,1,24,128]{3,2,1,0:T(8,128)(2,1)} %bitcast.20), calls=%async_computation.6 | async-start | bytes 393216 | tf_op jit(solution)/shard_map/all_to_all | solution.py:336
  134.1 5.6 %collective-permute-start.7 = (bf16[5,16,128]{2,1,0:T(8,128)(2,1)S(1)}, bf16[5,16,128]{2,1,0:T(8,128)(2,1)S(1)}, u32[]{:S(2)}, u32[]{:S(2)}) collective-permute-start(bf16[5,16,128]{2,1,0:T(8,128)(2,1)S(1)} %get-tuple-element.33), channel_id=1, source_target_pairs={{32,0},{64,32},{96,64},{128,96},{160,128},{192,160},{224,192},{256... | collective-permute-start | bytes 61448 | tf_op jit(solution)/shard_map/ppermute | solution.py:313
  136.1 4.4 %collective-permute-start.6 = (bf16[5,16,128]{2,1,0:T(8,128)(2,1)S(1)}, bf16[5,16,128]{2,1,0:T(8,128)(2,1)S(1)}, u32[]{:S(2)}, u32[]{:S(2)}) collective-permute-start(bf16[5,16,128]{2,1,0:T(8,128)(2,1)S(1)} %get-tuple-element.33), channel_id=1, source_target_pairs={{0,32},{32,64},{64,96},{96,128},{128,160},{160,192},{192,224},{224... | collective-permute-start | bytes 61448 | tf_op jit(solution)/shard_map/ppermute | solution.py:313
  145.5 13.7 %all-to-all-start.7 = ((bf16[16,1,24,128]{3,2,1,0:T(8,128)(2,1)}), bf16[16,1,24,128]{3,2,1,0:T(8,128)(2,1)S(1)}, u32[]{:S(2)}, u32[]{:S(2)}) async-start(bf16[16,1,24,128]{3,2,1,0:T(8,128)(2,1)} %broadcast_in_dim.22), calls=%async_computation.7 | async-start | bytes 196608 | tf_op jit(solution)/shard_map/all_to_all | solution.py:341
  150.7 5.3 %collective-permute-start.9 = (bf16[3,5,16,128]{3,2,1,0:T(8,128)(2,1)S(1)}, bf16[3,5,16,128]{3,2,1,0:T(8,128)(2,1)S(1)}, u32[]{:S(2)}, u32[]{:S(2)}) collective-permute-start(bf16[3,5,16,128]{3,2,1,0:T(8,128)(2,1)S(1)} %pad_maximum_fusion.2.mid), channel_id=1, source_target_pairs={{4,0},{8,4},{12,8},{16,12},{20,16},{24,20},{28,24},{5,1},{9,5},{13... | collective-permute-start | bytes 184328 | tf_op jit(solution)/shard_map/ppermute | solution.py:313
  152.0 5.3 %collective-permute-start.8 = (bf16[3,5,16,128]{3,2,1,0:T(8,128)(2,1)S(1)}, bf16[3,5,16,128]{3,2,1,0:T(8,128)(2,1)S(1)}, u32[]{:S(2)}, u32[]{:S(2)}) collective-permute-start(bf16[3,5,16,128]{3,2,1,0:T(8,128)(2,1)S(1)} %pad_maximum_fusion.2.mid), channel_id=1, source_target_pairs={{0,4},{4,8},{8,12},{12,16},{16,20},{20,24},{24,28},{1,5},{5,9},{9,... | collective-permute-start | bytes 184328 | tf_op jit(solution)/shard_map/ppermute | solution.py:313
  159.9 16.1 %all-to-all-start.8 = ((bf16[32,1,24,128]{3,2,1,0:T(8,128)(2,1)}), bf16[32,1,24,128]{3,2,1,0:T(8,128)(2,1)S(1)}, u32[]{:S(2)}, u32[]{:S(2)}) async-start(bf16[32,1,24,128]{3,2,1,0:T(8,128)(2,1)} %broadcast_in_dim.23), calls=%async_computation.8 | async-start | bytes 393216 | tf_op jit(solution)/shard_map/all_to_all | solution.py:346

commit v5 on v4

--- a/solution.py
+++ b/solution.py
@@ -182,7 +182,7 @@
             hidden_ref[z, y] = jnp.where(inside & exists, folded, 0.0).astype(bf16)
         return carry
 
-    lax.fori_loop(0, 4, layer, 0)
+    lax.fori_loop(0, 4, layer, 0, unroll=True)
     pack = jnp.zeros((EMBED, LANES), f32)
     at = lane((EMBED, LANES))
     for r in range(4):
@@ -198,7 +198,7 @@
     store_lines(lines_ref, jnp.concatenate([sums, counts[:8]], axis=0))
 
 
-def direct_kernel(place, lines_ref, embed_ref, ids_ref, pack_ref, direct_ref, out_ref):
+def direct_kernel(place, lines_ref, embed_ref, ids_ref, pack_ref, direct_ref, sent_ref):
     centers, table = [], []
     row = lax.broadcasted_iota(jnp.int32, (16, CELLS), 0)
     counts = load_lines(lines_ref, 8, 1)
@@ -218,6 +218,13 @@
     row = lax.broadcasted_iota(jnp.int32, (8, ids.shape[1]), 0)
     marks = jnp.where(row == 0, ids.astype(f32), jnp.where(row == 1, share, 0.0))
     direct_ref[...] = jnp.concatenate([direct, marks], axis=0)
+    few = jnp.where(row == 0, (ids >> 8).astype(f32), jnp.where(row == 1, (ids & 255).astype(f32), 0.0))
+    shares = split(share)
+    few = jnp.where(row == 2, shares[0].astype(f32), jnp.where(row == 3, shares[1].astype(f32), few))
+    for i, part in enumerate((direct[:8], direct[8:], few)):
+        for k in range(5):
+            sent_ref[5 * i + k, 2] = part[:, LANES * k : LANES * (k + 1)].astype(bf16)
+    sent_ref[15, 2] = jnp.zeros((8, LANES), bf16)
     sums, _ = scatter(direct[:, :ROW_COLS], ids_ref[...])
     mine = lane((EMBED, CELLS)) == place[3]
     scale = 8.0 / (SEGMENTS * (SEGMENTS - 1.0))
@@ -230,7 +237,10 @@
             total = total + jnp.maximum(push_margin - distance, 0.0) * difference
         push = -scale * jnp.sum(total, axis=1, keepdims=True)
         grad = jnp.where(mine, push, 0.0) - sums[EMBED * g : EMBED * (g + 1)]
-        store_tiles(out_ref, grad, g)
+        for k in range(4):
+            for half in range(2):
+                part = grad[8 * half : 8 * half + 8, LANES * k : LANES * (k + 1)]
+                sent_ref[4 * g + k, half] = part.astype(bf16)
 
 
 def backward_layers(hidden_ref, up_ref, taps_two, grad_ref):
@@ -240,22 +250,37 @@
             grad_ref[z, y] = jnp.where(hidden_ref[z, y].astype(f32) > 0.0, folded, 0.0).astype(bf16)
         return carry
 
-    lax.fori_loop(0, 4, layer, 0)
-
-
-def kernels_kernel(direct_ref, sums_ref, wide_ref, hidden_ref, taps_two, block_ref, tiles_ref, up_ref, grad_ref):
-    table = jnp.concatenate(
-        [jnp.concatenate([sums_ref[4 * i + k] for k in range(4)], axis=1) for i in range(GROUPS)], axis=0
-    )
-    direct = direct_ref[...]
-    ids = direct[EMBED : EMBED + 1].astype(jnp.int32)
-    upstream = VOXELS * (direct[:EMBED] + gather((table,), ids) * direct[EMBED + 1 : EMBED + 2])
-    upstream = upstream.astype(bf16)
-    for r in range(5):
-        block_ref[r] = upstream[:, LANES * r : LANES * (r + 1)]
+    lax.fori_loop(0, 4, layer, 0, unroll=True)
+
+
+def kernels_kernel(direct_ref, got_ref, wide_ref, hidden_ref, taps_two, block_ref, sent_ref, up_ref, grad_ref):
+    def tiles(first, count, which):
+        return jnp.concatenate([got_ref[first + k, which].astype(f32) for k in range(count)], axis=1)
+
+    table = jnp.concatenate([tiles(4 * g, 4, half) for g in range(GROUPS) for half in range(2)], axis=0).astype(bf16)
+    for zb in range(3):
+        if zb == 1:
+            direct = direct_ref[:EMBED]
+            ids = direct_ref[EMBED : EMBED + 1].astype(jnp.int32)
+            share = direct_ref[EMBED + 1 : EMBED + 2]
+        else:
+            which = 2 + zb // 2
+            direct = jnp.concatenate([tiles(0, 5, which), tiles(5, 5, which)], axis=0)
+            few = tiles(10, 5, which)
+            ids = (256.0 * few[0:1] + few[1:2]).astype(jnp.int32)
+            share = few[2:3] + few[3:4]
+        upstream = VOXELS * (direct + gather((table,), ids) * share)
+        rounded = upstream.astype(bf16)
+        for r in range(5):
+            block_ref[zb, r] = rounded[:, LANES * r : LANES * (r + 1)]
+            for half in range(2):
+                part = upstream[8 * half : 8 * half + 8, LANES * r : LANES * (r + 1)]
+                sent_ref[2 * (5 * zb + r) + half, 3] = part.astype(bf16)
+    for n in range(30, 32):
+        sent_ref[n, 3] = jnp.zeros((8, LANES), bf16)
     up_ref[...] = jnp.zeros(up_ref.shape, bf16)
     for r in range(4):
-        up_ref[2 + r // 2, 2 + r % 2, :, 0:LANES] = upstream[:, LANES * r : LANES * (r + 1)]
+        up_ref[2 + r // 2, 2 + r % 2, :, 0:LANES] = block_ref[1, r]
     backward_layers(hidden_ref, up_ref, taps_two, grad_ref)
     over_cells = (((1,), (1,)), ((), ()))
 
@@ -273,7 +298,7 @@
         return one, bias
 
     zeros = jnp.zeros((3 * CHANNELS, 9 * CHANNELS), f32), jnp.zeros((CHANNELS, WIDE), f32)
-    one, bias = lax.fori_loop(0, 4, layer, zeros)
+    one, bias = lax.fori_loop(0, 4, layer, zeros, unroll=True)
     ones = jnp.ones((16, 2 * WIDE), bf16)
     bias = jnp.concatenate(split(bias), axis=1)
     bias = lax.dot_general(ones, bias, over_cells, preferred_element_type=f32)
@@ -283,19 +308,33 @@
     one = jnp.concatenate([one, jnp.zeros((3 * CHANNELS, 80), f32)], axis=1)
     bias = jnp.concatenate([bias] * 3, axis=0)
     two = jnp.concatenate([two, bias, jnp.zeros((3 * EMBED, 32), f32)], axis=1)
-    store_tiles(tiles_ref, jnp.concatenate([one, two], axis=0))
-
-
-def features_kernel(low, mid, high, hidden_ref, taps_two, taps_one, features_ref, up_ref, grad_ref):
+    whole = jnp.concatenate([one, two], axis=0)
+    for i in range(8):
+        for k in range(4):
+            for j in range(3):
+                part = whole[24 * i + 8 * j : 24 * i + 8 * j + 8, LANES * k : LANES * (k + 1)]
+                sent_ref[4 * i + k, j] = part.astype(bf16)
+
+
+def last_kernel(got_ref, mid, hidden_ref, taps_two, taps_one, *rest):
+    features_ref, one_ref, bias_ref, two_ref, low, high, up_ref, grad_ref = rest
+    for n in range(15):
+        for which, ref in ((3, low), (4, high)):
+            tile = [got_ref[2 * n + half, which].astype(f32) for half in range(2)]
+            ref[n // 5, n % 5] = jnp.concatenate(tile, axis=0).astype(bf16)
     widen((low, mid, high), up_ref)
     backward_layers(hidden_ref, up_ref, taps_two, grad_ref)
     for r in range(4):
         folded = fold(jnp.dot(taps_one[...], window(grad_ref, r // 2, r % 2), preferred_element_type=f32))
         features_ref[:, r // 2, r % 2, :] = folded[:, :LANES].astype(bf16)
-
-
-def result_kernel(tiles_ref, one_ref, bias_ref, two_ref):
-    whole = load_tiles(tiles_ref, 0, 8) * (1.0 / VOXELS)
+    whole = jnp.concatenate(
+        [
+            jnp.concatenate([got_ref[4 * i + k, j].astype(f32) for k in range(4)], axis=1)
+            for i in range(8)
+            for j in range(3)
+        ],
+        axis=0,
+    ) * (1.0 / VOXELS)
     for c in range(3):
         part = whole[CHANNELS * c : CHANNELS * (c + 1)]
         for ab in range(9):
@@ -313,13 +352,6 @@
     return lax.ppermute(high, axis, forward), lax.ppermute(low, axis, backward)
 
 
-def surround(block, beside=lambda held: held, then=lambda held: held):
-    low, high = beside(passed(block, block, "gz"))
-    block = jnp.stack([low, block, high])
-    low, high = then(passed(block, block, "gy"))
-    return low, block, high
-
-
 def add_up(pieces):
     return jnp.sum(pieces.astype(f32), 0).astype(pieces.dtype)
 
@@ -328,33 +360,22 @@
     return jnp.broadcast_to(piece[None], (lax.axis_size(axes),) + piece.shape)
 
 
-def steps(tiles, outer, inner):
-    groups = lax.axis_size(outer)
-    held = [tiles.reshape((groups, tiles.shape[0] // groups) + tiles.shape[1:])]
-
-    def scattered(other):
-        other, pieces = lax.optimization_barrier((other, lax.all_to_all(held[0], outer, 0, 0)))
-        held[0] = copies(add_up(pieces), inner)
-        return other
-
-    def exchanged(other):
-        other, pieces = lax.optimization_barrier((other, lax.all_to_all(held[0], inner, 0, 0)))
-        held[0] = copies(add_up(pieces), outer)
-        return other
-
-    def gathered(other):
-        other, pieces = lax.optimization_barrier((other, lax.all_to_all(held[0], outer, 0, 0)))
-        held[0] = pieces.reshape(tiles.shape)
-        return other
-
-    return (scattered, exchanged, gathered), held
-
-
-def total(tiles, outer, inner):
-    moves, held = steps(tiles, outer, inner)
-    for move in moves:
-        move(())
-    return held[0]
+def total(pieces, outer, inner):
+    piece = add_up(lax.all_to_all(pieces, outer, 0, 0))
+    piece = add_up(lax.all_to_all(copies(piece, inner), inner, 0, 0))
+    return lax.all_to_all(copies(piece, outer), outer, 0, 0)
+
+
+def total_and_relay(pieces, outer, inner, stride):
+    held = lax.all_to_all(pieces, outer, 0, 0)
+    piece = add_up(held[:, :-1])
+    pieces = lax.all_to_all(copies(piece, inner), inner, 0, 0)
+    pieces, held = lax.optimization_barrier((pieces, held))
+    piece, block = add_up(pieces), held[:, -1:]
+    none = jnp.zeros_like(block[:stride])
+    low = jnp.concatenate([none, block[:-stride]], axis=0)
+    high = jnp.concatenate([block[stride:], none], axis=0)
+    return lax.all_to_all(jnp.concatenate([copies(piece, outer), low, high], axis=1), outer, 0, 0)
 
 
 def shards(features, segment_ids, kernel_one, bias_one, kernel_two):
@@ -384,7 +405,10 @@
     )(features, segment_ids)
     left, right = passed(first, last, "gx")
     pack = left + right
-    low, mid, high = surround(jnp.concatenate([rows, pack[None, :CHANNELS]], axis=0))
+    block = jnp.concatenate([rows, pack[None, :CHANNELS]], axis=0)
+    low, high = passed(block, block, "gz")
+    mid = jnp.stack([low, block, high])
+    low, high = passed(mid, mid, "gy")
     marks = pack[CHANNELS:]
     wide, hidden, embedding, lines = kernel_call(
         embed_kernel,
@@ -396,24 +420,27 @@
         ],
         scalars=1,
     )(place, low, mid, high, taps_one, taps_two, bias_one[:, None], ids, back_one, back_two, marks)
-    lines = total(lines, ("gy", "gx"), "gz")
-    direct, tiles = kernel_call(direct_kernel, [((24, ROW_COLS + LANES), f32), ((16, 16, LANES), bf16)], scalars=1)(
-        place, lines, embedding, ids, marks
+    lines = total(lines.reshape(32, 9, 1, LANES), ("gy", "gx"), "gz").reshape(lines.shape)
+    direct, sent = kernel_call(
+        direct_kernel, [((24, ROW_COLS + LANES), f32), ((16, 3, 8, LANES), bf16)], scalars=1
+    )(place, lines, embedding, ids, marks)
+    got = total_and_relay(sent, "gz", ("gy", "gx"), 1)
+    back = [((6, 6, EMBED, WIDE), bf16), ((4, 4, CHANNELS, WIDE), bf16)]
+    block = ((3, 5, EMBED, LANES), bf16)
+    mid, sent = kernel_call(kernels_kernel, [block, ((32, 4, 8, LANES), bf16)], scratch=back)(
+        direct, got, wide, hidden, back_two
     )
-    tiles = total(tiles, "gz", ("gy", "gx"))
-    back = [((6, 6, EMBED, WIDE), bf16), ((4, 4, CHANNELS, WIDE), bf16)]
-    block, tiles = kernel_call(
-        kernels_kernel, [((5, EMBED, LANES), bf16), ((32, 24, LANES), bf16)], scratch=back
-    )(direct, tiles, wide, hidden, back_two)
-    moves, held = steps(tiles, ("gy", "gx"), "gz")
-    low, mid, high = surround(block, *moves[:2])
-    (grad_features,) = kernel_call(features_kernel, [((CHANNELS, 2, 2, LANES), bf16)], scratch=back)(
-        low, mid, high, hidden, back_two, back_one
-    )
-    moves[2](())
-    grad_one, grad_bias, grad_two = kernel_call(
-        result_kernel, [((27, CHANNELS, CHANNELS), f32), ((1, CHANNELS), f32), ((27, EMBED, CHANNELS), f32)]
-    )(held[0])
+    got = total_and_relay(sent, ("gy", "gx"), "gz", lax.axis_size("gx"))
+    grad_features, grad_one, grad_bias, grad_two = kernel_call(
+        last_kernel,
+        [
+            ((CHANNELS, 2, 2, LANES), bf16),
+            ((27, CHANNELS, CHANNELS), f32),
+            ((1, CHANNELS), f32),
+            ((27, EMBED, CHANNELS), f32),
+        ],
+        scratch=[block, block] + back,
+    )(got, mid, hidden, back_two, back_one)
     return (
         grad_features,
         grad_one.reshape(3, 3, 3, CHANNELS, CHANNELS),

time: 179 us -> 177 us (0.989)
  blocking collectives: 90.2 us -> 137 us
  starting transfers between devices: 46.1 us -> 20 us
  waiting for transfers between devices: 21.1 us -> 5.26 us
  Pallas kernels: 14.1 us -> 9.88 us
    all_to_all x6 -> x9, blocking collectives: 90.2 us -> 137 us  [the longest x2 29.6 us: total_and_relay(): lax.all_to_all(jnp.concatenate([copies(piece, outer), low, high], axis=1)...]
    all_to_all x3 -> x0, starting transfers between devices: 15.2 us -> none  [the longest x1 6.18 us: gathered(): lax.all_to_all(held[0], outer, 0, 0)]
    all_to_all x3 -> x0, waiting for transfers between devices: 13.7 us -> none  [the longest x1 7.45 us: gathered(): lax.all_to_all(held[0], outer, 0, 0)]
    ppermute x5 -> x3, starting transfers between devices: 17.5 us -> 10 us  [passed(): lax.ppermute(high, axis, forward)]
    pallas_call x5 -> x4, Pallas kernels: 12.4 us -> 8.22 us  [call(): pl.pallas_call(body, out_shape=[jax.ShapeDtypeStruct(shape, dtype) for sh...]
    ppermute x5 -> x3, starting transfers between devices: 13.4 us -> 10 us  [passed(): lax.ppermute(low, axis, backward)]
    ppermute x5 -> x3, waiting for transfers between devices: 3.52 us -> 1.38 us  [passed(): lax.ppermute(high, axis, forward)]
    ppermute x5 -> x3, waiting for transfers between devices: 3.88 us -> 3.88 us  [passed(): lax.ppermute(low, axis, backward)]
  transfers between devices with their start and end apart: 13 -> 6, of which waited for: 9 -> 4; matrix products, arithmetic and copies ran while one was open for 1% -> 1% of each run, Pallas kernels for 1% -> 0%
where the time goes in v5:
time: 177 us; the launch traced here: 176 us
  blocking collectives  137 us (77%)
  starting transfers between devices  20 us (11%)
  Pallas kernels  9.88 us (6%)
  waiting for transfers between devices  5.26 us (3%)
  local copies, waits for them, and re-layouts  3.14 us (2%)
    all_to_all x2, blocking collectives, total_and_relay(): lax.all_to_all(jnp.concatenate([copies(piece, outer), low, high], axis=1)...  29.6 us
    all_to_all x2, blocking collectives, total_and_relay(): held = lax.all_to_all(pieces, outer, 0, 0)  27.8 us
    all_to_all x2, blocking collectives, total_and_relay(): pieces = lax.all_to_all(copies(piece, inner), inner, 0, 0)  25.6 us
    all_to_all x1, blocking collectives, total(): piece = add_up(lax.all_to_all(copies(piece, inner), inner, 0, 0))  20.7 us
    all_to_all x1, blocking collectives, total(): piece = add_up(lax.all_to_all(pieces, outer, 0, 0))  19.8 us
    all_to_all x1, blocking collectives, total(): return lax.all_to_all(copies(piece, outer), outer, 0, 0)  13.2 us
    ppermute x3, starting transfers between devices, passed(): lax.ppermute(high, axis, forward)  10 us
    ppermute x3, starting transfers between devices, passed(): lax.ppermute(low, axis, backward)  10 us
  transfers between devices with their start and end apart: 6, of which 4 were waited for; matrix products, arithmetic and copies ran while one was open for 1% of the time, Pallas kernels for 0%

profile of v5, /device:TPU:1, one launch (start us, length us, event | category | flops | bytes accessed | tf_op | source)
XLA Modules:
  0.0 176.3 jit_solution(18412470621153636492)
XLA Ops:
  0.6 1.7 shard_map.84
  2.3 4.1 %collective-permute-start = (bf16[64,128]{1,0:T(8,128)(2,1)}, bf16[64,128]{1,0:T(8,128)(2,1)S(1)}, u32[]{:S(2)}, u32[]{:S(2)}) collective-permute-start(bf16[64,128]{1,0:T(8,128)(2,1)} %get-tuple-element.24), channel_id=1, source_target_pairs={{0,1},{1,2},{2,3},{4,5},{5,6},{6,7},{8,9},{9,10},{10,11},{12,13},{... | collective-permute-start | bytes 49160 | tf_op jit(solution)/shard_map/ppermute | solution.py:352
  6.4 1.3 collective-permute-start.1
  7.7 3.4 %collective-permute-done.1 = bf16[64,128]{1,0:T(8,128)(2,1)S(1)} collective-permute-done((bf16[64,128]{1,0:T(8,128)(2,1)}, bf16[64,128]{1,0:T(8,128)(2,1)S(1)}, u32[]{:S(2)}, u32[]{:S(2)}) %collective-permute-start.1) | collective-permute-done | bytes 16416 | tf_op jit(solution)/shard_map/ppermute | solution.py:352
  11.1 7.3 %collective-permute-start.3 = (bf16[5,48,128]{2,1,0:T(8,128)(2,1)S(1)}, bf16[5,48,128]{2,1,0:T(8,128)(2,1)S(1)}, u32[]{:S(2)}, u32[]{:S(2)}) collective-permute-start(bf16[5,48,128]{2,1,0:T(8,128)(2,1)S(1)} %get-tuple-element.47), channel_id=1, source_target_pairs={{32,0},{64,32},{96,64},{128,96},{160,128},{192,160},{224,192},{256... | collective-permute-start | bytes 184328 | tf_op jit(solution)/shard_map/ppermute | solution.py:352
  18.4 1.9 %collective-permute-start.2 = (bf16[5,48,128]{2,1,0:T(8,128)(2,1)S(1)}, bf16[5,48,128]{2,1,0:T(8,128)(2,1)S(1)}, u32[]{:S(2)}, u32[]{:S(2)}) collective-permute-start(bf16[5,48,128]{2,1,0:T(8,128)(2,1)S(1)} %get-tuple-element.47), channel_id=1, source_target_pairs={{0,32},{32,64},{64,96},{96,128},{128,160},{160,192},{192,224},{224... | collective-permute-start | bytes 184328 | tf_op jit(solution)/shard_map/ppermute | solution.py:352
  20.4 0.6 copy-done.4
  21.1 0.5 collective-permute-done.2
  21.7 1.4 collective-permute-start.5
  23.1 4.0 %collective-permute-start.4 = (bf16[3,5,48,128]{3,2,1,0:T(8,128)(2,1)S(1)}, bf16[3,5,48,128]{3,2,1,0:T(8,128)(2,1)S(1)}, u32[]{:S(2)}, u32[]{:S(2)}) collective-permute-start(bf16[3,5,48,128]{3,2,1,0:T(8,128)(2,1)S(1)} %pad_maximum_fusion.mid), channel_id=1, source_target_pairs={{0,4},{4,8},{8,12},{12,16},{16,20},{20,24},{24,28},{1,5},{5,9},{9,... | collective-permute-start | bytes 552968 | tf_op jit(solution)/shard_map/ppermute | solution.py:352
  27.2 0.1 reshape.56
  27.5 0.1 reshape.53.taps_two
  27.7 0.7 copy-done.1
  28.3 0.2 copy.32
  28.6 0.3 reshape.55.back_one.taps_one
  28.8 0.2 copy.30
  29.0 0.3 reshape.52.taps_one
  29.4 0.5 collective-permute-done.5.high
  29.9 0.9 collective-permute-done.4.low
  30.8 2.0 %shard_map.85 = (bf16[6,6,48,256]{3,2,1,0:T(8,128)(2,1)S(1)}, bf16[4,4,48,256]{3,2,1,0:T(8,128)(2,1)S(1)}, f32[16,640]{1,0:T(8,128)S(1)}, f32[288,1,128]{2,1,0:T(1,128)S(1)}) custom-call(s32[7]{0:T(128)S(1)} %stack.31.place, bf16[3,5,48,128]{3,2,1,0:T(8,128)(2,1)S(1)} %collective-permute-done.4.low, bf16[3,5,48,128]{3,2,1,0:T(8,128)(2,1)S(1)} %pad_maximum_fusion.mid, ...), custom_call_target="tpu_custom_call" | custom-call | tf_op jit(solution)/shard_map/pallas_call | solution.py:28
  32.7 19.8 %all_to_all.45 = f32[32,9,1,128]{3,2,1,0:T(1,128)S(1)} all-to-all(f32[32,9,1,128]{3,2,1,0:T(1,128)S(1)} %bitcast.26), channel_id=1, replica_groups=mesh['gz'=16,'gy'=8,'gx'=4] {'gy','gx'}, dimensions={0} | all-to-all | bytes 294912 | tf_op jit(solution)/shard_map/all_to_all | solution.py:364
  52.6 20.7 %all_to_all.46 = f32[16,9,1,128]{3,2,1,0:T(1,128)S(1)} all-to-all(f32[16,9,1,128]{3,2,1,0:T(1,128)S(1)} %broadcast_in_dim.18), channel_id=1, replica_groups=mesh['gz'=16,'gy'=8,'gx'=4] {'gz'}, dimensions={0} | all-to-all | bytes 147456 | tf_op jit(solution)/shard_map/all_to_all | solution.py:365
  73.5 13.2 %all_to_all.47 = f32[32,9,1,128]{3,2,1,0:T(1,128)S(1)} all-to-all(f32[32,9,1,128]{3,2,1,0:T(1,128)S(1)} %broadcast_in_dim.19), channel_id=1, replica_groups=mesh['gz'=16,'gy'=8,'gx'=4] {'gy','gx'}, dimensions={0} | all-to-all | bytes 294912 | tf_op jit(solution)/shard_map/all_to_all | solution.py:366
  86.7 1.3 shard_map.86
  88.0 12.5 %all_to_all.48 = bf16[16,3,8,128]{3,2,1,0:T(8,128)(2,1)S(1)} all-to-all(bf16[16,3,8,128]{3,2,1,0:T(8,128)(2,1)S(1)} %get-tuple-element.29), channel_id=1, replica_groups=mesh['gz'=16,'gy'=8,'gx'=4] {'gz'}, dimensions={0} | all-to-all | bytes 196608 | tf_op jit(solution)/shard_map/all_to_all | solution.py:370
  100.5 13.1 %all_to_all.49 = bf16[32,2,8,128]{3,2,1,0:T(8,128)(2,1)S(1)} all-to-all(bf16[32,2,8,128]{3,2,1,0:T(8,128)(2,1)S(1)} %broadcast_in_dim.20), channel_id=1, replica_groups=mesh['gz'=16,'gy'=8,'gx'=4] {'gy','gx'}, dimensions={0} | all-to-all | bytes 262144 | tf_op jit(solution)/shard_map/all_to_all | solution.py:372
  113.7 13.0 %all_to_all.50.got_ref = bf16[16,4,8,128]{3,2,1,0:T(8,128)(2,1)S(1)} all-to-all(bf16[16,4,8,128]{3,2,1,0:T(8,128)(2,1)S(1)} %fusion.9), channel_id=1, replica_groups=mesh['gz'=16,'gy'=8,'gx'=4] {'gz'}, dimensions={0} | all-to-all | bytes 262144 | tf_op jit(solution)/shard_map/all_to_all | solution.py:378
  126.7 3.0 %shard_map.87 = (bf16[3,5,16,128]{3,2,1,0:T(8,128)(2,1)S(1)}, bf16[32,4,8,128]{3,2,1,0:T(8,128)(2,1)S(1)}) custom-call(f32[24,640]{1,0:T(8,128)S(1)} %get-tuple-element.28.direct_ref, bf16[16,4,8,128]{3,2,1,0:T(8,128)(2,1)S(1)} %all_to_all.50.got_ref, bf16[6,6,48,256]{3,2,1,0:T(8,128)(2,1)S(1)} %get-tuple-element.32.wide_ref, ...), custom_call_target="tpu_custom_call" | custom-call | tf_op jit(solution)/shard_map/pallas_call | solution.py:28
  129.7 15.3 %all_to_all.51 = bf16[32,4,8,128]{3,2,1,0:T(8,128)(2,1)S(1)} all-to-all(bf16[32,4,8,128]{3,2,1,0:T(8,128)(2,1)S(1)} %get-tuple-element.34), channel_id=1, replica_groups=mesh['gz'=16,'gy'=8,'gx'=4] {'gy','gx'}, dimensions={0} | all-to-all | bytes 524288 | tf_op jit(solution)/shard_map/all_to_all | solution.py:370
  145.1 12.5 %all_to_all.52 = bf16[16,3,8,128]{3,2,1,0:T(8,128)(2,1)S(1)} all-to-all(bf16[16,3,8,128]{3,2,1,0:T(8,128)(2,1)S(1)} %broadcast_in_dim.22), channel_id=1, replica_groups=mesh['gz'=16,'gy'=8,'gx'=4] {'gz'}, dimensions={0} | all-to-all | bytes 196608 | tf_op jit(solution)/shard_map/all_to_all | solution.py:372
  157.8 16.6 %all_to_all.53.got_ref = bf16[32,5,8,128]{3,2,1,0:T(8,128)(2,1)S(1)} all-to-all(bf16[32,5,8,128]{3,2,1,0:T(8,128)(2,1)S(1)} %fusion.4), channel_id=1, replica_groups=mesh['gz'=16,'gy'=8,'gx'=4] {'gy','gx'}, dimensions={0} | all-to-all | bytes 655360 | tf_op jit(solution)/shard_map/all_to_all | solution.py:378
  174.3 2.0 %shard_map.88 = (bf16[48,2,2,128]{3,2,1,0:T(2,128)(2,1)}, f32[27,48,48]{2,1,0:T(8,128)}, f32[1,48]{1,0:T(1,128)}, f32[27,16,48]{2,1,0:T(8,128)}) custom-call(bf16[32,5,8,128]{3,2,1,0:T(8,128)(2,1)S(1)} %all_to_all.53.got_ref, bf16[3,5,16,128]{3,2,1,0:T(8,128)(2,1)S(1)} %get-tuple-element.37.mid, bf16[4,4,48,256]{3,2,1,0:T(8,128)(2,1)S(1)} %get-tuple-element.33.hidden_ref, ...), custom_call_target="tpu_custom_call" | custom-call | tf_op jit(solution)/shard_map/pallas_call | solution.py:28
  (38 shorter events, 1.1 us)
Async XLA Ops:
  2.3 8.8 %copy-start.3 = (bf16[4,48,128]{2,1,0:T(8,128)(2,1)S(1)}, bf16[4,48,128]{2,1,0:T(8,128)(2,1)}, u32[]{:S(2)}) copy-start(bf16[4,48,128]{2,1,0:T(8,128)(2,1)} %get-tuple-element.23) | copy-start | bytes 147460
  2.3 5.4 %collective-permute-start = (bf16[64,128]{1,0:T(8,128)(2,1)}, bf16[64,128]{1,0:T(8,128)(2,1)S(1)}, u32[]{:S(2)}, u32[]{:S(2)}) collective-permute-start(bf16[64,128]{1,0:T(8,128)(2,1)} %get-tuple-element.24), channel_id=1, source_target_pairs={{0,1},{1,2},{2,3},{4,5},{5,6},{6,7},{8,9},{9,10},{10,11},{12,13},{... | collective-permute-start | bytes 49160 | tf_op jit(solution)/shard_map/ppermute | solution.py:352
  6.4 4.7 %collective-permute-start.1 = (bf16[64,128]{1,0:T(8,128)(2,1)}, bf16[64,128]{1,0:T(8,128)(2,1)S(1)}, u32[]{:S(2)}, u32[]{:S(2)}) collective-permute-start(bf16[64,128]{1,0:T(8,128)(2,1)} %get-tuple-element.25), channel_id=1, source_target_pairs={{1,0},{2,1},{3,2},{5,4},{6,5},{7,6},{9,8},{10,9},{11,10},{13,12},{... | collective-permute-start | bytes 49160 | tf_op jit(solution)/shard_map/ppermute | solution.py:352
  11.1 10.0 %collective-permute-start.3 = (bf16[5,48,128]{2,1,0:T(8,128)(2,1)S(1)}, bf16[5,48,128]{2,1,0:T(8,128)(2,1)S(1)}, u32[]{:S(2)}, u32[]{:S(2)}) collective-permute-start(bf16[5,48,128]{2,1,0:T(8,128)(2,1)S(1)} %get-tuple-element.47), channel_id=1, source_target_pairs={{32,0},{64,32},{96,64},{128,96},{160,128},{192,160},{224,192},{256... | collective-permute-start | bytes 184328 | tf_op jit(solution)/shard_map/ppermute | solution.py:352
  18.4 3.2 %collective-permute-start.2 = (bf16[5,48,128]{2,1,0:T(8,128)(2,1)S(1)}, bf16[5,48,128]{2,1,0:T(8,128)(2,1)S(1)}, u32[]{:S(2)}, u32[]{:S(2)}) collective-permute-start(bf16[5,48,128]{2,1,0:T(8,128)(2,1)S(1)} %get-tuple-element.47), channel_id=1, source_target_pairs={{0,32},{32,64},{64,96},{96,128},{128,160},{160,192},{192,224},{224... | collective-permute-start | bytes 184328 | tf_op jit(solution)/shard_map/ppermute | solution.py:352
  20.4 0.7 copy-start.4
  21.6 5.5 %copy-start.2 = (bf16[3,3,3,16,48]{4,3,2,1,0:T(8,128)(2,1)S(1)}, bf16[3,3,3,16,48]{4,3,2,1,0:T(8,128)(2,1)}, u32[]{:S(2)}) copy-start(bf16[3,3,3,16,48]{4,3,2,1,0:T(8,128)(2,1)} %param.9) | copy-start | bytes 124420
  21.7 8.2 %collective-permute-start.5 = (bf16[3,5,48,128]{3,2,1,0:T(8,128)(2,1)S(1)}, bf16[3,5,48,128]{3,2,1,0:T(8,128)(2,1)S(1)}, u32[]{:S(2)}, u32[]{:S(2)}) collective-permute-start(bf16[3,5,48,128]{3,2,1,0:T(8,128)(2,1)S(1)} %pad_maximum_fusion.mid), channel_id=1, source_target_pairs={{4,0},{8,4},{12,8},{16,12},{20,16},{24,20},{28,24},{5,1},{9,5},{13... | collective-permute-start | bytes 552968 | tf_op jit(solution)/shard_map/ppermute | solution.py:352
  23.1 7.7 %collective-permute-start.4 = (bf16[3,5,48,128]{3,2,1,0:T(8,128)(2,1)S(1)}, bf16[3,5,48,128]{3,2,1,0:T(8,128)(2,1)S(1)}, u32[]{:S(2)}, u32[]{:S(2)}) collective-permute-start(bf16[3,5,48,128]{3,2,1,0:T(8,128)(2,1)S(1)} %pad_maximum_fusion.mid), channel_id=1, source_target_pairs={{0,4},{4,8},{8,12},{12,16},{16,20},{20,24},{24,28},{1,5},{5,9},{9,... | collective-permute-start | bytes 552968 | tf_op jit(solution)/shard_map/ppermute | solution.py:352
  27.3 1.0 copy-start.1
  29.4 1.4 copy-start

commit v6 on v5

--- a/solution.py
+++ b/solution.py
@@ -74,22 +74,26 @@
     return pltpu.roll(taps[:size], 1, 1) + taps[size : 2 * size] + pltpu.roll(taps[2 * size :], WIDE - 1, 1)
 
 
-def split(value):
-    high = value.astype(bf16)
-    return high, (value - high.astype(f32)).astype(bf16)
+def split(value, count):
+    parts = []
+    for _ in range(count):
+        parts.append(value.astype(bf16))
+        value = value - parts[-1].astype(f32)
+    return tuple(parts)
 
 
 def hot(cell):
     return jnp.where(lax.broadcasted_iota(jnp.int32, (CELLS, cell.shape[1]), 0) == cell, 1.0, 0.0).astype(bf16)
 
 
-def scatter(values, ids, more=()):
+def scatter(values, ids, count, more=()):
     group, cell = ids >> 9, ids & (CELLS - 1)
     spread = jnp.concatenate([jnp.where(group == g, values, 0.0) for g in range(GROUPS)], axis=0)
     size = spread.shape[0]
-    both = jnp.concatenate(split(spread) + tuple(more), axis=0)
-    sums = lax.dot_general(both, hot(cell), (((1,), (1,)), ((), ())), preferred_element_type=f32)
-    return sums[:size] + sums[size : 2 * size], sums[2 * size :]
+    parts = jnp.concatenate(split(spread, count) + tuple(more), axis=0)
+    sums = lax.dot_general(parts, hot(cell), (((1,), (1,)), ((), ())), preferred_element_type=f32)
+    found = sum(sums[size * i : size * (i + 1)] for i in range(1, count)) + sums[:size]
+    return found, sums[count * size :]
 
 
 def gather(parts, ids):
@@ -143,7 +147,7 @@
     )
 
 
-def edge_kernel(features_hbm, ids_hbm, rows_ref, first_ref, last_ref, features_ref, ids_ref, done):
+def edge_kernel(features_hbm, ids_hbm, first_ref, last_ref, features_ref, ids_ref, done):
     fetches = [
         pltpu.make_async_copy(features_hbm, features_ref, done.at[0]),
         pltpu.make_async_copy(ids_hbm, ids_ref, done.at[1]),
@@ -157,7 +161,6 @@
     rows = []
     for r in range(4):
         mine = features[:, r // 2, r % 2, :]
-        rows_ref[r] = mine.astype(bf16)
         ids = ids_ref[r // 2, r % 2 : r % 2 + 1]
         marks = jnp.where(row == 0, ids >> 8, jnp.where(row == 1, ids & 255, jnp.where(row == 2, 1, 0)))
         rows.append(jnp.concatenate([mine, marks.astype(f32)], axis=0))
@@ -194,7 +197,7 @@
     ids = ids_ref[...]
     row = lax.broadcasted_iota(jnp.int32, (16, CELLS), 0)
     ones = jnp.where((ids >> 9) == row, 1.0, 0.0).astype(bf16)
-    sums, counts = scatter(embed_ref[:, :ROW_COLS], ids, (ones,))
+    sums, counts = scatter(embed_ref[:, :ROW_COLS], ids, 3, (ones,))
     store_lines(lines_ref, jnp.concatenate([sums, counts[:8]], axis=0))
 
 
@@ -210,7 +213,7 @@
     pack_ids = (256.0 * pack[0:1] + pack[1:2]).astype(jnp.int32)
     ids = jnp.concatenate([ids_ref[...], pack_ids], axis=1)
     mark = jnp.concatenate([jnp.ones((1, ROW_COLS), f32), pack[2:3]], axis=1)
-    near = gather(split(jnp.concatenate(table, axis=0)), ids)
+    near = gather(split(jnp.concatenate(table, axis=0), 3), ids)
     share = near[EMBED : EMBED + 1] * mark
     offset = embed_ref[...] - near[:EMBED]
     hinge = jnp.maximum(jnp.sum(offset * offset, axis=0, keepdims=True) - pull_margin, 0.0)
@@ -219,13 +222,13 @@
     marks = jnp.where(row == 0, ids.astype(f32), jnp.where(row == 1, share, 0.0))
     direct_ref[...] = jnp.concatenate([direct, marks], axis=0)
     few = jnp.where(row == 0, (ids >> 8).astype(f32), jnp.where(row == 1, (ids & 255).astype(f32), 0.0))
-    shares = split(share)
+    shares = split(share, 2)
     few = jnp.where(row == 2, shares[0].astype(f32), jnp.where(row == 3, shares[1].astype(f32), few))
     for i, part in enumerate((direct[:8], direct[8:], few)):
         for k in range(5):
             sent_ref[5 * i + k, 2] = part[:, LANES * k : LANES * (k + 1)].astype(bf16)
     sent_ref[15, 2] = jnp.zeros((8, LANES), bf16)
-    sums, _ = scatter(direct[:, :ROW_COLS], ids_ref[...])
+    sums, _ = scatter(direct[:, :ROW_COLS], ids_ref[...], 2)
     mine = lane((EMBED, CELLS)) == place[3]
     scale = 8.0 / (SEGMENTS * (SEGMENTS - 1.0))
     for g in range(GROUPS):
@@ -300,7 +303,7 @@
     zeros = jnp.zeros((3 * CHANNELS, 9 * CHANNELS), f32), jnp.zeros((CHANNELS, WIDE), f32)
     one, bias = lax.fori_loop(0, 4, layer, zeros, unroll=True)
     ones = jnp.ones((16, 2 * WIDE), bf16)
-    bias = jnp.concatenate(split(bias), axis=1)
+    bias = jnp.concatenate(split(bias, 2), axis=1)
     bias = lax.dot_general(ones, bias, over_cells, preferred_element_type=f32)
     moved = jnp.concatenate([shifted(up_ref[2 + r // 2, 2 + r % 2]) for r in range(4)], axis=1)
     seen = jnp.concatenate([window(hidden_ref, r // 2, r % 2) for r in range(4)], axis=1)
@@ -391,18 +394,18 @@
     back_two = jnp.transpose(kernel_two[::-1, ::-1, ::-1], (2, 4, 0, 1, 3)).reshape(3 * CHANNELS, 9 * EMBED)
     ids = segment_ids.reshape(1, ROW_COLS)
 
-    rows, first, last = pl.pallas_call(
+    first, last = pl.pallas_call(
         edge_kernel,
-        out_shape=[jax.ShapeDtypeStruct((4, CHANNELS, LANES), bf16)]
-        + [jax.ShapeDtypeStruct((CHANNELS + 16, LANES), bf16)] * 2,
+        out_shape=[jax.ShapeDtypeStruct((CHANNELS + 16, LANES), bf16)] * 2,
         in_specs=[pl.BlockSpec(memory_space=pl.ANY)] * 2,
-        out_specs=[pl.BlockSpec(memory_space=pltpu.VMEM)] * 3,
+        out_specs=[pl.BlockSpec(memory_space=pltpu.VMEM)] * 2,
         scratch_shapes=[
             pltpu.VMEM(features.shape, bf16),
             pltpu.VMEM(segment_ids.shape, jnp.int32),
             pltpu.SemaphoreType.DMA((2,)),
         ],
     )(features, segment_ids)
+    rows = jnp.transpose(features, (1, 2, 0, 3)).reshape(4, CHANNELS, LANES)
     left, right = passed(first, last, "gx")
     pack = left + right
     block = jnp.concatenate([rows, pack[None, :CHANNELS]], axis=0)

time: 177 us -> 177 us (level)
  no operation moved by 1% of the time
where the time goes in v6:
time: 177 us; the launch traced here: 176 us
  blocking collectives  137 us (77%)
  starting transfers between devices  19.9 us (11%)
  Pallas kernels  9.99 us (6%)
  waiting for transfers between devices  5.23 us (3%)
  local copies, waits for them, and re-layouts  3.14 us (2%)
    all_to_all x2, blocking collectives, total_and_relay(): lax.all_to_all(jnp.concatenate([copies(piece, outer), low, high], axis=1)...  29.6 us
    all_to_all x2, blocking collectives, total_and_relay(): held = lax.all_to_all(pieces, outer, 0, 0)  27.8 us
    all_to_all x2, blocking collectives, total_and_relay(): pieces = lax.all_to_all(copies(piece, inner), inner, 0, 0)  25.6 us
    all_to_all x1, blocking collectives, total(): piece = add_up(lax.all_to_all(copies(piece, inner), inner, 0, 0))  20.8 us
    all_to_all x1, blocking collectives, total(): piece = add_up(lax.all_to_all(pieces, outer, 0, 0))  19.7 us
    all_to_all x1, blocking collectives, total(): return lax.all_to_all(copies(piece, outer), outer, 0, 0)  13.2 us
    ppermute x3, starting transfers between devices, passed(): lax.ppermute(low, axis, backward)  10 us
    ppermute x3, starting transfers between devices, passed(): lax.ppermute(high, axis, forward)  9.88 us
  transfers between devices with their start and end apart: 6, of which 4 were waited for; matrix products, arithmetic and copies ran while one was open for 1% of the time, Pallas kernels for 0%

profile of v6, /device:TPU:1, one launch (start us, length us, event | category | flops | bytes accessed | tf_op | source)
XLA Modules:
  0.0 176.3 jit_solution(1343394042697808245)
XLA Ops:
  0.6 1.6 shard_map.84
  2.3 3.9 %collective-permute-start = (bf16[64,128]{1,0:T(8,128)(2,1)}, bf16[64,128]{1,0:T(8,128)(2,1)S(1)}, u32[]{:S(2)}, u32[]{:S(2)}) collective-permute-start(bf16[64,128]{1,0:T(8,128)(2,1)} %get-tuple-element.22), channel_id=1, source_target_pairs={{0,1},{1,2},{2,3},{4,5},{5,6},{6,7},{8,9},{9,10},{10,11},{12,13},{... | collective-permute-start | bytes 49160 | tf_op jit(solution)/shard_map/ppermute | solution.py:355
  6.2 1.3 collective-permute-start.1
  7.6 3.4 %collective-permute-done.1 = bf16[64,128]{1,0:T(8,128)(2,1)S(1)} collective-permute-done((bf16[64,128]{1,0:T(8,128)(2,1)}, bf16[64,128]{1,0:T(8,128)(2,1)S(1)}, u32[]{:S(2)}, u32[]{:S(2)}) %collective-permute-start.1) | collective-permute-done | bytes 16416 | tf_op jit(solution)/shard_map/ppermute | solution.py:355
  11.0 7.3 %collective-permute-start.3 = (bf16[5,48,128]{2,1,0:T(8,128)(2,1)S(1)}, bf16[5,48,128]{2,1,0:T(8,128)(2,1)S(1)}, u32[]{:S(2)}, u32[]{:S(2)}) collective-permute-start(bf16[5,48,128]{2,1,0:T(8,128)(2,1)S(1)} %get-tuple-element.45), channel_id=1, source_target_pairs={{32,0},{64,32},{96,64},{128,96},{160,128},{192,160},{224,192},{256... | collective-permute-start | bytes 184328 | tf_op jit(solution)/shard_map/ppermute | solution.py:355
  18.3 1.9 %collective-permute-start.2 = (bf16[5,48,128]{2,1,0:T(8,128)(2,1)S(1)}, bf16[5,48,128]{2,1,0:T(8,128)(2,1)S(1)}, u32[]{:S(2)}, u32[]{:S(2)}) collective-permute-start(bf16[5,48,128]{2,1,0:T(8,128)(2,1)S(1)} %get-tuple-element.45), channel_id=1, source_target_pairs={{0,32},{32,64},{64,96},{96,128},{128,160},{160,192},{192,224},{224... | collective-permute-start | bytes 184328 | tf_op jit(solution)/shard_map/ppermute | solution.py:355
  20.2 0.6 copy-done.4
  21.0 0.5 collective-permute-done.2
  21.5 1.4 collective-permute-start.5
  22.9 4.0 %collective-permute-start.4 = (bf16[3,5,48,128]{3,2,1,0:T(8,128)(2,1)S(1)}, bf16[3,5,48,128]{3,2,1,0:T(8,128)(2,1)S(1)}, u32[]{:S(2)}, u32[]{:S(2)}) collective-permute-start(bf16[3,5,48,128]{3,2,1,0:T(8,128)(2,1)S(1)} %pad_maximum_fusion.mid), channel_id=1, source_target_pairs={{0,4},{4,8},{8,12},{12,16},{16,20},{20,24},{24,28},{1,5},{5,9},{9,... | collective-permute-start | bytes 552968 | tf_op jit(solution)/shard_map/ppermute | solution.py:355
  27.0 0.1 reshape.60
  27.4 0.1 reshape.57.taps_two
  27.5 0.7 copy-done.1
  28.2 0.2 copy.36
  28.4 0.3 reshape.59.back_one.taps_one
  28.7 0.2 copy.34
  28.9 0.3 reshape.56.taps_one
  29.2 0.5 collective-permute-done.5.high
  29.7 0.9 collective-permute-done.4.low
  30.6 2.0 %shard_map.85 = (bf16[6,6,48,256]{3,2,1,0:T(8,128)(2,1)S(1)}, bf16[4,4,48,256]{3,2,1,0:T(8,128)(2,1)S(1)}, f32[16,640]{1,0:T(8,128)S(1)}, f32[288,1,128]{2,1,0:T(1,128)S(1)}) custom-call(s32[7]{0:T(128)S(1)} %stack.31.place, bf16[3,5,48,128]{3,2,1,0:T(8,128)(2,1)S(1)} %collective-permute-done.4.low, bf16[3,5,48,128]{3,2,1,0:T(8,128)(2,1)S(1)} %pad_maximum_fusion.mid, ...), custom_call_target="tpu_custom_call" | custom-call | tf_op jit(solution)/shard_map/pallas_call | solution.py:28
  32.6 19.7 %all_to_all.45 = f32[32,9,1,128]{3,2,1,0:T(1,128)S(1)} all-to-all(f32[32,9,1,128]{3,2,1,0:T(1,128)S(1)} %bitcast.28), channel_id=1, replica_groups=mesh['gz'=16,'gy'=8,'gx'=4] {'gy','gx'}, dimensions={0} | all-to-all | bytes 294912 | tf_op jit(solution)/shard_map/all_to_all | solution.py:367
  52.5 20.8 %all_to_all.46 = f32[16,9,1,128]{3,2,1,0:T(1,128)S(1)} all-to-all(f32[16,9,1,128]{3,2,1,0:T(1,128)S(1)} %broadcast_in_dim.18), channel_id=1, replica_groups=mesh['gz'=16,'gy'=8,'gx'=4] {'gz'}, dimensions={0} | all-to-all | bytes 147456 | tf_op jit(solution)/shard_map/all_to_all | solution.py:368
  73.4 13.2 %all_to_all.47 = f32[32,9,1,128]{3,2,1,0:T(1,128)S(1)} all-to-all(f32[32,9,1,128]{3,2,1,0:T(1,128)S(1)} %broadcast_in_dim.19), channel_id=1, replica_groups=mesh['gz'=16,'gy'=8,'gx'=4] {'gy','gx'}, dimensions={0} | all-to-all | bytes 294912 | tf_op jit(solution)/shard_map/all_to_all | solution.py:369
  86.6 1.4 shard_map.86
  88.0 12.5 %all_to_all.48 = bf16[16,3,8,128]{3,2,1,0:T(8,128)(2,1)S(1)} all-to-all(bf16[16,3,8,128]{3,2,1,0:T(8,128)(2,1)S(1)} %get-tuple-element.27), channel_id=1, replica_groups=mesh['gz'=16,'gy'=8,'gx'=4] {'gz'}, dimensions={0} | all-to-all | bytes 196608 | tf_op jit(solution)/shard_map/all_to_all | solution.py:373
  100.5 13.1 %all_to_all.49 = bf16[32,2,8,128]{3,2,1,0:T(8,128)(2,1)S(1)} all-to-all(bf16[32,2,8,128]{3,2,1,0:T(8,128)(2,1)S(1)} %broadcast_in_dim.20), channel_id=1, replica_groups=mesh['gz'=16,'gy'=8,'gx'=4] {'gy','gx'}, dimensions={0} | all-to-all | bytes 262144 | tf_op jit(solution)/shard_map/all_to_all | solution.py:375
  113.7 13.0 %all_to_all.50.got_ref = bf16[16,4,8,128]{3,2,1,0:T(8,128)(2,1)S(1)} all-to-all(bf16[16,4,8,128]{3,2,1,0:T(8,128)(2,1)S(1)} %fusion.9), channel_id=1, replica_groups=mesh['gz'=16,'gy'=8,'gx'=4] {'gz'}, dimensions={0} | all-to-all | bytes 262144 | tf_op jit(solution)/shard_map/all_to_all | solution.py:381
  126.7 3.0 %shard_map.87 = (bf16[3,5,16,128]{3,2,1,0:T(8,128)(2,1)S(1)}, bf16[32,4,8,128]{3,2,1,0:T(8,128)(2,1)S(1)}) custom-call(f32[24,640]{1,0:T(8,128)S(1)} %get-tuple-element.26.direct_ref, bf16[16,4,8,128]{3,2,1,0:T(8,128)(2,1)S(1)} %all_to_all.50.got_ref, bf16[6,6,48,256]{3,2,1,0:T(8,128)(2,1)S(1)} %get-tuple-element.30.wide_ref, ...), custom_call_target="tpu_custom_call" | custom-call | tf_op jit(solution)/shard_map/pallas_call | solution.py:28
  129.7 15.3 %all_to_all.51 = bf16[32,4,8,128]{3,2,1,0:T(8,128)(2,1)S(1)} all-to-all(bf16[32,4,8,128]{3,2,1,0:T(8,128)(2,1)S(1)} %get-tuple-element.32), channel_id=1, replica_groups=mesh['gz'=16,'gy'=8,'gx'=4] {'gy','gx'}, dimensions={0} | all-to-all | bytes 524288 | tf_op jit(solution)/shard_map/all_to_all | solution.py:373
  145.1 12.5 %all_to_all.52 = bf16[16,3,8,128]{3,2,1,0:T(8,128)(2,1)S(1)} all-to-all(bf16[16,3,8,128]{3,2,1,0:T(8,128)(2,1)S(1)} %broadcast_in_dim.22), channel_id=1, replica_groups=mesh['gz'=16,'gy'=8,'gx'=4] {'gz'}, dimensions={0} | all-to-all | bytes 196608 | tf_op jit(solution)/shard_map/all_to_all | solution.py:375
  157.7 16.6 %all_to_all.53.got_ref = bf16[32,5,8,128]{3,2,1,0:T(8,128)(2,1)S(1)} all-to-all(bf16[32,5,8,128]{3,2,1,0:T(8,128)(2,1)S(1)} %fusion.4), channel_id=1, replica_groups=mesh['gz'=16,'gy'=8,'gx'=4] {'gy','gx'}, dimensions={0} | all-to-all | bytes 655360 | tf_op jit(solution)/shard_map/all_to_all | solution.py:381
  174.3 2.0 %shard_map.88 = (bf16[48,2,2,128]{3,2,1,0:T(2,128)(2,1)}, f32[27,48,48]{2,1,0:T(8,128)}, f32[1,48]{1,0:T(1,128)}, f32[27,16,48]{2,1,0:T(8,128)}) custom-call(bf16[32,5,8,128]{3,2,1,0:T(8,128)(2,1)S(1)} %all_to_all.53.got_ref, bf16[3,5,16,128]{3,2,1,0:T(8,128)(2,1)S(1)} %get-tuple-element.35.mid, bf16[4,4,48,256]{3,2,1,0:T(8,128)(2,1)S(1)} %get-tuple-element.31.hidden_ref, ...), custom_call_target="tpu_custom_call" | custom-call | tf_op jit(solution)/shard_map/pallas_call | solution.py:28
  (39 shorter events, 1.1 us)
Async XLA Ops:
  0.6 6.9 %copy-start.3 = (bf16[48,2,2,128]{3,2,1,0:T(2,128)(2,1)S(1)}, bf16[48,2,2,128]{3,2,1,0:T(2,128)(2,1)}, u32[]{:S(2)}) copy-start(bf16[48,2,2,128]{3,2,1,0:T(2,128)(2,1)} %features_hbm.1) | copy-start | bytes 147460
  2.3 5.3 %collective-permute-start = (bf16[64,128]{1,0:T(8,128)(2,1)}, bf16[64,128]{1,0:T(8,128)(2,1)S(1)}, u32[]{:S(2)}, u32[]{:S(2)}) collective-permute-start(bf16[64,128]{1,0:T(8,128)(2,1)} %get-tuple-element.22), channel_id=1, source_target_pairs={{0,1},{1,2},{2,3},{4,5},{5,6},{6,7},{8,9},{9,10},{10,11},{12,13},{... | collective-permute-start | bytes 49160 | tf_op jit(solution)/shard_map/ppermute | solution.py:355
  6.2 4.7 %collective-permute-start.1 = (bf16[64,128]{1,0:T(8,128)(2,1)}, bf16[64,128]{1,0:T(8,128)(2,1)S(1)}, u32[]{:S(2)}, u32[]{:S(2)}) collective-permute-start(bf16[64,128]{1,0:T(8,128)(2,1)} %get-tuple-element.23), channel_id=1, source_target_pairs={{1,0},{2,1},{3,2},{5,4},{6,5},{7,6},{9,8},{10,9},{11,10},{13,12},{... | collective-permute-start | bytes 49160 | tf_op jit(solution)/shard_map/ppermute | solution.py:355
  11.0 10.0 %collective-permute-start.3 = (bf16[5,48,128]{2,1,0:T(8,128)(2,1)S(1)}, bf16[5,48,128]{2,1,0:T(8,128)(2,1)S(1)}, u32[]{:S(2)}, u32[]{:S(2)}) collective-permute-start(bf16[5,48,128]{2,1,0:T(8,128)(2,1)S(1)} %get-tuple-element.45), channel_id=1, source_target_pairs={{32,0},{64,32},{96,64},{128,96},{160,128},{192,160},{224,192},{256... | collective-permute-start | bytes 184328 | tf_op jit(solution)/shard_map/ppermute | solution.py:355
  18.3 3.2 %collective-permute-start.2 = (bf16[5,48,128]{2,1,0:T(8,128)(2,1)S(1)}, bf16[5,48,128]{2,1,0:T(8,128)(2,1)S(1)}, u32[]{:S(2)}, u32[]{:S(2)}) collective-permute-start(bf16[5,48,128]{2,1,0:T(8,128)(2,1)S(1)} %get-tuple-element.45), channel_id=1, source_target_pairs={{0,32},{32,64},{64,96},{96,128},{128,160},{160,192},{192,224},{224... | collective-permute-start | bytes 184328 | tf_op jit(solution)/shard_map/ppermute | solution.py:355
  20.2 0.7 copy-start.4
  21.5 5.5 %copy-start.2 = (bf16[3,3,3,16,48]{4,3,2,1,0:T(8,128)(2,1)S(1)}, bf16[3,3,3,16,48]{4,3,2,1,0:T(8,128)(2,1)}, u32[]{:S(2)}) copy-start(bf16[3,3,3,16,48]{4,3,2,1,0:T(8,128)(2,1)} %param.9) | copy-start | bytes 124420
  21.5 8.2 %collective-permute-start.5 = (bf16[3,5,48,128]{3,2,1,0:T(8,128)(2,1)S(1)}, bf16[3,5,48,128]{3,2,1,0:T(8,128)(2,1)S(1)}, u32[]{:S(2)}, u32[]{:S(2)}) collective-permute-start(bf16[3,5,48,128]{3,2,1,0:T(8,128)(2,1)S(1)} %pad_maximum_fusion.mid), channel_id=1, source_target_pairs={{4,0},{8,4},{12,8},{16,12},{20,16},{24,20},{28,24},{5,1},{9,5},{13... | collective-permute-start | bytes 552968 | tf_op jit(solution)/shard_map/ppermute | solution.py:355
  22.9 7.7 %collective-permute-start.4 = (bf16[3,5,48,128]{3,2,1,0:T(8,128)(2,1)S(1)}, bf16[3,5,48,128]{3,2,1,0:T(8,128)(2,1)S(1)}, u32[]{:S(2)}, u32[]{:S(2)}) collective-permute-start(bf16[3,5,48,128]{3,2,1,0:T(8,128)(2,1)S(1)} %pad_maximum_fusion.mid), channel_id=1, source_target_pairs={{0,4},{4,8},{8,12},{12,16},{16,20},{20,24},{24,28},{1,5},{5,9},{9,... | collective-permute-start | bytes 552968 | tf_op jit(solution)/shard_map/ppermute | solution.py:355
  27.2 1.0 copy-start.1
  29.2 1.4 copy-start

commit v7 on v6

--- a/solution.py
+++ b/solution.py
@@ -147,26 +147,38 @@
     )
 
 
-def edge_kernel(features_hbm, ids_hbm, first_ref, last_ref, features_ref, ids_ref, done):
+def edge_kernel(features_hbm, ids_hbm, sent_ref, features_ref, ids_ref, done):
     fetches = [
         pltpu.make_async_copy(features_hbm, features_ref, done.at[0]),
         pltpu.make_async_copy(ids_hbm, ids_ref, done.at[1]),
     ]
     for fetch in fetches:
         fetch.start()
-    for fetch in fetches:
-        fetch.wait()
+    row = lax.broadcasted_iota(jnp.int32, (16, LANES), 0)
+    fetches[1].wait()
+    marked = []
+    for r in range(4):
+        ids = ids_ref[r // 2, r % 2 : r % 2 + 1]
+        marks = jnp.where(row == 0, ids >> 8, jnp.where(row == 1, ids & 255, jnp.where(row == 2, 1, 0)))
+        marked.append(marks.astype(f32))
+    fetches[0].wait()
     features = features_ref[...].astype(f32)
-    row = lax.broadcasted_iota(jnp.int32, (16, LANES), 0)
     rows = []
     for r in range(4):
         mine = features[:, r // 2, r % 2, :]
-        ids = ids_ref[r // 2, r % 2 : r % 2 + 1]
-        marks = jnp.where(row == 0, ids >> 8, jnp.where(row == 1, ids & 255, jnp.where(row == 2, 1, 0)))
-        rows.append(jnp.concatenate([mine, marks.astype(f32)], axis=0))
+        rows.append(jnp.concatenate([mine, marked[r]], axis=0))
     first, last = edges(rows)
-    first_ref[...] = first.astype(bf16)
-    last_ref[...] = last.astype(bf16)
+    gx = lax.axis_index("gx")
+    first, last = first.astype(bf16), last.astype(bf16)
+    sent_ref[...] = jnp.zeros(sent_ref.shape, bf16)
+
+    @pl.when(gx > 0)
+    def _():
+        sent_ref[jnp.maximum(gx - 1, 0)] = first
+
+    @pl.when(gx < sent_ref.shape[0] - 1)
+    def _():
+        sent_ref[jnp.minimum(gx + 1, sent_ref.shape[0] - 1)] = last
 
 
 def embed_kernel(place, low, mid, high, taps_one, taps_two, bias, ids_ref, back_one, back_two, marks, *outs):
@@ -394,11 +406,11 @@
     back_two = jnp.transpose(kernel_two[::-1, ::-1, ::-1], (2, 4, 0, 1, 3)).reshape(3 * CHANNELS, 9 * EMBED)
     ids = segment_ids.reshape(1, ROW_COLS)
 
-    first, last = pl.pallas_call(
+    sent = pl.pallas_call(
         edge_kernel,
-        out_shape=[jax.ShapeDtypeStruct((CHANNELS + 16, LANES), bf16)] * 2,
+        out_shape=jax.ShapeDtypeStruct((lax.axis_size("gx"), CHANNELS + 16, LANES), bf16),
         in_specs=[pl.BlockSpec(memory_space=pl.ANY)] * 2,
-        out_specs=[pl.BlockSpec(memory_space=pltpu.VMEM)] * 2,
+        out_specs=pl.BlockSpec(memory_space=pltpu.VMEM),
         scratch_shapes=[
             pltpu.VMEM(features.shape, bf16),
             pltpu.VMEM(segment_ids.shape, jnp.int32),
@@ -406,8 +418,7 @@
         ],
     )(features, segment_ids)
     rows = jnp.transpose(features, (1, 2, 0, 3)).reshape(4, CHANNELS, LANES)
-    left, right = passed(first, last, "gx")
-    pack = left + right
+    pack = add_up(lax.all_to_all(sent, "gx", 0, 0))
     block = jnp.concatenate([rows, pack[None, :CHANNELS]], axis=0)
     low, high = passed(block, block, "gz")
     mid = jnp.stack([low, block, high])

time: 177 us -> 176 us (level)
  blocking collectives: 137 us -> 134 us
    all_to_all x0 -> x1, starting transfers between devices: none -> 4.99 us  [shards(): pack = add_up(lax.all_to_all(sent, 'gx', 0, 0))]
    all_to_all x0 -> x1, waiting for transfers between devices: none -> 4.46 us  [shards(): pack = add_up(lax.all_to_all(sent, 'gx', 0, 0))]
    ppermute x3 -> x2, starting transfers between devices: 9.88 us -> 5.94 us  [passed(): lax.ppermute(high, axis, forward)]
    ppermute x3 -> x2, waiting for transfers between devices: 3.85 us -> 0.5 us  [passed(): lax.ppermute(low, axis, backward)]
    all_to_all x1, blocking collectives: 19.7 us -> 17.1 us  [total(): piece = add_up(lax.all_to_all(pieces, outer, 0, 0))]
    ppermute x3 -> x2, starting transfers between devices: 10 us -> 9.77 us  [passed(): lax.ppermute(low, axis, backward)]
  transfers between devices with their start and end apart: 6 -> 5, of which waited for: 4 -> 4; matrix products, arithmetic and copies ran while one was open for 1% -> 1% of each run, Pallas kernels for 0% -> 0%
where the time goes in v7:
time: 176 us
  blocking collectives  134 us (76%)
  starting transfers between devices  20.7 us (12%)
  Pallas kernels  9.96 us (6%)
  waiting for transfers between devices  6.34 us (4%)
  local copies, waits for them, and re-layouts  3.14 us (2%)
    all_to_all x2, blocking collectives, total_and_relay(): lax.all_to_all(jnp.concatenate([copies(piece, outer), low, high], axis=1)...  29.6 us
    all_to_all x2, blocking collectives, total_and_relay(): held = lax.all_to_all(pieces, outer, 0, 0)  27.8 us
    all_to_all x2, blocking collectives, total_and_relay(): pieces = lax.all_to_all(copies(piece, inner), inner, 0, 0)  25.6 us
    all_to_all x1, blocking collectives, total(): piece = add_up(lax.all_to_all(copies(piece, inner), inner, 0, 0))  20.7 us
    all_to_all x1, blocking collectives, total(): piece = add_up(lax.all_to_all(pieces, outer, 0, 0))  17.1 us
    all_to_all x1, blocking collectives, total(): return lax.all_to_all(copies(piece, outer), outer, 0, 0)  13.2 us
    ppermute x2, starting transfers between devices, passed(): lax.ppermute(low, axis, backward)  9.77 us
    pallas_call x4, Pallas kernels, call(): pl.pallas_call(body, out_shape=[jax.ShapeDtypeStruct(shape, dtype) for sh...  8.35 us
  transfers between devices with their start and end apart: 5, of which 4 were waited for; matrix products, arithmetic and copies ran while one was open for 1% of the time, Pallas kernels for 0%

profile of v7, /device:TPU:1, one launch (start us, length us, event | category | flops | bytes accessed | tf_op | source)
XLA Modules:
  0.0 175.5 jit_solution(12071731286411000185)
XLA Ops:
  0.6 1.6 shard_map.84
  2.3 5.0 %all-to-all-start = ((bf16[4,64,128]{2,1,0:T(8,128)(2,1)}), bf16[4,64,128]{2,1,0:T(8,128)(2,1)S(1)}, u32[]{:S(2)}, u32[]{:S(2)}) async-start(bf16[4,64,128]{2,1,0:T(8,128)(2,1)} %shard_map.84), calls=%async_computation | async-start | bytes 131072 | tf_op jit(solution)/shard_map/all_to_all | solution.py:421
  7.3 4.5 %all-to-all-done = bf16[4,64,128]{2,1,0:T(8,128)(2,1)S(1)} async-done(((bf16[4,64,128]{2,1,0:T(8,128)(2,1)}), bf16[4,64,128]{2,1,0:T(8,128)(2,1)S(1)}, u32[]{:S(2)}, u32[]{:S(2)}) %all-to-all-start) | async-done | bytes 65568 | tf_op jit(solution)/shard_map/all_to_all | solution.py:421
  11.8 8.3 %collective-permute-start.1 = (bf16[5,48,128]{2,1,0:T(8,128)(2,1)S(1)}, bf16[5,48,128]{2,1,0:T(8,128)(2,1)S(1)}, u32[]{:S(2)}, u32[]{:S(2)}) collective-permute-start(bf16[5,48,128]{2,1,0:T(8,128)(2,1)S(1)} %get-tuple-element.41), channel_id=1, source_target_pairs={{32,0},{64,32},{96,64},{128,96},{160,128},{192,160},{224,192},{256... | collective-permute-start | bytes 184328 | tf_op jit(solution)/shard_map/ppermute | solution.py:367
  20.1 1.9 %collective-permute-start = (bf16[5,48,128]{2,1,0:T(8,128)(2,1)S(1)}, bf16[5,48,128]{2,1,0:T(8,128)(2,1)S(1)}, u32[]{:S(2)}, u32[]{:S(2)}) collective-permute-start(bf16[5,48,128]{2,1,0:T(8,128)(2,1)S(1)} %get-tuple-element.41), channel_id=1, source_target_pairs={{0,32},{32,64},{64,96},{96,128},{128,160},{160,192},{192,224},{224... | collective-permute-start | bytes 184328 | tf_op jit(solution)/shard_map/ppermute | solution.py:367
  22.1 0.6 copy-done.4
  22.8 0.5 collective-permute-done
  23.4 1.4 collective-permute-start.3
  24.8 4.0 %collective-permute-start.2 = (bf16[3,5,48,128]{3,2,1,0:T(8,128)(2,1)S(1)}, bf16[3,5,48,128]{3,2,1,0:T(8,128)(2,1)S(1)}, u32[]{:S(2)}, u32[]{:S(2)}) collective-permute-start(bf16[3,5,48,128]{3,2,1,0:T(8,128)(2,1)S(1)} %pad_maximum_fusion.mid), channel_id=1, source_target_pairs={{0,4},{4,8},{8,12},{12,16},{16,20},{20,24},{24,28},{1,5},{5,9},{9,... | collective-permute-start | bytes 552968 | tf_op jit(solution)/shard_map/ppermute | solution.py:367
  28.9 0.1 reshape.60
  29.2 0.1 reshape.57.taps_two
  29.3 0.7 copy-done.1
  30.0 0.2 copy.36
  30.3 0.3 reshape.59.back_one.taps_one
  30.5 0.2 copy.34
  30.7 0.3 reshape.56.taps_one
  31.1 0.5 collective-permute-done.3.high
  31.6 0.9 collective-permute-done.2.low
  32.4 2.0 %shard_map.85 = (bf16[6,6,48,256]{3,2,1,0:T(8,128)(2,1)S(1)}, bf16[4,4,48,256]{3,2,1,0:T(8,128)(2,1)S(1)}, f32[16,640]{1,0:T(8,128)S(1)}, f32[288,1,128]{2,1,0:T(1,128)S(1)}) custom-call(s32[7]{0:T(128)S(1)} %stack.31.place, bf16[3,5,48,128]{3,2,1,0:T(8,128)(2,1)S(1)} %collective-permute-done.2.low, bf16[3,5,48,128]{3,2,1,0:T(8,128)(2,1)S(1)} %pad_maximum_fusion.mid, ...), custom_call_target="tpu_custom_call" | custom-call | tf_op jit(solution)/shard_map/pallas_call | solution.py:28
  34.4 17.1 %all_to_all.50 = f32[32,9,1,128]{3,2,1,0:T(1,128)S(1)} all-to-all(f32[32,9,1,128]{3,2,1,0:T(1,128)S(1)} %bitcast.28), channel_id=1, replica_groups=mesh['gz'=16,'gy'=8,'gx'=4] {'gy','gx'}, dimensions={0} | all-to-all | bytes 294912 | tf_op jit(solution)/shard_map/all_to_all | solution.py:379
  51.6 0.1 reduce_sum.79
  51.7 20.7 %all_to_all.51 = f32[16,9,1,128]{3,2,1,0:T(1,128)S(1)} all-to-all(f32[16,9,1,128]{3,2,1,0:T(1,128)S(1)} %broadcast_in_dim.18), channel_id=1, replica_groups=mesh['gz'=16,'gy'=8,'gx'=4] {'gz'}, dimensions={0} | all-to-all | bytes 147456 | tf_op jit(solution)/shard_map/all_to_all | solution.py:380
  72.6 13.2 %all_to_all.52 = f32[32,9,1,128]{3,2,1,0:T(1,128)S(1)} all-to-all(f32[32,9,1,128]{3,2,1,0:T(1,128)S(1)} %broadcast_in_dim.19), channel_id=1, replica_groups=mesh['gz'=16,'gy'=8,'gx'=4] {'gy','gx'}, dimensions={0} | all-to-all | bytes 294912 | tf_op jit(solution)/shard_map/all_to_all | solution.py:381
  85.8 1.4 shard_map.86
  87.2 12.5 %all_to_all.53 = bf16[16,3,8,128]{3,2,1,0:T(8,128)(2,1)S(1)} all-to-all(bf16[16,3,8,128]{3,2,1,0:T(8,128)(2,1)S(1)} %get-tuple-element.23), channel_id=1, replica_groups=mesh['gz'=16,'gy'=8,'gx'=4] {'gz'}, dimensions={0} | all-to-all | bytes 196608 | tf_op jit(solution)/shard_map/all_to_all | solution.py:385
  99.7 13.1 %all_to_all.54 = bf16[32,2,8,128]{3,2,1,0:T(8,128)(2,1)S(1)} all-to-all(bf16[32,2,8,128]{3,2,1,0:T(8,128)(2,1)S(1)} %broadcast_in_dim.20), channel_id=1, replica_groups=mesh['gz'=16,'gy'=8,'gx'=4] {'gy','gx'}, dimensions={0} | all-to-all | bytes 262144 | tf_op jit(solution)/shard_map/all_to_all | solution.py:387
  112.9 13.0 %all_to_all.55.got_ref = bf16[16,4,8,128]{3,2,1,0:T(8,128)(2,1)S(1)} all-to-all(bf16[16,4,8,128]{3,2,1,0:T(8,128)(2,1)S(1)} %fusion.9), channel_id=1, replica_groups=mesh['gz'=16,'gy'=8,'gx'=4] {'gz'}, dimensions={0} | all-to-all | bytes 262144 | tf_op jit(solution)/shard_map/all_to_all | solution.py:393
  126.0 3.0 %shard_map.87 = (bf16[3,5,16,128]{3,2,1,0:T(8,128)(2,1)S(1)}, bf16[32,4,8,128]{3,2,1,0:T(8,128)(2,1)S(1)}) custom-call(f32[24,640]{1,0:T(8,128)S(1)} %get-tuple-element.22.direct_ref, bf16[16,4,8,128]{3,2,1,0:T(8,128)(2,1)S(1)} %all_to_all.55.got_ref, bf16[6,6,48,256]{3,2,1,0:T(8,128)(2,1)S(1)} %get-tuple-element.26.wide_ref, ...), custom_call_target="tpu_custom_call" | custom-call | tf_op jit(solution)/shard_map/pallas_call | solution.py:28
  128.9 15.3 %all_to_all.56 = bf16[32,4,8,128]{3,2,1,0:T(8,128)(2,1)S(1)} all-to-all(bf16[32,4,8,128]{3,2,1,0:T(8,128)(2,1)S(1)} %get-tuple-element.28), channel_id=1, replica_groups=mesh['gz'=16,'gy'=8,'gx'=4] {'gy','gx'}, dimensions={0} | all-to-all | bytes 524288 | tf_op jit(solution)/shard_map/all_to_all | solution.py:385
  144.3 12.5 %all_to_all.57 = bf16[16,3,8,128]{3,2,1,0:T(8,128)(2,1)S(1)} all-to-all(bf16[16,3,8,128]{3,2,1,0:T(8,128)(2,1)S(1)} %broadcast_in_dim.22), channel_id=1, replica_groups=mesh['gz'=16,'gy'=8,'gx'=4] {'gz'}, dimensions={0} | all-to-all | bytes 196608 | tf_op jit(solution)/shard_map/all_to_all | solution.py:387
  157.0 16.6 %all_to_all.58.got_ref = bf16[32,5,8,128]{3,2,1,0:T(8,128)(2,1)S(1)} all-to-all(bf16[32,5,8,128]{3,2,1,0:T(8,128)(2,1)S(1)} %fusion.4), channel_id=1, replica_groups=mesh['gz'=16,'gy'=8,'gx'=4] {'gy','gx'}, dimensions={0} | all-to-all | bytes 655360 | tf_op jit(solution)/shard_map/all_to_all | solution.py:393
  173.6 2.0 %shard_map.88 = (bf16[48,2,2,128]{3,2,1,0:T(2,128)(2,1)}, f32[27,48,48]{2,1,0:T(8,128)}, f32[1,48]{1,0:T(1,128)}, f32[27,16,48]{2,1,0:T(8,128)}) custom-call(bf16[32,5,8,128]{3,2,1,0:T(8,128)(2,1)S(1)} %all_to_all.58.got_ref, bf16[3,5,16,128]{3,2,1,0:T(8,128)(2,1)S(1)} %get-tuple-element.31.mid, bf16[4,4,48,256]{3,2,1,0:T(8,128)(2,1)S(1)} %get-tuple-element.27.hidden_ref, ...), custom_call_target="tpu_custom_call" | custom-call | tf_op jit(solution)/shard_map/pallas_call | solution.py:28
  (37 shorter events, 1.0 us)
Async XLA Ops:
  2.2 5.0 %copy-start.3 = (bf16[48,2,2,128]{3,2,1,0:T(2,128)(2,1)S(1)}, bf16[48,2,2,128]{3,2,1,0:T(2,128)(2,1)}, u32[]{:S(2)}) copy-start(bf16[48,2,2,128]{3,2,1,0:T(2,128)(2,1)} %features_hbm.1) | copy-start | bytes 147460
  2.3 9.5 %all-to-all-start = ((bf16[4,64,128]{2,1,0:T(8,128)(2,1)}), bf16[4,64,128]{2,1,0:T(8,128)(2,1)S(1)}, u32[]{:S(2)}, u32[]{:S(2)}) async-start(bf16[4,64,128]{2,1,0:T(8,128)(2,1)} %shard_map.84), calls=%async_computation | async-start | bytes 131072 | tf_op jit(solution)/shard_map/all_to_all | solution.py:421
  11.8 11.0 %collective-permute-start.1 = (bf16[5,48,128]{2,1,0:T(8,128)(2,1)S(1)}, bf16[5,48,128]{2,1,0:T(8,128)(2,1)S(1)}, u32[]{:S(2)}, u32[]{:S(2)}) collective-permute-start(bf16[5,48,128]{2,1,0:T(8,128)(2,1)S(1)} %get-tuple-element.41), channel_id=1, source_target_pairs={{32,0},{64,32},{96,64},{128,96},{160,128},{192,160},{224,192},{256... | collective-permute-start | bytes 184328 | tf_op jit(solution)/shard_map/ppermute | solution.py:367
  20.1 3.2 %collective-permute-start = (bf16[5,48,128]{2,1,0:T(8,128)(2,1)S(1)}, bf16[5,48,128]{2,1,0:T(8,128)(2,1)S(1)}, u32[]{:S(2)}, u32[]{:S(2)}) collective-permute-start(bf16[5,48,128]{2,1,0:T(8,128)(2,1)S(1)} %get-tuple-element.41), channel_id=1, source_target_pairs={{0,32},{32,64},{64,96},{96,128},{128,160},{160,192},{192,224},{224... | collective-permute-start | bytes 184328 | tf_op jit(solution)/shard_map/ppermute | solution.py:367
  22.1 0.7 copy-start.4
  23.3 5.5 %copy-start.2 = (bf16[3,3,3,16,48]{4,3,2,1,0:T(8,128)(2,1)S(1)}, bf16[3,3,3,16,48]{4,3,2,1,0:T(8,128)(2,1)}, u32[]{:S(2)}) copy-start(bf16[3,3,3,16,48]{4,3,2,1,0:T(8,128)(2,1)} %param.9) | copy-start | bytes 124420
  23.4 8.2 %collective-permute-start.3 = (bf16[3,5,48,128]{3,2,1,0:T(8,128)(2,1)S(1)}, bf16[3,5,48,128]{3,2,1,0:T(8,128)(2,1)S(1)}, u32[]{:S(2)}, u32[]{:S(2)}) collective-permute-start(bf16[3,5,48,128]{3,2,1,0:T(8,128)(2,1)S(1)} %pad_maximum_fusion.mid), channel_id=1, source_target_pairs={{4,0},{8,4},{12,8},{16,12},{20,16},{24,20},{28,24},{5,1},{9,5},{13... | collective-permute-start | bytes 552968 | tf_op jit(solution)/shard_map/ppermute | solution.py:367
  24.8 7.7 %collective-permute-start.2 = (bf16[3,5,48,128]{3,2,1,0:T(8,128)(2,1)S(1)}, bf16[3,5,48,128]{3,2,1,0:T(8,128)(2,1)S(1)}, u32[]{:S(2)}, u32[]{:S(2)}) collective-permute-start(bf16[3,5,48,128]{3,2,1,0:T(8,128)(2,1)S(1)} %pad_maximum_fusion.mid), channel_id=1, source_target_pairs={{0,4},{4,8},{8,12},{12,16},{16,20},{20,24},{24,28},{1,5},{5,9},{9,... | collective-permute-start | bytes 552968 | tf_op jit(solution)/shard_map/ppermute | solution.py:367
  29.0 1.0 copy-start.1
  31.1 1.4 copy-start

commit v8 on v7

--- a/solution.py
+++ b/solution.py
@@ -53,13 +53,14 @@
     return first, last
 
 
-def widen(blocks, wide_ref):
+def widen(blocks, wide_ref, by_depth=False):
     for yb, ref in enumerate(blocks):
         for zb in range(3):
             pack = ref[zb, 4].astype(f32)
             for r in range(4):
                 edge = pack if r == 0 else pltpu.roll(pack, LANES - 8 * r, 1)
-                z, y = 2 * zb + r // 2, 2 * yb + r % 2
+                z, y = (yb, zb) if by_depth else (zb, yb)
+                z, y = 2 * z + r // 2, 2 * y + r % 2
                 wide_ref[z, y, :, 0:LANES] = ref[zb, r]
                 wide_ref[z, y, :, LANES:WIDE] = edge.astype(bf16)
 
@@ -183,7 +184,7 @@
 
 def embed_kernel(place, low, mid, high, taps_one, taps_two, bias, ids_ref, back_one, back_two, marks, *outs):
     wide_ref, hidden_ref, embed_ref, lines_ref = outs
-    widen((low, mid, high), wide_ref)
+    widen((low, mid, high), wide_ref, by_depth=True)
     gz, gy, gx = place[0], place[1], place[2]
     at = lane((CHANNELS, WIDE))
     inside = (at < LANES) | ((at < LANES + 3) & (gx < place[6])) | ((at >= WIDE - 3) & (gx > 0))
@@ -420,9 +421,9 @@
     rows = jnp.transpose(features, (1, 2, 0, 3)).reshape(4, CHANNELS, LANES)
     pack = add_up(lax.all_to_all(sent, "gx", 0, 0))
     block = jnp.concatenate([rows, pack[None, :CHANNELS]], axis=0)
-    low, high = passed(block, block, "gz")
+    low, high = passed(block, block, "gy")
     mid = jnp.stack([low, block, high])
-    low, high = passed(mid, mid, "gy")
+    low, high = passed(mid, mid, "gz")
     marks = pack[CHANNELS:]
     wide, hidden, embedding, lines = kernel_call(
         embed_kernel,

time: 176 us -> 176 us (level)
  transfers between devices with their start and end apart: 5 -> 5, of which waited for: 4 -> 3; matrix products, arithmetic and copies ran while one was open for 1% -> 1% of each run, Pallas kernels for 0% -> 0%
where the time goes in v8:
time: 176 us
  blocking collectives  134 us (76%)
  starting transfers between devices  21.8 us (12%)
  Pallas kernels  9.96 us (6%)
  waiting for transfers between devices  5.16 us (3%)
  local copies, waits for them, and re-layouts  3.63 us (2%)
    all_to_all x2, blocking collectives, total_and_relay(): lax.all_to_all(jnp.concatenate([copies(piece, outer), low, high], axis=1)...  29.6 us
    all_to_all x2, blocking collectives, total_and_relay(): held = lax.all_to_all(pieces, outer, 0, 0)  27.8 us
    all_to_all x2, blocking collectives, total_and_relay(): pieces = lax.all_to_all(copies(piece, inner), inner, 0, 0)  25.6 us
    all_to_all x1, blocking collectives, total(): piece = add_up(lax.all_to_all(copies(piece, inner), inner, 0, 0))  20 us
    all_to_all x1, blocking collectives, total(): piece = add_up(lax.all_to_all(pieces, outer, 0, 0))  17.5 us
    all_to_all x1, blocking collectives, total(): return lax.all_to_all(copies(piece, outer), outer, 0, 0)  13.1 us
    ppermute x2, starting transfers between devices, passed(): lax.ppermute(low, axis, backward)  10.9 us
    pallas_call x4, Pallas kernels, call(): pl.pallas_call(body, out_shape=[jax.ShapeDtypeStruct(shape, dtype) for sh...  8.35 us
  transfers between devices with their start and end apart: 5, of which 3 were waited for; matrix products, arithmetic and copies ran while one was open for 1% of the time, Pallas kernels for 0%

profile of v8, /device:TPU:1, one launch (start us, length us, event | category | flops | bytes accessed | tf_op | source)
XLA Modules:
  0.0 175.5 jit_solution(1261911340788447303)
XLA Ops:
  0.6 1.6 shard_map.84
  2.3 5.0 %all-to-all-start = ((bf16[4,64,128]{2,1,0:T(8,128)(2,1)}), bf16[4,64,128]{2,1,0:T(8,128)(2,1)S(1)}, u32[]{:S(2)}, u32[]{:S(2)}) async-start(bf16[4,64,128]{2,1,0:T(8,128)(2,1)} %shard_map.84), calls=%async_computation | async-start | bytes 131072 | tf_op jit(solution)/shard_map/all_to_all | solution.py:422
  7.3 4.5 %all-to-all-done = bf16[4,64,128]{2,1,0:T(8,128)(2,1)S(1)} async-done(((bf16[4,64,128]{2,1,0:T(8,128)(2,1)}), bf16[4,64,128]{2,1,0:T(8,128)(2,1)S(1)}, u32[]{:S(2)}, u32[]{:S(2)}) %all-to-all-start) | async-done | bytes 65568 | tf_op jit(solution)/shard_map/all_to_all | solution.py:422
  11.8 1.3 collective-permute-start.1
  13.1 4.0 %collective-permute-start = (bf16[5,48,128]{2,1,0:T(8,128)(2,1)S(1)}, bf16[5,48,128]{2,1,0:T(8,128)(2,1)S(1)}, u32[]{:S(2)}, u32[]{:S(2)}) collective-permute-start(bf16[5,48,128]{2,1,0:T(8,128)(2,1)S(1)} %get-tuple-element.41), channel_id=1, source_target_pairs={{0,4},{4,8},{8,12},{12,16},{16,20},{20,24},{24,28},{1,5},{5,9},{9,... | collective-permute-start | bytes 184328 | tf_op jit(solution)/shard_map/ppermute | solution.py:368
  17.1 0.6 copy-done.4
  17.8 0.5 collective-permute-done
  18.4 9.6 %collective-permute-start.3 = (bf16[3,5,48,128]{3,2,1,0:T(8,128)(2,1)S(1)}, bf16[3,5,48,128]{3,2,1,0:T(8,128)(2,1)S(1)}, u32[]{:S(2)}, u32[]{:S(2)}) collective-permute-start(bf16[3,5,48,128]{3,2,1,0:T(8,128)(2,1)S(1)} %pad_maximum_fusion.mid), channel_id=1, source_target_pairs={{32,0},{64,32},{96,64},{128,96},{160,128},{192,160},{224,192},{256... | collective-permute-start | bytes 552968 | tf_op jit(solution)/shard_map/ppermute | solution.py:368
  28.0 1.9 %collective-permute-start.2 = (bf16[3,5,48,128]{3,2,1,0:T(8,128)(2,1)S(1)}, bf16[3,5,48,128]{3,2,1,0:T(8,128)(2,1)S(1)}, u32[]{:S(2)}, u32[]{:S(2)}) collective-permute-start(bf16[3,5,48,128]{3,2,1,0:T(8,128)(2,1)S(1)} %pad_maximum_fusion.mid), channel_id=1, source_target_pairs={{0,32},{32,64},{64,96},{96,128},{128,160},{160,192},{192,224},{224... | collective-permute-start | bytes 552968 | tf_op jit(solution)/shard_map/ppermute | solution.py:368
  30.0 0.1 reshape.60
  30.3 0.1 reshape.57.taps_two
  30.4 0.7 copy-done.1
  31.1 0.2 copy.36
  31.4 0.3 reshape.59.back_one.taps_one
  31.6 0.2 copy.34
  31.8 0.3 reshape.56.taps_one
  32.2 0.2 collective-permute-done.2.low
  32.4 0.5 copy-done
  32.9 2.0 %shard_map.85 = (bf16[6,6,48,256]{3,2,1,0:T(8,128)(2,1)S(1)}, bf16[4,4,48,256]{3,2,1,0:T(8,128)(2,1)S(1)}, f32[16,640]{1,0:T(8,128)S(1)}, f32[288,1,128]{2,1,0:T(1,128)S(1)}) custom-call(s32[7]{0:T(128)S(1)} %stack.31.place, bf16[3,5,48,128]{3,2,1,0:T(8,128)(2,1)S(1)} %collective-permute-done.2.low, bf16[3,5,48,128]{3,2,1,0:T(8,128)(2,1)S(1)} %pad_maximum_fusion.mid, ...), custom_call_target="tpu_custom_call" | custom-call | tf_op jit(solution)/shard_map/pallas_call | solution.py:28
  34.9 17.5 %all_to_all.50 = f32[32,9,1,128]{3,2,1,0:T(1,128)S(1)} all-to-all(f32[32,9,1,128]{3,2,1,0:T(1,128)S(1)} %bitcast.28), channel_id=1, replica_groups=mesh['gz'=16,'gy'=8,'gx'=4] {'gy','gx'}, dimensions={0} | all-to-all | bytes 294912 | tf_op jit(solution)/shard_map/all_to_all | solution.py:380
  52.4 0.1 reduce_sum.79
  52.5 20.0 %all_to_all.51 = f32[16,9,1,128]{3,2,1,0:T(1,128)S(1)} all-to-all(f32[16,9,1,128]{3,2,1,0:T(1,128)S(1)} %broadcast_in_dim.18), channel_id=1, replica_groups=mesh['gz'=16,'gy'=8,'gx'=4] {'gz'}, dimensions={0} | all-to-all | bytes 147456 | tf_op jit(solution)/shard_map/all_to_all | solution.py:381
  72.7 13.1 %all_to_all.52 = f32[32,9,1,128]{3,2,1,0:T(1,128)S(1)} all-to-all(f32[32,9,1,128]{3,2,1,0:T(1,128)S(1)} %broadcast_in_dim.19), channel_id=1, replica_groups=mesh['gz'=16,'gy'=8,'gx'=4] {'gy','gx'}, dimensions={0} | all-to-all | bytes 294912 | tf_op jit(solution)/shard_map/all_to_all | solution.py:382
  85.8 1.4 shard_map.86
  87.2 12.5 %all_to_all.53 = bf16[16,3,8,128]{3,2,1,0:T(8,128)(2,1)S(1)} all-to-all(bf16[16,3,8,128]{3,2,1,0:T(8,128)(2,1)S(1)} %get-tuple-element.23), channel_id=1, replica_groups=mesh['gz'=16,'gy'=8,'gx'=4] {'gz'}, dimensions={0} | all-to-all | bytes 196608 | tf_op jit(solution)/shard_map/all_to_all | solution.py:386
  99.7 13.1 %all_to_all.54 = bf16[32,2,8,128]{3,2,1,0:T(8,128)(2,1)S(1)} all-to-all(bf16[32,2,8,128]{3,2,1,0:T(8,128)(2,1)S(1)} %broadcast_in_dim.20), channel_id=1, replica_groups=mesh['gz'=16,'gy'=8,'gx'=4] {'gy','gx'}, dimensions={0} | all-to-all | bytes 262144 | tf_op jit(solution)/shard_map/all_to_all | solution.py:388
  112.9 13.0 %all_to_all.55.got_ref = bf16[16,4,8,128]{3,2,1,0:T(8,128)(2,1)S(1)} all-to-all(bf16[16,4,8,128]{3,2,1,0:T(8,128)(2,1)S(1)} %fusion.9), channel_id=1, replica_groups=mesh['gz'=16,'gy'=8,'gx'=4] {'gz'}, dimensions={0} | all-to-all | bytes 262144 | tf_op jit(solution)/shard_map/all_to_all | solution.py:394
  126.0 3.0 %shard_map.87 = (bf16[3,5,16,128]{3,2,1,0:T(8,128)(2,1)S(1)}, bf16[32,4,8,128]{3,2,1,0:T(8,128)(2,1)S(1)}) custom-call(f32[24,640]{1,0:T(8,128)S(1)} %get-tuple-element.22.direct_ref, bf16[16,4,8,128]{3,2,1,0:T(8,128)(2,1)S(1)} %all_to_all.55.got_ref, bf16[6,6,48,256]{3,2,1,0:T(8,128)(2,1)S(1)} %get-tuple-element.26.wide_ref, ...), custom_call_target="tpu_custom_call" | custom-call | tf_op jit(solution)/shard_map/pallas_call | solution.py:28
  128.9 15.3 %all_to_all.56 = bf16[32,4,8,128]{3,2,1,0:T(8,128)(2,1)S(1)} all-to-all(bf16[32,4,8,128]{3,2,1,0:T(8,128)(2,1)S(1)} %get-tuple-element.28), channel_id=1, replica_groups=mesh['gz'=16,'gy'=8,'gx'=4] {'gy','gx'}, dimensions={0} | all-to-all | bytes 524288 | tf_op jit(solution)/shard_map/all_to_all | solution.py:386
  144.3 12.5 %all_to_all.57 = bf16[16,3,8,128]{3,2,1,0:T(8,128)(2,1)S(1)} all-to-all(bf16[16,3,8,128]{3,2,1,0:T(8,128)(2,1)S(1)} %broadcast_in_dim.22), channel_id=1, replica_groups=mesh['gz'=16,'gy'=8,'gx'=4] {'gz'}, dimensions={0} | all-to-all | bytes 196608 | tf_op jit(solution)/shard_map/all_to_all | solution.py:388
  157.0 16.6 %all_to_all.58.got_ref = bf16[32,5,8,128]{3,2,1,0:T(8,128)(2,1)S(1)} all-to-all(bf16[32,5,8,128]{3,2,1,0:T(8,128)(2,1)S(1)} %fusion.4), channel_id=1, replica_groups=mesh['gz'=16,'gy'=8,'gx'=4] {'gy','gx'}, dimensions={0} | all-to-all | bytes 655360 | tf_op jit(solution)/shard_map/all_to_all | solution.py:394
  173.6 2.0 %shard_map.88 = (bf16[48,2,2,128]{3,2,1,0:T(2,128)(2,1)}, f32[27,48,48]{2,1,0:T(8,128)}, f32[1,48]{1,0:T(1,128)}, f32[27,16,48]{2,1,0:T(8,128)}) custom-call(bf16[32,5,8,128]{3,2,1,0:T(8,128)(2,1)S(1)} %all_to_all.58.got_ref, bf16[3,5,16,128]{3,2,1,0:T(8,128)(2,1)S(1)} %get-tuple-element.31.mid, bf16[4,4,48,256]{3,2,1,0:T(8,128)(2,1)S(1)} %get-tuple-element.27.hidden_ref, ...), custom_call_target="tpu_custom_call" | custom-call | tf_op jit(solution)/shard_map/pallas_call | solution.py:28
  (37 shorter events, 1.0 us)
Async XLA Ops:
  2.2 5.0 %copy-start.3 = (bf16[48,2,2,128]{3,2,1,0:T(2,128)(2,1)S(1)}, bf16[48,2,2,128]{3,2,1,0:T(2,128)(2,1)}, u32[]{:S(2)}) copy-start(bf16[48,2,2,128]{3,2,1,0:T(2,128)(2,1)} %features_hbm.1) | copy-start | bytes 147460
  2.3 9.5 %all-to-all-start = ((bf16[4,64,128]{2,1,0:T(8,128)(2,1)}), bf16[4,64,128]{2,1,0:T(8,128)(2,1)S(1)}, u32[]{:S(2)}, u32[]{:S(2)}) async-start(bf16[4,64,128]{2,1,0:T(8,128)(2,1)} %shard_map.84), calls=%async_computation | async-start | bytes 131072 | tf_op jit(solution)/shard_map/all_to_all | solution.py:422
  11.8 6.1 %collective-permute-start.1 = (bf16[5,48,128]{2,1,0:T(8,128)(2,1)S(1)}, bf16[5,48,128]{2,1,0:T(8,128)(2,1)S(1)}, u32[]{:S(2)}, u32[]{:S(2)}) collective-permute-start(bf16[5,48,128]{2,1,0:T(8,128)(2,1)S(1)} %get-tuple-element.41), channel_id=1, source_target_pairs={{4,0},{8,4},{12,8},{16,12},{20,16},{24,20},{28,24},{5,1},{9,5},{13... | collective-permute-start | bytes 184328 | tf_op jit(solution)/shard_map/ppermute | solution.py:368
  13.1 5.3 %collective-permute-start = (bf16[5,48,128]{2,1,0:T(8,128)(2,1)S(1)}, bf16[5,48,128]{2,1,0:T(8,128)(2,1)S(1)}, u32[]{:S(2)}, u32[]{:S(2)}) collective-permute-start(bf16[5,48,128]{2,1,0:T(8,128)(2,1)S(1)} %get-tuple-element.41), channel_id=1, source_target_pairs={{0,4},{4,8},{8,12},{12,16},{16,20},{20,24},{24,28},{1,5},{5,9},{9,... | collective-permute-start | bytes 184328 | tf_op jit(solution)/shard_map/ppermute | solution.py:368
  17.1 0.7 copy-start.4
  18.3 11.6 %copy-start.2 = (bf16[3,3,3,16,48]{4,3,2,1,0:T(8,128)(2,1)S(1)}, bf16[3,3,3,16,48]{4,3,2,1,0:T(8,128)(2,1)}, u32[]{:S(2)}) copy-start(bf16[3,3,3,16,48]{4,3,2,1,0:T(8,128)(2,1)} %param.9) | copy-start | bytes 124420
  18.4 13.8 %collective-permute-start.3 = (bf16[3,5,48,128]{3,2,1,0:T(8,128)(2,1)S(1)}, bf16[3,5,48,128]{3,2,1,0:T(8,128)(2,1)S(1)}, u32[]{:S(2)}, u32[]{:S(2)}) collective-permute-start(bf16[3,5,48,128]{3,2,1,0:T(8,128)(2,1)S(1)} %pad_maximum_fusion.mid), channel_id=1, source_target_pairs={{32,0},{64,32},{96,64},{128,96},{160,128},{192,160},{224,192},{256... | collective-permute-start | bytes 552968 | tf_op jit(solution)/shard_map/ppermute | solution.py:368
  28.0 4.4 %collective-permute-start.2 = (bf16[3,5,48,128]{3,2,1,0:T(8,128)(2,1)S(1)}, bf16[3,5,48,128]{3,2,1,0:T(8,128)(2,1)S(1)}, u32[]{:S(2)}, u32[]{:S(2)}) collective-permute-start(bf16[3,5,48,128]{3,2,1,0:T(8,128)(2,1)S(1)} %pad_maximum_fusion.mid), channel_id=1, source_target_pairs={{0,32},{32,64},{64,96},{96,128},{128,160},{160,192},{192,224},{224... | collective-permute-start | bytes 552968 | tf_op jit(solution)/shard_map/ppermute | solution.py:368
  30.1 1.0 copy-start.1
  32.2 0.7 copy-start
